TPU v7x, 256 devices: a whole 4x4x8 slice. The times are simulated.
256 devices in a mesh: gx: 8 (over z), gy: 32 (over y, x, core).
Axes of the slice: x: 4, y: 4, z: 8, core: 2. Of those that a mesh axis runs over, the one named last changes fastest.
Arguments:
- design: float32 [128, 256, 1024], P('gx', 'gy'), may hold values from 0 to 1
- filtered: float32 [128, 256, 1024], P('gx', 'gy'), may hold values from 0 to 1
- sensitivity: float32 [128, 256, 1024], P('gx', 'gy'), may hold values from -400 to 400
- first_moment: float32 [128, 256, 1024], P('gx', 'gy'), may hold values from -0.6 to 0.6
- second_moment: float32 [128, 256, 1024], P('gx', 'gy'), may hold values from 0.001 to 0.1
- lagrange: float32 [2], replicated, may hold values from 0.5 to 2
- trace_values: float32 [8, 2048, 128], P('gx', 'gy'), may hold values from -6 to 6
- trace_anchor: int32 [8, 2048], P('gx', 'gy'), may hold values from 0 to 1023
- trace_owner: int32 [8, 2048, 1], P('gx', 'gy'), may hold values from 0 to 31; in each aligned block of 64 rows (0 to 63, 64 to 127, ..., all dimensions but the last counted through in order) at most 8 rows name the same one
Outputs:
- new_design: float32 [128, 256, 1024], P('gx', 'gy')
- new_first: float32 [128, 256, 1024], P('gx', 'gy')
- new_second: float32 [128, 256, 1024], P('gx', 'gy')
- gradient: float32 [128, 256, 1024], P('gx', 'gy')
Inputs may be any that keep to these rules, and one draw needn't show every extreme that they name: `trace_owner`: among the 64 rows of one device no gy index is named more than 8 times; some index is named exactly 8 times.
All inputs are finite; a program needn't handle non-finite values.
Results may differ from a plain program's by a relative error of at most 0.00002.
Values sent between devices are 32-bit elements; how exact they have to be, the bound alone decides.
No kernel may reach another device: no remote copies, remote signals or barrier semaphores. Data moves between devices by JAX's collectives and lax.ppermute only.
A program may use at most 64 MiB of HBM per device.

v0:
```python
import jax
import jax.numpy as jnp
from jax import lax
from jax.sharding import PartitionSpec as P

SWEEPS = 4
ADAM_STEP = 10


def with_halo(cells, sides, width):
    for axis, dim in sides:
        count = lax.axis_size(axis)
        ends = count - 1
        head = lax.slice_in_dim(cells, 0, width, axis=dim)
        tail = lax.slice_in_dim(cells, cells.shape[dim] - width, cells.shape[dim], axis=dim)
        cells = jnp.concatenate(
            [
                lax.ppermute(tail, axis, [(i, (i + 1) % count) for i in range(ends)]),
                cells,
                lax.ppermute(head, axis, [((i + 1) % count, i) for i in range(ends)]),
            ],
            axis=dim,
        )
    return cells


def neighbours(padded):
    centre = padded[:, 1:-1, 1:-1]
    zpadded = jnp.pad(centre, ((0, 0), (0, 0), (0, 0), (1, 1)))
    nearby = padded[:, 2:, 1:-1] + padded[:, :-2, 1:-1] + padded[:, 1:-1, 2:] + padded[:, 1:-1, :-2]
    return nearby + zpadded[..., 2:] + zpadded[..., :-2]


def smooth(source):
    field = source
    for sweep in range(SWEEPS):
        padded = with_halo(field, (("gx", 1), ("gy", 2)), 1)
        field = (source + 4.0 * neighbours(padded)) / 25.0
    return field


def deliver(trace_values, trace_anchor, trace_owner, block_rows):
    every_values, every_anchor, every_owner = (
        lax.all_gather(trace_values, "gy", axis=1, tiled=True),
        lax.all_gather(trace_anchor, "gy", axis=1, tiled=True),
        lax.all_gather(trace_owner, "gy", axis=1, tiled=True),
    )
    owned = (every_owner[0, :, 0] == lax.axis_index("gy")).astype(jnp.float32)
    zeros_rows = jnp.zeros((block_rows, trace_values.shape[2]), jnp.float32)
    return zeros_rows.at[every_anchor[0]].add(every_values[0] * owned[:, None])


def per_device(
    design,
    filtered,
    sensitivity,
    first_moment,
    second_moment,
    lagrange,
    trace_values,
    trace_anchor,
    trace_owner,
):
    width_x, width_y, depth = design.shape
    cells = float(width_x * width_y * depth * lax.axis_size("gx") * lax.axis_size("gy"))
    slope_part = jnp.tanh(8.0 * (filtered - 0.5))
    denominator = 2.0 * jnp.tanh(4.0)
    projected = (jnp.tanh(4.0) + slope_part) / denominator
    slope = 8.0 * (1.0 - slope_part * slope_part) / denominator
    local_volume = jnp.sum(projected)
    block_rows = width_x * width_y * depth // trace_values.shape[2]
    trace_field = deliver(trace_values, trace_anchor, trace_owner, block_rows).reshape(
        width_x, width_y, depth
    )
    volume = lax.psum(local_volume, ("gx", "gy"))
    weight = lagrange[0] + lagrange[1] * (volume / cells / 0.4 - 1.0)
    source = slope * (sensitivity + trace_field + weight)
    raw = smooth(source[None])[0]
    total = lax.psum(jnp.sum(raw * raw), ("gx", "gy"))
    gradient = raw / jnp.sqrt(total / cells + 1e-06)
    new_first = 0.9 * first_moment + 0.1 * gradient
    new_second = 0.999 * second_moment + 0.001 * gradient * gradient
    first_hat = new_first / (1.0 - 0.9**ADAM_STEP)
    second_hat = new_second / (1.0 - 0.999**ADAM_STEP)
    new_design = jnp.clip(design - 0.05 * first_hat / (jnp.sqrt(second_hat) + 1e-08), 0.0, 1.0)
    return (new_design, new_first, new_second, gradient)


def solution(mesh):
    return jax.shard_map(
        per_device,
        mesh=mesh,
        in_specs=(
            P("gx", "gy", None),
            P("gx", "gy", None),
            P("gx", "gy", None),
            P("gx", "gy", None),
            P("gx", "gy", None),
            P(),
            P("gx", "gy", None),
            P("gx", "gy"),
            P("gx", "gy", None),
        ),
        out_specs=(
            P("gx", "gy", None),
            P("gx", "gy", None),
            P("gx", "gy", None),
            P("gx", "gy", None),
        ),
        check_vma=False,
    )
```

profile of v0, /device:TPU:1, one launch (start us, length us, event | category | flops | bytes accessed | tf_op | source)
XLA Modules:
  0.0 387.5 jit_solution(6533192978553132089)
XLA Ops:
  7.2 0.7 all-gather.2.cloned.1.call-update
  7.9 1.8 multiply_reduce_fusion.1
  9.7 81.3 %psum.14 = f32[]{:T(128)} all-reduce(f32[]{:T(128)} %multiply_reduce_fusion.1), channel_id=1, replica_groups=mesh['gx'=8,'gy'=32] {'gx','gy'}, use_global_device_ids=true, to_apply=%region_2.0 | all-reduce | flops 1 | bytes 8 | tf_op jit(solution)/shard_map/psum | solution.py:75
  91.7 0.7 copy-done.8
  92.4 0.6 dynamic-slice
  93.6 0.6 fusion.42
  95.5 0.6 copy-done.6
  96.3 0.7 copy-done.7
  97.0 119.6 %all-reduce.6 = (s32[2048]{0:T(1024)S(1)}, s32[2048]{0:T(1024)S(1)}) all-reduce(s32[2048]{0:T(1024)S(1)} %bitcast_dynamic-update-slice_fusion.1, s32[2048]{0:T(1024)S(1)} %bitcast_dynamic-update-slice_fusion), channel_id=1, replica_groups=mesh['gx'=8,'gy'=32] {'gy'}, use_global_device_ids=true, to_apply=%add.4 | all-reduce | flops 4096 | bytes 32768
  216.7 13.0 %scatter_custom_fusion = f32[1024,128]{1,0:T(8,128)S(1)} fusion(s32[2048]{0:T(1024)S(1)} %bitcast.17, f32[1,2048,128]{2,1,0:T(8,128)} %all-gather.2.cloned.1.call-done, f32[2048]{0:T(1024)S(1)} %compare_convert_fusion, f32[]{:T(128)} %constant.23.clone.1), kind=kCustom, calls=%fused_computation.2 | custom fusion | flops 524288 | bytes 1581060 | tf_op jit(solution)/shard_map/scatter-add | solution.py:50
  229.8 0.9 copy-done
  230.8 0.2 copy-done.1
  230.9 0.2 multiply_bitcast_fusion
  231.1 2.6 collective-permute-start.1
  233.7 1.3 collective-permute-start
  235.1 3.3 collective-permute-done
  238.4 0.1 pad_maximum_fusion.43
  238.5 9.0 %collective-permute-start.2 = (f32[1,18,1,1024]{3,2,1,0:T(1,128)S(1)}, f32[1,18,1,1024]{3,2,1,0:T(1,128)S(1)}, u32[]{:S(2)}, u32[]{:S(2)}) collective-permute-start(f32[1,18,1,1024]{3,2,1,0:T(1,128)S(1)} %get-tuple-element.18), channel_id=1, source_target_pairs={{1,0},{2,1},{3,2},{4,3},{5,4},{6,5},{7,6},{8,7},{9,8},{10,9},{11,1... | collective-permute-start | bytes 221192 | tf_op jit(solution)/shard_map/ppermute | solution.py:20
  247.5 1.9 collective-permute-start.3
  249.4 1.4 collective-permute-done.3
  250.8 0.4 fusion.5
  251.2 1.6 collective-permute-start.5
  252.9 1.3 collective-permute-start.4
  254.2 3.6 collective-permute-done.4
  257.8 0.1 pad_maximum_fusion.40
  257.9 3.1 collective-permute-start.6
  261.0 4.3 %collective-permute-start.7 = (f32[1,18,1,1024]{3,2,1,0:T(1,128)S(1)}, f32[1,18,1,1024]{3,2,1,0:T(1,128)S(1)}, u32[]{:S(2)}, u32[]{:S(2)}) collective-permute-start(f32[1,18,1,1024]{3,2,1,0:T(1,128)S(1)} %get-tuple-element.17), channel_id=1, source_target_pairs={{0,1},{1,2},{2,3},{3,4},{4,5},{5,6},{6,7},{7,8},{8,9},{9,10},{10,1... | collective-permute-start | bytes 221192 | tf_op jit(solution)/shard_map/ppermute | solution.py:18
  265.3 0.1 collective-permute-done.6
  265.4 1.3 collective-permute-done.7
  266.7 0.4 fusion.10
  267.1 4.0 %collective-permute-start.9 = (f32[1,1,8,1024]{3,2,1,0:T(8,128)S(1)}, f32[1,1,8,1024]{3,2,1,0:T(8,128)S(1)}, u32[]{:S(2)}, u32[]{:S(2)}) collective-permute-start(f32[1,1,8,1024]{3,2,1,0:T(8,128)S(1)} %get-tuple-element.22), channel_id=1, source_target_pairs={{0,32},{32,64},{64,96},{96,128},{128,160},{160,192},{192,224},{1,3... | collective-permute-start | bytes 98312 | tf_op jit(solution)/shard_map/ppermute | solution.py:18
  271.1 1.3 collective-permute-start.8
  272.4 3.6 collective-permute-done.8
  276.0 0.1 pad_maximum_fusion.37
  276.1 1.9 collective-permute-start.10
  278.1 5.4 %collective-permute-start.11 = (f32[1,18,1,1024]{3,2,1,0:T(1,128)S(1)}, f32[1,18,1,1024]{3,2,1,0:T(1,128)S(1)}, u32[]{:S(2)}, u32[]{:S(2)}) collective-permute-start(f32[1,18,1,1024]{3,2,1,0:T(1,128)S(1)} %get-tuple-element.15), channel_id=1, source_target_pairs={{0,1},{1,2},{2,3},{3,4},{4,5},{5,6},{6,7},{7,8},{8,9},{9,10},{10,1... | collective-permute-start | bytes 221192 | tf_op jit(solution)/shard_map/ppermute | solution.py:18
  283.5 0.1 collective-permute-done.10
  283.6 1.3 collective-permute-done.11
  284.9 0.4 fusion.15
  285.3 3.7 collective-permute-start.13
  289.0 1.3 collective-permute-start.12
  290.3 3.6 collective-permute-done.12
  294.0 1.9 collective-permute-start.14
  296.0 5.6 %collective-permute-start.15 = (f32[1,18,1,1024]{3,2,1,0:T(1,128)S(1)}, f32[1,18,1,1024]{3,2,1,0:T(1,128)S(1)}, u32[]{:S(2)}, u32[]{:S(2)}) collective-permute-start(f32[1,18,1,1024]{3,2,1,0:T(1,128)S(1)} %get-tuple-element.13), channel_id=1, source_target_pairs={{0,1},{1,2},{2,3},{3,4},{4,5},{5,6},{6,7},{7,8},{8,9},{9,10},{10,1... | collective-permute-start | bytes 221192 | tf_op jit(solution)/shard_map/ppermute | solution.py:18
  301.6 1.4 collective-permute-done.15
  302.9 1.0 multiply_reduce_fusion
  304.0 74.5 %psum.15 = f32[]{:T(128)} all-reduce(f32[]{:T(128)} %get-tuple-element.10), channel_id=1, replica_groups=mesh['gx'=8,'gy'=32] {'gx','gy'}, use_global_device_ids=true, to_apply=%region_4.5 | all-reduce | flops 1 | bytes 8 | tf_op jit(solution)/shard_map/psum | solution.py:79
  379.1 1.5 subtract_clamp_fusion
  (33 shorter events, 0.5 us)
Async XLA Ops:
  7.2 209.5 %all-gather.2.cloned.1.call-start = ((), (), s32[]{:S(2)}) async-start(), calls=%async_computation | async-start | bytes 1081344 | tf_op jit(solution)/shard_map/all_gather | solution.py:44
  91.7 0.7 copy-start.8
  92.9 0.7 copy-start.5
  95.5 0.7 copy-start.6
  96.3 0.7 copy-start.7
  229.7 1.0 copy-start
  229.7 1.2 copy-start.1
  231.1 3.9 %collective-permute-start.1 = (f32[1,1,8,1024]{3,2,1,0:T(8,128)S(1)}, f32[1,1,8,1024]{3,2,1,0:T(8,128)S(1)}, u32[]{:S(2)}, u32[]{:S(2)}) collective-permute-start(f32[1,1,8,1024]{3,2,1,0:T(8,128)S(1)} %get-tuple-element.26), channel_id=1, source_target_pairs={{0,32},{32,64},{64,96},{96,128},{128,160},{160,192},{192,224},{1,3... | collective-permute-start | bytes 98312 | tf_op jit(solution)/shard_map/ppermute | solution.py:18
  233.7 4.7 %collective-permute-start = (f32[1,1,8,1024]{3,2,1,0:T(8,128)S(1)}, f32[1,1,8,1024]{3,2,1,0:T(8,128)S(1)}, u32[]{:S(2)}, u32[]{:S(2)}) collective-permute-start(f32[1,1,8,1024]{3,2,1,0:T(8,128)S(1)} %get-tuple-element.27), channel_id=1, source_target_pairs={{32,0},{64,32},{96,64},{128,96},{160,128},{192,160},{224,192},{33,... | collective-permute-start | bytes 98312 | tf_op jit(solution)/shard_map/ppermute | solution.py:20
  238.5 10.9 %collective-permute-start.2 = (f32[1,18,1,1024]{3,2,1,0:T(1,128)S(1)}, f32[1,18,1,1024]{3,2,1,0:T(1,128)S(1)}, u32[]{:S(2)}, u32[]{:S(2)}) collective-permute-start(f32[1,18,1,1024]{3,2,1,0:T(1,128)S(1)} %get-tuple-element.18), channel_id=1, source_target_pairs={{1,0},{2,1},{3,2},{4,3},{5,4},{6,5},{7,6},{8,7},{9,8},{10,9},{11,1... | collective-permute-start | bytes 221192 | tf_op jit(solution)/shard_map/ppermute | solution.py:20
  247.5 3.3 collective-permute-start.3
  251.2 3.0 collective-permute-start.5
  252.9 4.9 %collective-permute-start.4 = (f32[1,1,8,1024]{3,2,1,0:T(8,128)S(1)}, f32[1,1,8,1024]{3,2,1,0:T(8,128)S(1)}, u32[]{:S(2)}, u32[]{:S(2)}) collective-permute-start(f32[1,1,8,1024]{3,2,1,0:T(8,128)S(1)} %get-tuple-element.25), channel_id=1, source_target_pairs={{32,0},{64,32},{96,64},{128,96},{160,128},{192,160},{224,192},{33,... | collective-permute-start | bytes 98312 | tf_op jit(solution)/shard_map/ppermute | solution.py:20
  257.9 7.5 %collective-permute-start.6 = (f32[1,18,1,1024]{3,2,1,0:T(1,128)S(1)}, f32[1,18,1,1024]{3,2,1,0:T(1,128)S(1)}, u32[]{:S(2)}, u32[]{:S(2)}) collective-permute-start(f32[1,18,1,1024]{3,2,1,0:T(1,128)S(1)} %get-tuple-element.16), channel_id=1, source_target_pairs={{1,0},{2,1},{3,2},{4,3},{5,4},{6,5},{7,6},{8,7},{9,8},{10,9},{11,1... | collective-permute-start | bytes 221192 | tf_op jit(solution)/shard_map/ppermute | solution.py:20
  261.0 5.7 %collective-permute-start.7 = (f32[1,18,1,1024]{3,2,1,0:T(1,128)S(1)}, f32[1,18,1,1024]{3,2,1,0:T(1,128)S(1)}, u32[]{:S(2)}, u32[]{:S(2)}) collective-permute-start(f32[1,18,1,1024]{3,2,1,0:T(1,128)S(1)} %get-tuple-element.17), channel_id=1, source_target_pairs={{0,1},{1,2},{2,3},{3,4},{4,5},{5,6},{6,7},{7,8},{8,9},{9,10},{10,1... | collective-permute-start | bytes 221192 | tf_op jit(solution)/shard_map/ppermute | solution.py:18
  267.1 5.3 %collective-permute-start.9 = (f32[1,1,8,1024]{3,2,1,0:T(8,128)S(1)}, f32[1,1,8,1024]{3,2,1,0:T(8,128)S(1)}, u32[]{:S(2)}, u32[]{:S(2)}) collective-permute-start(f32[1,1,8,1024]{3,2,1,0:T(8,128)S(1)} %get-tuple-element.22), channel_id=1, source_target_pairs={{0,32},{32,64},{64,96},{96,128},{128,160},{160,192},{192,224},{1,3... | collective-permute-start | bytes 98312 | tf_op jit(solution)/shard_map/ppermute | solution.py:18
  271.1 4.9 %collective-permute-start.8 = (f32[1,1,8,1024]{3,2,1,0:T(8,128)S(1)}, f32[1,1,8,1024]{3,2,1,0:T(8,128)S(1)}, u32[]{:S(2)}, u32[]{:S(2)}) collective-permute-start(f32[1,1,8,1024]{3,2,1,0:T(8,128)S(1)} %get-tuple-element.23), channel_id=1, source_target_pairs={{32,0},{64,32},{96,64},{128,96},{160,128},{192,160},{224,192},{33,... | collective-permute-start | bytes 98312 | tf_op jit(solution)/shard_map/ppermute | solution.py:20
  276.1 7.5 %collective-permute-start.10 = (f32[1,18,1,1024]{3,2,1,0:T(1,128)S(1)}, f32[1,18,1,1024]{3,2,1,0:T(1,128)S(1)}, u32[]{:S(2)}, u32[]{:S(2)}) collective-permute-start(f32[1,18,1,1024]{3,2,1,0:T(1,128)S(1)} %get-tuple-element.14), channel_id=1, source_target_pairs={{1,0},{2,1},{3,2},{4,3},{5,4},{6,5},{7,6},{8,7},{9,8},{10,9},{11,1... | collective-permute-start | bytes 221192 | tf_op jit(solution)/shard_map/ppermute | solution.py:20
  278.1 6.8 %collective-permute-start.11 = (f32[1,18,1,1024]{3,2,1,0:T(1,128)S(1)}, f32[1,18,1,1024]{3,2,1,0:T(1,128)S(1)}, u32[]{:S(2)}, u32[]{:S(2)}) collective-permute-start(f32[1,18,1,1024]{3,2,1,0:T(1,128)S(1)} %get-tuple-element.15), channel_id=1, source_target_pairs={{0,1},{1,2},{2,3},{3,4},{4,5},{5,6},{6,7},{7,8},{8,9},{9,10},{10,1... | collective-permute-start | bytes 221192 | tf_op jit(solution)/shard_map/ppermute | solution.py:18
  285.3 5.0 %collective-permute-start.13 = (f32[1,1,8,1024]{3,2,1,0:T(8,128)S(1)}, f32[1,1,8,1024]{3,2,1,0:T(8,128)S(1)}, u32[]{:S(2)}, u32[]{:S(2)}) collective-permute-start(f32[1,1,8,1024]{3,2,1,0:T(8,128)S(1)} %get-tuple-element.20), channel_id=1, source_target_pairs={{0,32},{32,64},{64,96},{96,128},{128,160},{160,192},{192,224},{1,3... | collective-permute-start | bytes 98312 | tf_op jit(solution)/shard_map/ppermute | solution.py:18
  289.0 4.9 %collective-permute-start.12 = (f32[1,1,8,1024]{3,2,1,0:T(8,128)S(1)}, f32[1,1,8,1024]{3,2,1,0:T(8,128)S(1)}, u32[]{:S(2)}, u32[]{:S(2)}) collective-permute-start(f32[1,1,8,1024]{3,2,1,0:T(8,128)S(1)} %get-tuple-element.21), channel_id=1, source_target_pairs={{32,0},{64,32},{96,64},{128,96},{160,128},{192,160},{224,192},{33,... | collective-permute-start | bytes 98312 | tf_op jit(solution)/shard_map/ppermute | solution.py:20
  294.0 7.5 %collective-permute-start.14 = (f32[1,18,1,1024]{3,2,1,0:T(1,128)S(1)}, f32[1,18,1,1024]{3,2,1,0:T(1,128)S(1)}, u32[]{:S(2)}, u32[]{:S(2)}) collective-permute-start(f32[1,18,1,1024]{3,2,1,0:T(1,128)S(1)} %get-tuple-element.12), channel_id=1, source_target_pairs={{1,0},{2,1},{3,2},{4,3},{5,4},{6,5},{7,6},{8,7},{9,8},{10,9},{11,1... | collective-permute-start | bytes 221192 | tf_op jit(solution)/shard_map/ppermute | solution.py:20
  295.9 83.2 %copy-start.2 = (f32[16,8,1024]{2,1,0:T(8,128)S(1)}, f32[16,8,1024]{2,1,0:T(8,128)}, u32[]{:S(2)}) copy-start(f32[16,8,1024]{2,1,0:T(8,128)} %param.9) | copy-start | bytes 1572868
  296.0 83.2 %copy-start.3 = (f32[16,8,1024]{2,1,0:T(8,128)S(1)}, f32[16,8,1024]{2,1,0:T(8,128)}, u32[]{:S(2)}) copy-start(f32[16,8,1024]{2,1,0:T(8,128)} %param.12) | copy-start | bytes 1572868
  296.0 83.2 %copy-start.4 = (f32[16,8,1024]{2,1,0:T(8,128)S(1)}, f32[16,8,1024]{2,1,0:T(8,128)}, u32[]{:S(2)}) copy-start(f32[16,8,1024]{2,1,0:T(8,128)} %param.13) | copy-start | bytes 1572868
  296.0 7.0 %collective-permute-start.15 = (f32[1,18,1,1024]{3,2,1,0:T(1,128)S(1)}, f32[1,18,1,1024]{3,2,1,0:T(1,128)S(1)}, u32[]{:S(2)}, u32[]{:S(2)}) collective-permute-start(f32[1,18,1,1024]{3,2,1,0:T(1,128)S(1)} %get-tuple-element.13), channel_id=1, source_target_pairs={{0,1},{1,2},{2,3},{3,4},{4,5},{5,6},{6,7},{7,8},{8,9},{9,10},{10,1... | collective-permute-start | bytes 221192 | tf_op jit(solution)/shard_map/ppermute | solution.py:18
Sparse Core Ops, SparseCore 0:
  10.6 52.0 all-gather.1
where the time goes:
time: 388 us; the launch traced here: 387 us
  blocking collectives  275 us (71%)
  starting transfers between devices  50.3 us (13%)
  waiting for transfers between devices  20.5 us (5%)
  other arithmetic  19 us (5%)
  between operations  17.7 us (5%)
  local copies, waits for them, and re-layouts  4.54 us (1%)
    unnamed x1, blocking collectives  120 us
    psum x1, blocking collectives, per_device(): volume = lax.psum(local_volume, ('gx', 'gy'))  81.3 us
    psum x1, blocking collectives, per_device(): total = lax.psum(jnp.sum(raw * raw), ('gx', 'gy'))  74.5 us
    ppermute x8, starting transfers between devices, with_halo(): lax.ppermute(tail, axis, [(i, (i + 1) % count) for i in range(ends)])  29.2 us
    ppermute x8, starting transfers between devices, with_halo(): lax.ppermute(head, axis, [((i + 1) % count, i) for i in range(ends)])  21.1 us
    ppermute x8, waiting for transfers between devices, with_halo(): lax.ppermute(head, axis, [((i + 1) % count, i) for i in range(ends)])  14.4 us
    scatter-add x1, other arithmetic, deliver(): return zeros_rows.at[every_anchor[0]].add(every_values[0] * owned[:, None])  13 us
  transfers between devices with their start and end apart: 17, of which 10 were waited for; matrix products, arithmetic and copies ran while one was open for 1% of the time, Pallas kernels for 0%

commit v1 on v0

v1 whole, which is shorter than its diff:
```python
import functools

import jax
import jax.numpy as jnp
from jax import lax
from jax.experimental import pallas as pl
from jax.experimental.pallas import tpu as pltpu
from jax.sharding import PartitionSpec as P

SWEEPS = 4
ADAM_STEP = 10
CAP = 8
LANES = 128
HALO = 4
F32 = jnp.float32
HIGHEST = lax.Precision.HIGHEST
VMEM_LIMIT = 40 * 1024 * 1024


def params():
    return pltpu.CompilerParams(vmem_limit_bytes=VMEM_LIMIT)


def vmem():
    return pl.BlockSpec(memory_space=pltpu.VMEM)


def smem():
    return pl.BlockSpec(memory_space=pltpu.SMEM)


def iota(shape, dim):
    return lax.broadcasted_iota(jnp.int32, shape, dim)


def bucket_kernel(width_z, values_ref, anchor_ref, owner_ref, out_ref):
    rows = values_ref.shape[0]
    owners = out_ref.shape[0]
    owner = owner_ref[...]
    anchor = anchor_ref[...]
    chunks = width_z // LANES
    place = (anchor // (8 * chunks)) * (8 * chunks) + (anchor % chunks) * 8 + (anchor // chunks) % 8
    down = iota((rows, rows), 0)
    across = iota((rows, rows), 1)
    owner_f = owner.astype(F32)
    owner_column = jnp.sum(
        jnp.where(down == across, jnp.broadcast_to(owner_f, (rows, rows)), 0.0), axis=1, keepdims=True
    )
    earlier = (owner_column == owner_f) & (down < across)
    rank = jnp.sum(jnp.where(earlier, 1.0, 0.0), axis=0, keepdims=True)
    slot = iota((owners * CAP, rows), 0)
    chosen = (slot // CAP == owner) & ((slot % CAP).astype(F32) == rank)
    packed = jnp.dot(
        jnp.where(chosen, 1.0, 0.0), values_ref[...], precision=HIGHEST, preferred_element_type=F32
    )
    out_ref[:, 0:CAP, :] = packed.reshape(owners, CAP, LANES)
    named = jnp.where(iota((owners, rows), 0) == owner, 1.0, 0.0)
    lane = iota((LANES, rows), 0)
    marked = jnp.where((lane % CAP).astype(F32) == rank, place.astype(F32) + 1.0, 0.0)
    anchors = lax.dot_general(
        named, marked, (((1,), (1,)), ((), ())), precision=HIGHEST, preferred_element_type=F32
    )
    out_ref[:, CAP : 2 * CAP, :] = jnp.broadcast_to(anchors[:, None, :] - 1.0, (owners, CAP, LANES))


def bucket(values, anchor, owner, owners, width_z):
    return pl.pallas_call(
        functools.partial(bucket_kernel, width_z),
        out_shape=jax.ShapeDtypeStruct((owners, 2 * CAP, LANES), F32),
        in_specs=[vmem()] * 3,
        out_specs=vmem(),
        compiler_params=params(),
    )(values, anchor, owner)


def source_kernel(recv_ref, filtered_ref, sensitivity_ref, lagrange_ref, s_ref, low_ref, high_ref, volume_ref, field):
    width_x, width_y, width_z = filtered_ref.shape
    chunks = width_z // LANES
    owners = recv_ref.shape[0]
    group = LANES // CAP
    sent = recv_ref[:, CAP, :]
    peer = iota(sent.shape, 0)
    lane = iota(sent.shape, 1)
    kept = jnp.where(lane // CAP == peer % group, sent + 1.0, 0.0)
    anchors = [
        jnp.sum(kept[g : g + group], axis=0, keepdims=True) - 1.0 for g in range(0, owners, group)
    ]
    anchors = jnp.concatenate(anchors, axis=1) if len(anchors) > 1 else anchors[0][:, : owners * CAP]
    values = recv_ref[:, 0:CAP, :].reshape(owners * CAP, LANES)
    top = values.astype(jnp.bfloat16)
    rest = values - top.astype(F32)
    middle = rest.astype(jnp.bfloat16)
    last = (rest - middle.astype(F32)).astype(jnp.bfloat16)
    parts = jnp.concatenate([top, middle, last], axis=1)
    block_rows = width_x * width_y * chunks
    step = min(block_rows, 256)
    for start in range(0, block_rows, step):
        row = (iota((step, owners * CAP), 0) + start).astype(F32)
        hot = jnp.where(row == anchors, 1.0, 0.0).astype(jnp.bfloat16)
        added = jnp.dot(hot, parts, preferred_element_type=F32)
        field[start : start + step, :] = (
            added[:, 0:LANES] + added[:, LANES : 2 * LANES] + added[:, 2 * LANES : 3 * LANES]
        )
    base = lagrange_ref[0] + 0.25 * lagrange_ref[1]
    edge = jnp.tanh(jnp.full((8, LANES), 4.0, F32))
    inverse = 1.0 / (edge + edge)
    eight = 8.0 * inverse

    def layer(x, total):
        for c in range(chunks):
            at = pl.ds(c * LANES, LANES)
            part = jnp.tanh(8.0 * (filtered_ref[x, :, at] - 0.5))
            total = total + (edge + part) * inverse
            slope = (1.0 - part * part) * eight
            trace = field[pl.ds(pl.multiple_of((x * chunks + c) * 8, 8), 8), :]
            s_ref[0, x, :, at] = slope * ((sensitivity_ref[x, :, at] + trace) + base)
            s_ref[1, x, :, at] = slope
        return total

    volume_ref[...] = lax.fori_loop(0, width_x, layer, jnp.zeros((8, LANES), F32))
    low_ref[...] = s_ref[:, 0:HALO]
    high_ref[...] = s_ref[:, width_x - HALO :]


def make_source(recv, filtered, sensitivity, lagrange):
    width_x, width_y, width_z = filtered.shape
    face = jax.ShapeDtypeStruct((2, HALO, width_y, width_z), F32)
    return pl.pallas_call(
        source_kernel,
        out_shape=(
            jax.ShapeDtypeStruct((2, width_x, width_y, width_z), F32),
            face,
            face,
            jax.ShapeDtypeStruct((8, LANES), F32),
        ),
        in_specs=[vmem(), vmem(), vmem(), smem()],
        out_specs=(vmem(),) * 4,
        scratch_shapes=[pltpu.VMEM((width_x * width_y * width_z // LANES, LANES), F32)],
        compiler_params=params(),
    )(recv, filtered, sensitivity, lagrange)


def pack_kernel(s_ref, left_ref, right_ref, low_ref, high_ref):
    width_x, width_y, width_z = s_ref.shape[1:]
    row = iota((width_y, width_z), 0)
    half = row < 4
    for f in range(2):
        for i in range(width_x // 2):
            even, odd = s_ref[f, 2 * i], pltpu.roll(s_ref[f, 2 * i + 1], 4, 0)
            low_ref[f, i] = jnp.where(half, even, odd)
            high_ref[f, i] = jnp.where(half, odd, even)
        for i, (near, mid, far) in enumerate(
            ((left_ref[f, 3], left_ref[f, 2], left_ref[f, 1]), (right_ref[f, 0], right_ref[f, 1], right_ref[f, 2]))
        ):
            tile = width_x // 2 + i
            mid = pltpu.roll(mid, 4, 0)
            low_ref[f, tile] = jnp.where(row < 3, near, jnp.where(row == 3, pltpu.roll(far, 3, 0), mid))
            high_ref[f, tile] = jnp.where(row > 4, near, jnp.where(row == 4, pltpu.roll(far, 5, 0), mid))


def pack(s, left, right):
    _, width_x, width_y, width_z = s.shape
    face = jax.ShapeDtypeStruct((2, width_x // 2 + 2, width_y, width_z), F32)
    return pl.pallas_call(
        pack_kernel,
        out_shape=(face, face),
        in_specs=[vmem()] * 3,
        out_specs=(vmem(),) * 2,
        compiler_params=params(),
    )(s, left, right)


def smooth_kernel(
    s_ref, left_ref, right_ref, above_ref, below_ref, volume_ref, inside_ref, raw_ref, sums_ref, source, first, second
):
    width_x, width_y, width_z = s_ref.shape[1:]
    chunks = width_z // LANES
    layers = width_x + 2 * HALO
    inside_left = inside_ref[0]
    inside_right = inside_ref[1]
    row = iota((width_y, LANES), 0)
    lane = iota((width_y, LANES), 1)
    half = row < 4
    rim = jnp.where(half, inside_ref[3], inside_ref[2])
    wide_half = iota((width_y, width_z), 0) < 4
    wide_rim = jnp.where(wide_half, inside_ref[3], inside_ref[2])

    for f in range(2):
        source[f, 0, 0:HALO] = left_ref[f] * inside_left
        source[f, 0, HALO : HALO + width_x] = s_ref[f]
        source[f, 0, HALO + width_x :] = right_ref[f] * inside_right
        for i in range(width_x // 2):
            low, high = above_ref[f, i], below_ref[f, i]
            source[f, 1, HALO + 2 * i] = jnp.where(wide_half, low, high) * wide_rim
            source[f, 1, HALO + 2 * i + 1] = pltpu.roll(jnp.where(wide_half, high, low), 4, 0) * wide_rim
        for i, (near, step, keep) in enumerate(((HALO - 1, -1, inside_left), (HALO + width_x, 1, inside_right))):
            low, high = above_ref[f, width_x // 2 + i], below_ref[f, width_x // 2 + i]
            scale = wide_rim * keep
            source[f, 1, near] = jnp.where(wide_half, low, high) * scale
            source[f, 1, near + step] = pltpu.roll(jnp.where(wide_half, high, low), 4, 0) * scale
            source[f, 1, near + 2 * step] = (
                jnp.where(wide_half, pltpu.roll(low, 5, 0), pltpu.roll(high, 3, 0)) * scale
            )
            source[f, 1, near + 3 * step] = jnp.zeros((width_y, width_z), F32)

    def load(ref, f, tile, x):
        return [ref[f, tile, x, :, pl.ds(c * LANES, LANES)] for c in range(chunks)]

    def along_z(v):
        up = [pltpu.roll(t, LANES - 1, 1) for t in v]
        down = [pltpu.roll(t, 1, 1) for t in v]
        zero = jnp.zeros_like(v[0])
        return [
            jnp.where(lane == LANES - 1, up[c + 1] if c + 1 < chunks else zero, up[c])
            + jnp.where(lane == 0, down[c - 1] if c else zero, down[c])
            for c in range(chunks)
        ]

    def step(ref, f, x, both, weight):
        a, b = load(ref, f, 0, x), load(ref, f, 1, x)
        results = []
        a_z = along_z(a)
        b_z = along_z(b) if both else None
        out_a, out_b = [], []
        for c in range(chunks):
            at = pl.ds(c * LANES, LANES)
            a_up, b_up = pltpu.roll(a[c], 7, 0), pltpu.roll(b[c], 7, 0)
            a_down, b_down = pltpu.roll(a[c], 1, 0), pltpu.roll(b[c], 1, 0)
            sum_a = jnp.where(row == 7, b_up, a_up) + jnp.where(row == 0, b_down, a_down)
            sum_a = sum_a + a_z[c] + (ref[f, 0, x - 1, :, at] + ref[f, 0, x + 1, :, at])
            out_a.append(sum_a + weight * source[f, 0, x, :, at])
            if both:
                sum_b = jnp.where(row == 7, a_up, b_up) + jnp.where(row == 0, a_down, b_down)
                sum_b = sum_b + b_z[c] + (ref[f, 1, x - 1, :, at] + ref[f, 1, x + 1, :, at])
                out_b.append((sum_b + weight * source[f, 1, x, :, at]) * rim)
        return out_a, out_b

    def store(ref, f, tile, x, values, keep=None):
        for c in range(chunks):
            ref[f, tile, x, :, pl.ds(c * LANES, LANES)] = values[c] if keep is None else values[c] * keep

    refs = (source, first, second, first)
    for k in range(1, SWEEPS):
        weight = (25.0 / 4.0) ** k / 25.0
        reach = SWEEPS - k
        old, new = refs[k - 1], refs[k]
        for f in range(2):

            def body(x, carry, f=f, old=old, new=new, weight=weight):
                a, b = step(old, f, x, True, weight)
                store(new, f, 0, x, a)
                store(new, f, 1, x, b)
                return carry

            lax.fori_loop(HALO, HALO + width_x, body, 0)
            for d in range(1, reach + 1):
                for x, keep in ((HALO - d, inside_left), (HALO + width_x - 1 + d, inside_right)):
                    a, b = step(old, f, x, d < reach, weight)
                    store(new, f, 0, x, a, keep)
                    if b:
                        store(new, f, 1, x, b, keep)

    last = refs[SWEEPS - 1]
    weight = (25.0 / 4.0) ** SWEEPS / 25.0
    scale = (4.0 / 25.0) ** SWEEPS

    def finish(x, sums):
        one, _ = step(last, 0, x + HALO, False, weight)
        two, _ = step(last, 1, x + HALO, False, weight)
        aa, ab, bb = sums
        for c in range(chunks):
            at = pl.ds(c * LANES, LANES)
            u, v = one[c] * scale, two[c] * scale
            raw_ref[0, x, :, at] = u
            raw_ref[1, x, :, at] = v
            aa, ab, bb = aa + u * u, ab + u * v, bb + v * v
        return aa, ab, bb

    zeros = jnp.zeros((8, LANES), F32)
    aa, ab, bb = lax.fori_loop(0, width_x, finish, (zeros, zeros, zeros))
    rows = [jnp.sum(t, axis=0, keepdims=True) for t in (volume_ref[...], aa, ab, bb)]
    tile = jnp.where(
        row == 0, rows[0], jnp.where(row == 1, rows[1], jnp.where(row == 2, rows[2], jnp.where(row == 3, rows[3], 0.0)))
    )
    for i in range(sums_ref.shape[0]):
        sums_ref[i] = tile


def smooth(s, left, right, above, below, volume, inside, copies):
    _, width_x, width_y, width_z = s.shape
    extended = pltpu.VMEM((2, 2, width_x + 2 * HALO, width_y, width_z), F32)
    return pl.pallas_call(
        smooth_kernel,
        out_shape=(
            jax.ShapeDtypeStruct(s.shape, F32),
            jax.ShapeDtypeStruct((copies, 8, LANES), F32),
        ),
        in_specs=[vmem()] * 6 + [smem()],
        out_specs=(vmem(),) * 2,
        scratch_shapes=[extended] * 3,
        compiler_params=params(),
    )(s, left, right, above, below, volume, inside)


def adam_kernel(
    cells, sums_ref, lagrange_ref, raw_ref, design_ref, first_ref, second_ref, d_ref, m_ref, v_ref, g_ref
):
    sums = jnp.sum(sums_ref[...], axis=0)
    volume = jnp.sum(sums[0:1], axis=1, keepdims=True)
    shift = lagrange_ref[1] * (volume / cells / 0.4 - 1.25)
    total = jnp.sum(sums[1:2] + 2.0 * shift * sums[2:3] + shift * shift * sums[3:4], axis=1, keepdims=True)
    inverse = 1.0 / jnp.sqrt(jnp.maximum(total, 0.0) / cells + 1e-06)
    gradient = (raw_ref[0] + shift[:, :, None] * raw_ref[1]) * inverse[:, :, None]
    new_first = 0.9 * first_ref[...] + 0.1 * gradient
    new_second = 0.999 * second_ref[...] + 0.001 * gradient * gradient
    first_hat = new_first / (1.0 - 0.9**ADAM_STEP)
    second_hat = new_second / (1.0 - 0.999**ADAM_STEP)
    d_ref[...] = jnp.clip(design_ref[...] - 0.05 * first_hat / (jnp.sqrt(second_hat) + 1e-08), 0.0, 1.0)
    m_ref[...] = new_first
    v_ref[...] = new_second
    g_ref[...] = gradient


def adam(cells, sums, lagrange, raw, design, first_moment, second_moment):
    width_x, width_y, width_z = design.shape
    steps = 4
    block = (width_x // steps, width_y, width_z)
    spec = pl.BlockSpec(block, lambda i: (i, 0, 0))
    return pl.pallas_call(
        functools.partial(adam_kernel, cells),
        grid=(steps,),
        out_shape=(jax.ShapeDtypeStruct(design.shape, F32),) * 4,
        in_specs=[
            pl.BlockSpec(sums.shape, lambda i: (0, 0, 0)),
            smem(),
            pl.BlockSpec((2,) + block, lambda i: (0, i, 0, 0)),
            spec,
            spec,
            spec,
        ],
        out_specs=(spec,) * 4,
        compiler_params=params(),
    )(sums, lagrange, raw, design, first_moment, second_moment)


def shift(cells, axis, by):
    count = lax.axis_size(axis)
    return lax.ppermute(cells, axis, [(i, (i + by) % count) for i in range(count)])


def per_device(
    design,
    filtered,
    sensitivity,
    first_moment,
    second_moment,
    lagrange,
    trace_values,
    trace_anchor,
    trace_owner,
):
    width_x, width_y, depth = design.shape
    count_x, count_y = lax.axis_size("gx"), lax.axis_size("gy")
    cells = float(width_x * width_y * depth * count_x * count_y)
    index_x, index_y = lax.axis_index("gx"), lax.axis_index("gy")
    inside = jnp.stack([index_x > 0, index_x < count_x - 1, index_y > 0, index_y < count_y - 1]).astype(F32)

    rows = trace_values.shape[1]
    sent = bucket(trace_values[0], trace_anchor, trace_owner.reshape(1, rows), count_y, depth)
    received = lax.all_to_all(sent, "gy", 0, 0, tiled=True)
    s, low, high, volume = make_source(received, filtered, sensitivity, lagrange)
    left, right = shift(high, "gx", 1), shift(low, "gx", -1)
    low, high = pack(s, left, right)
    below, above = shift(high, "gy", 1), shift(low, "gy", -1)
    raw, sums = smooth(s, left, right, above, below, volume, inside, count_x)
    sums = jnp.sum(lax.all_to_all(sums, "gx", 0, 0, tiled=True), axis=0)
    sums = lax.all_to_all(jnp.broadcast_to(sums[None], (count_y,) + sums.shape), "gy", 0, 0, tiled=True)
    return adam(cells, sums, lagrange, raw, design, first_moment, second_moment)


def solution(mesh):
    block = P("gx", "gy", None)
    return jax.shard_map(
        per_device,
        mesh=mesh,
        in_specs=(block, block, block, block, block, P(), block, P("gx", "gy"), block),
        out_specs=(block, block, block, block),
        check_vma=False,
    )
```

time: 388 us -> 98 us (0.25)
  blocking collectives: 275 us -> 46.2 us
  starting transfers between devices: 50.3 us -> 7.48 us
  Pallas kernels: 0 us -> 19.7 us
  other arithmetic: 19 us -> 0.09 us
  between operations: 17.7 us -> 0.7 us
  waiting for transfers between devices: 20.5 us -> 15.1 us
    psum x2 -> x0, blocking collectives: 156 us -> none  [the longest x1 81.3 us: per_device(): volume = lax.psum(local_volume, ('gx', 'gy'))]
    unnamed x1 -> x0, blocking collectives: 120 us -> none
    all_to_all x0 -> x3, blocking collectives: none -> 46.2 us  [the longest x1 17.3 us: per_device(): received = lax.all_to_all(sent, 'gy', 0, 0, tiled=True)]
    ppermute x16 -> x4, starting transfers between devices: 50.2 us -> 7.48 us  [shift(): lax.ppermute(cells, axis, [(i, (i + by) % count) for i in range(count)])]
    pallas_call x0 -> x5, Pallas kernels: none -> 19.7 us  [the longest x1 13.6 us: smooth(): pl.pallas_call(smooth_kernel, out_shape=(jax.ShapeDtypeStruct(s.shape, F3...]
    scatter-add x1 -> x0, other arithmetic: 13 us -> none  [deliver(): return zeros_rows.at[every_anchor[0]].add(every_values[0] * owned[:, None])]
    ppermute x16 -> x4, waiting for transfers between devices: 19.8 us -> 15.1 us  [shift(): lax.ppermute(cells, axis, [(i, (i + by) % count) for i in range(count)])]
    unnamed x23 -> x22, local copies, waits for them, and re-layouts: 3.85 us -> 8.23 us
  transfers between devices with their start and end apart: 17 -> 4, of which waited for: 10 -> 2; matrix products, arithmetic and copies ran while one was open for 1% -> 0% of each run, Pallas kernels for 0% -> 0%
where the time goes in v1:
time: 98 us; the launch traced here: 97.5 us
  blocking collectives  46.2 us (47%)
  Pallas kernels  19.7 us (20%)
  waiting for transfers between devices  15.1 us (15%)
  local copies, waits for them, and re-layouts  8.24 us (8%)
  starting transfers between devices  7.48 us (8%)
    all_to_all x1, blocking collectives, per_device(): received = lax.all_to_all(sent, 'gy', 0, 0, tiled=True)  17.3 us
    all_to_all x1, blocking collectives, per_device(): lax.all_to_all(jnp.broadcast_to(sums[None], (count_y,) + sums.shape), 'gy...  17.3 us
    ppermute x4, waiting for transfers between devices, shift(): lax.ppermute(cells, axis, [(i, (i + by) % count) for i in range(count)])  15.1 us
    pallas_call x1, Pallas kernels, smooth(): pl.pallas_call(smooth_kernel, out_shape=(jax.ShapeDtypeStruct(s.shape, F3...  13.6 us
    all_to_all x1, blocking collectives, per_device(): sums = jnp.sum(lax.all_to_all(sums, 'gx', 0, 0, tiled=True), axis=0)  11.6 us
    unnamed x22, local copies, waits for them, and re-layouts  8.23 us
    ppermute x4, starting transfers between devices, shift(): lax.ppermute(cells, axis, [(i, (i + by) % count) for i in range(count)])  7.48 us
    pallas_call x1, Pallas kernels, adam(): pl.pallas_call(functools.partial(adam_kernel, cells), grid=(steps,), out_...  3.07 us
  transfers between devices with their start and end apart: 4, of which 2 were waited for; matrix products, arithmetic and copies ran while one was open for 0% of the time, Pallas kernels for 0%

profile of v1, /device:TPU:1, one launch (start us, length us, event | category | flops | bytes accessed | tf_op | source)
XLA Modules:
  0.0 97.5 jit_solution(5269043327984469785)
XLA Ops:
  0.6 0.0 copy-start.2
  0.6 0.0 copy-start.7
  0.7 0.8 copy-done.7
  1.5 0.0 copy-start.9
  1.5 0.7 copy-done.9
  2.1 0.0 copy-start.10
  2.1 0.7 copy-done.10
  2.8 0.4 shard_map.120
  3.2 0.0 copy-start.8
  3.2 17.3 %all_to_all.15.recv_ref = f32[32,16,128]{2,1,0:T(8,128)S(1)} all-to-all(f32[32,16,128]{2,1,0:T(8,128)S(1)} %shard_map.120), channel_id=1, replica_groups=mesh['gx'=8,'gy'=32] {'gy'}, dimensions={0} | all-to-all | bytes 524288 | tf_op jit(solution)/shard_map/all_to_all | solution.py:370
  20.5 0.0 copy-done.2
  20.5 0.0 copy-done.8
  20.5 0.0 copy-start.3
  20.5 1.0 %copy-done.3 = f32[16,8,1024]{2,1,0:T(8,128)S(1)} copy-done((f32[16,8,1024]{2,1,0:T(8,128)S(1)}, f32[16,8,1024]{2,1,0:T(8,128)}, u32[]{:S(2)}) %copy-start.3) | copy-done | bytes 524312
  21.6 1.4 %shard_map.121 = (f32[2,16,8,1024]{3,2,1,0:T(8,128)S(1)}, f32[2,4,8,1024]{3,2,1,0:T(8,128)S(1)}, f32[2,4,8,1024]{3,2,1,0:T(8,128)S(1)}, f32[8,128]{1,0:T(8,128)S(1)}) custom-call(f32[32,16,128]{2,1,0:T(8,128)S(1)} %all_to_all.15.recv_ref, f32[16,8,1024]{2,1,0:T(8,128)S(1)} %copy-done.2, f32[16,8,1024]{2,1,0:T(8,128)S(1)} %copy-done.3, f32[2]{0:T(128)S(1)} %copy-done.8), custom_call_target="tpu_custom_call" | custom-call | tf_op jit(solution)/shard_map/pallas_call | solution.py:128
  23.0 1.7 %collective-permute-start = (f32[2,4,8,1024]{3,2,1,0:T(8,128)S(1)}, f32[2,4,8,1024]{3,2,1,0:T(8,128)S(1)}, u32[]{:S(2)}, u32[]{:S(2)}) collective-permute-start(f32[2,4,8,1024]{3,2,1,0:T(8,128)S(1)} %get-tuple-element.13), channel_id=1, source_target_pairs={{0,32},{32,64},{64,96},{96,128},{128,160},{160,192},{192,224},{224... | collective-permute-start | bytes 786440 | tf_op jit(solution)/shard_map/ppermute | solution.py:348
  24.7 4.0 %collective-permute-start.1 = (f32[2,4,8,1024]{3,2,1,0:T(8,128)S(1)}, f32[2,4,8,1024]{3,2,1,0:T(8,128)S(1)}, u32[]{:S(2)}, u32[]{:S(2)}) collective-permute-start(f32[2,4,8,1024]{3,2,1,0:T(8,128)S(1)} %get-tuple-element.14), channel_id=1, source_target_pairs={{0,224},{32,0},{64,32},{96,64},{128,96},{160,128},{192,160},{224,1... | collective-permute-start | bytes 786440 | tf_op jit(solution)/shard_map/ppermute | solution.py:348
  28.7 6.4 %collective-permute-done.left_ref = f32[2,4,8,1024]{3,2,1,0:T(8,128)S(1)} collective-permute-done((f32[2,4,8,1024]{3,2,1,0:T(8,128)S(1)}, f32[2,4,8,1024]{3,2,1,0:T(8,128)S(1)}, u32[]{:S(2)}, u32[]{:S(2)}) %collective-permute-start) | collective-permute-done | bytes 262176 | tf_op jit(solution)/shard_map/ppermute | solution.py:348
  35.1 0.0 collective-permute-done.1.right_ref
  35.1 1.2 %shard_map.122 = (f32[2,10,8,1024]{3,2,1,0:T(8,128)}, f32[2,10,8,1024]{3,2,1,0:T(8,128)}) custom-call(f32[2,16,8,1024]{3,2,1,0:T(8,128)S(1)} %get-tuple-element.12.s_ref, f32[2,4,8,1024]{3,2,1,0:T(8,128)S(1)} %collective-permute-done.left_ref, f32[2,4,8,1024]{3,2,1,0:T(8,128)S(1)} %collective-permute-done.1.right_ref), custom_call_target="tpu_custom_call" | custom-call | tf_op jit(solution)/shard_map/pallas_call | solution.py:164
  36.3 0.7 collective-permute-start.2
  37.0 1.0 %collective-permute-start.3 = (f32[2,10,8,1024]{3,2,1,0:T(8,128)}, f32[2,10,8,1024]{3,2,1,0:T(8,128)S(1)}, u32[]{:S(2)}, u32[]{:S(2)}) collective-permute-start(f32[2,10,8,1024]{3,2,1,0:T(8,128)} %get-tuple-element.16), channel_id=1, source_target_pairs={{0,1},{1,2},{2,3},{3,4},{4,5},{5,6},{6,7},{7,8},{8,9},{9,10},{10,1... | collective-permute-start | bytes 1966088 | tf_op jit(solution)/shard_map/ppermute | solution.py:348
  38.1 0.1 add_convert_fusion.inside_ref
  38.1 8.7 %collective-permute-done.2.above_ref = f32[2,10,8,1024]{3,2,1,0:T(8,128)S(1)} collective-permute-done((f32[2,10,8,1024]{3,2,1,0:T(8,128)}, f32[2,10,8,1024]{3,2,1,0:T(8,128)S(1)}, u32[]{:S(2)}, u32[]{:S(2)}) %collective-permute-start.2) | collective-permute-done | bytes 655392 | tf_op jit(solution)/shard_map/ppermute | solution.py:348
  46.8 0.0 collective-permute-done.3.below_ref
  46.8 0.0 copy-start
  46.8 0.8 copy-done
  47.7 0.0 copy-start.1
  47.7 1.1 %copy-done.1 = f32[2,10,8,1024]{3,2,1,0:T(8,128)S(1)} copy-done((f32[2,10,8,1024]{3,2,1,0:T(8,128)S(1)}, f32[2,10,8,1024]{3,2,1,0:T(8,128)}, u32[]{:S(2)}) %copy-start.1) | copy-done | bytes 655384
  48.8 13.6 %shard_map.123 = (f32[2,16,8,1024]{3,2,1,0:T(8,128)S(1)}, f32[8,8,128]{2,1,0:T(8,128)S(1)}) custom-call(f32[2,16,8,1024]{3,2,1,0:T(8,128)S(1)} %get-tuple-element.12.s_ref, f32[2,4,8,1024]{3,2,1,0:T(8,128)S(1)} %collective-permute-done.left_ref, f32[2,4,8,1024]{3,2,1,0:T(8,128)S(1)} %collective-permute-done.1.right_ref, ...), custom_call_target="tpu_custom_call" | custom-call | tf_op jit(solution)/shard_map/pallas_call | solution.py:292
  62.4 11.6 %all_to_all.16 = f32[8,8,128]{2,1,0:T(8,128)S(1)} all-to-all(f32[8,8,128]{2,1,0:T(8,128)S(1)} %get-tuple-element.18), channel_id=1, replica_groups=mesh['gx'=8,'gy'=32] {'gx'}, dimensions={0} | all-to-all | bytes 65536 | tf_op jit(solution)/shard_map/all_to_all | solution.py:376
  74.0 17.3 %all_to_all.17.sums_ref = f32[32,8,128]{2,1,0:T(8,128)S(1)} all-to-all(f32[32,8,128]{2,1,0:T(8,128)S(1)} %broadcast_in_dim.2), channel_id=1, replica_groups=mesh['gx'=8,'gy'=32] {'gy'}, dimensions={0} | all-to-all | bytes 262144 | tf_op jit(solution)/shard_map/all_to_all | solution.py:377
  91.3 0.0 copy-start.4
  91.3 1.0 %copy-done.4 = f32[16,8,1024]{2,1,0:T(8,128)S(1)} copy-done((f32[16,8,1024]{2,1,0:T(8,128)S(1)}, f32[16,8,1024]{2,1,0:T(8,128)}, u32[]{:S(2)}) %copy-start.4) | copy-done | bytes 524312
  92.3 0.0 copy-start.5
  92.3 1.0 %copy-done.5 = f32[16,8,1024]{2,1,0:T(8,128)S(1)} copy-done((f32[16,8,1024]{2,1,0:T(8,128)S(1)}, f32[16,8,1024]{2,1,0:T(8,128)}, u32[]{:S(2)}) %copy-start.5) | copy-done | bytes 524312
  93.4 0.0 copy-start.6
  93.4 1.0 %copy-done.6 = f32[16,8,1024]{2,1,0:T(8,128)S(1)} copy-done((f32[16,8,1024]{2,1,0:T(8,128)S(1)}, f32[16,8,1024]{2,1,0:T(8,128)}, u32[]{:S(2)}) %copy-start.6) | copy-done | bytes 524312
  94.4 3.1 %shard_map.124 = (f32[16,8,1024]{2,1,0:T(8,128)}, f32[16,8,1024]{2,1,0:T(8,128)}, f32[16,8,1024]{2,1,0:T(8,128)}, f32[16,8,1024]{2,1,0:T(8,128)}) custom-call(f32[32,8,128]{2,1,0:T(8,128)S(1)} %all_to_all.17.sums_ref, f32[2]{0:T(128)S(1)} %copy-done.8, f32[2,16,8,1024]{3,2,1,0:T(8,128)S(1)} %get-tuple-element.19.raw_ref, f32[16,8,1024]{2,1,0:T(8,128)S(1)} %copy-done.4, ...), custom_call_target="tpu_custom_call" | custom-call | tf_op jit(solution)/shard_map/pallas_call | solution.py:329
  (2 shorter events, 0.0 us)
Async XLA Ops:
  0.6 19.9 %copy-start.2 = (f32[16,8,1024]{2,1,0:T(8,128)S(1)}, f32[16,8,1024]{2,1,0:T(8,128)}, u32[]{:S(2)}) copy-start(f32[16,8,1024]{2,1,0:T(8,128)} %filtered_ref.1) | copy-start | bytes 1572868
  0.6 0.8 copy-start.7
  1.5 0.7 copy-start.9
  2.1 0.7 copy-start.10
  3.2 17.3 %copy-start.8 = (f32[2]{0:T(128)S(1)}, f32[2]{0:T(128)}, u32[]{:S(2)}) copy-start(f32[2]{0:T(128)} %lagrange_ref.3) | copy-start | bytes 28
  20.5 1.0 %copy-start.3 = (f32[16,8,1024]{2,1,0:T(8,128)S(1)}, f32[16,8,1024]{2,1,0:T(8,128)}, u32[]{:S(2)}) copy-start(f32[16,8,1024]{2,1,0:T(8,128)} %sensitivity_ref.1) | copy-start | bytes 1572868
  23.0 12.2 %collective-permute-start = (f32[2,4,8,1024]{3,2,1,0:T(8,128)S(1)}, f32[2,4,8,1024]{3,2,1,0:T(8,128)S(1)}, u32[]{:S(2)}, u32[]{:S(2)}) collective-permute-start(f32[2,4,8,1024]{3,2,1,0:T(8,128)S(1)} %get-tuple-element.13), channel_id=1, source_target_pairs={{0,32},{32,64},{64,96},{96,128},{128,160},{160,192},{192,224},{224... | collective-permute-start | bytes 786440 | tf_op jit(solution)/shard_map/ppermute | solution.py:348
  24.7 10.5 %collective-permute-start.1 = (f32[2,4,8,1024]{3,2,1,0:T(8,128)S(1)}, f32[2,4,8,1024]{3,2,1,0:T(8,128)S(1)}, u32[]{:S(2)}, u32[]{:S(2)}) collective-permute-start(f32[2,4,8,1024]{3,2,1,0:T(8,128)S(1)} %get-tuple-element.14), channel_id=1, source_target_pairs={{0,224},{32,0},{64,32},{96,64},{128,96},{160,128},{192,160},{224,1... | collective-permute-start | bytes 786440 | tf_op jit(solution)/shard_map/ppermute | solution.py:348
  36.3 10.5 %collective-permute-start.2 = (f32[2,10,8,1024]{3,2,1,0:T(8,128)}, f32[2,10,8,1024]{3,2,1,0:T(8,128)S(1)}, u32[]{:S(2)}, u32[]{:S(2)}) collective-permute-start(f32[2,10,8,1024]{3,2,1,0:T(8,128)} %get-tuple-element.15), channel_id=1, source_target_pairs={{0,31},{1,0},{2,1},{3,2},{4,3},{5,4},{6,5},{7,6},{8,7},{9,8},{10,9... | collective-permute-start | bytes 1966088 | tf_op jit(solution)/shard_map/ppermute | solution.py:348
  37.0 9.8 %collective-permute-start.3 = (f32[2,10,8,1024]{3,2,1,0:T(8,128)}, f32[2,10,8,1024]{3,2,1,0:T(8,128)S(1)}, u32[]{:S(2)}, u32[]{:S(2)}) collective-permute-start(f32[2,10,8,1024]{3,2,1,0:T(8,128)} %get-tuple-element.16), channel_id=1, source_target_pairs={{0,1},{1,2},{2,3},{3,4},{4,5},{5,6},{6,7},{7,8},{8,9},{9,10},{10,1... | collective-permute-start | bytes 1966088 | tf_op jit(solution)/shard_map/ppermute | solution.py:348
  46.8 0.8 copy-start
  47.7 1.1 %copy-start.1 = (f32[2,10,8,1024]{3,2,1,0:T(8,128)S(1)}, f32[2,10,8,1024]{3,2,1,0:T(8,128)}, u32[]{:S(2)}) copy-start(f32[2,10,8,1024]{3,2,1,0:T(8,128)} %copy-done) | copy-start | bytes 1966084
  91.3 1.0 %copy-start.4 = (f32[16,8,1024]{2,1,0:T(8,128)S(1)}, f32[16,8,1024]{2,1,0:T(8,128)}, u32[]{:S(2)}) copy-start(f32[16,8,1024]{2,1,0:T(8,128)} %design_ref.1) | copy-start | bytes 1572868
  92.3 1.0 %copy-start.5 = (f32[16,8,1024]{2,1,0:T(8,128)S(1)}, f32[16,8,1024]{2,1,0:T(8,128)}, u32[]{:S(2)}) copy-start(f32[16,8,1024]{2,1,0:T(8,128)} %first_ref.1) | copy-start | bytes 1572868
  93.4 1.0 %copy-start.6 = (f32[16,8,1024]{2,1,0:T(8,128)S(1)}, f32[16,8,1024]{2,1,0:T(8,128)}, u32[]{:S(2)}) copy-start(f32[16,8,1024]{2,1,0:T(8,128)} %second_ref.1) | copy-start | bytes 1572868

commit v2 on v0

v2 whole, which is shorter than its diff:
```python
import functools

import jax
import jax.numpy as jnp
from jax import lax
from jax.experimental import pallas as pl
from jax.experimental.pallas import tpu as pltpu
from jax.sharding import PartitionSpec as P

SWEEPS = 4
ADAM_STEP = 10
CAP = 8
LANES = 128
HALO = 4
TALL = 16
GUARD = 8
FACE_ROWS = (8, 10, 12, 14)
FACE = sum(FACE_ROWS)
F32 = jnp.float32
BF16 = jnp.bfloat16
HIGHEST = lax.Precision.HIGHEST
MIB = 1024 * 1024


def params(mib):
    return pltpu.CompilerParams(vmem_limit_bytes=mib * MIB)


VMEM = pl.BlockSpec(memory_space=pltpu.VMEM)
SMEM = pl.BlockSpec(memory_space=pltpu.SMEM)
HBM = pl.BlockSpec(memory_space=pltpu.HBM)


def iota(shape, dim):
    return lax.broadcasted_iota(jnp.int32, shape, dim)


def start_all(pairs, sems):
    copies = [pltpu.make_async_copy(src, dst, sems.at[i]) for i, (src, dst) in enumerate(pairs)]
    for copy in copies:
        copy.start()
    return copies


def send_kernel(
    values_hbm, anchor_hbm, owner_hbm, filtered_hbm, sensitivity_hbm,
    out_ref, low_ref, high_ref, filtered_ref, sensitivity_ref,
    values_ref, anchor_ref, owner_ref, sems,
):
    copies = start_all(
        (
            (anchor_hbm, anchor_ref),
            (owner_hbm, owner_ref),
            (values_hbm, values_ref),
            (filtered_hbm, filtered_ref),
            (sensitivity_hbm, sensitivity_ref),
        ),
        sems,
    )
    width_x, width_y, width_z = filtered_ref.shape
    chunks = width_z // LANES
    rows = values_ref.shape[0]
    owners = out_ref.shape[0]
    copies[0].wait()
    copies[1].wait()
    owner = owner_ref[...]
    anchor = anchor_ref[...]
    place = (anchor // (8 * chunks)) * (8 * chunks) + (anchor % chunks) * 8 + (anchor // chunks) % 8
    down = iota((rows, rows), 0)
    across = iota((rows, rows), 1)
    owner_f = owner.astype(F32)
    owner_column = jnp.sum(
        jnp.where(down == across, jnp.broadcast_to(owner_f, (rows, rows)), 0.0), axis=1, keepdims=True
    )
    earlier = (owner_column == owner_f) & (down < across)
    rank = jnp.sum(jnp.where(earlier, 1.0, 0.0), axis=0, keepdims=True)
    slot = iota((owners * CAP, rows), 0)
    chosen = jnp.where((slot // CAP == owner) & ((slot % CAP).astype(F32) == rank), 1.0, 0.0)
    named = jnp.where(iota((owners, rows), 0) == owner, 1.0, 0.0)
    lane = iota((LANES, rows), 0)
    marked = jnp.where((lane % CAP).astype(F32) == rank, place.astype(F32) + 1.0, 0.0)
    anchors = lax.dot_general(
        named, marked, (((1,), (1,)), ((), ())), precision=HIGHEST, preferred_element_type=F32
    )
    lower = (anchors.astype(jnp.int32) - 1) % 8 < 4
    blank = jnp.zeros((1, LANES), F32)
    from_next = jnp.concatenate([jnp.where(lower, anchors, 0.0)[1:], blank], axis=0)
    from_last = jnp.concatenate([blank, jnp.where(lower, 0.0, anchors)[:-1]], axis=0)
    for i, line in enumerate((anchors, from_next, from_last)):
        out_ref[:, 3 * CAP + i, :] = line
    copies[2].wait()
    packed = jnp.dot(chosen, values_ref[...], precision=HIGHEST, preferred_element_type=F32)
    packed = packed.reshape(owners, CAP, LANES)
    nothing = jnp.zeros((1, CAP, LANES), F32)
    out_ref[:, 0:CAP, :] = packed
    out_ref[0 : owners - 1, CAP : 2 * CAP, :] = packed[1:]
    out_ref[owners - 1 :, CAP : 2 * CAP, :] = nothing
    out_ref[1:, 2 * CAP : 3 * CAP, :] = packed[:-1]
    out_ref[0:1, 2 * CAP : 3 * CAP, :] = nothing
    half = iota((width_y, width_z), 0) < 4
    for f, ref in enumerate((filtered_ref, sensitivity_ref)):
        copies[3 + f].wait()
        for i in range(width_x // 2):
            even, odd = ref[2 * i], pltpu.roll(ref[2 * i + 1], 4, 0)
            low_ref[f, i] = jnp.where(half, even, odd)
            high_ref[f, i] = jnp.where(half, odd, even)


def make_send(values, anchor, owner, filtered, sensitivity, owners):
    width_x, width_y, width_z = filtered.shape
    block = jax.ShapeDtypeStruct(filtered.shape, F32)
    face = jax.ShapeDtypeStruct((2, width_x // 2, width_y, width_z), F32)
    return pl.pallas_call(
        send_kernel,
        out_shape=(jax.ShapeDtypeStruct((owners, 4 * CAP, LANES), F32), face, face, block, block),
        in_specs=[HBM] * 5,
        out_specs=(VMEM,) * 5,
        scratch_shapes=[
            pltpu.VMEM(values.shape, F32),
            pltpu.VMEM(anchor.shape, jnp.int32),
            pltpu.VMEM(owner.shape, jnp.int32),
            pltpu.SemaphoreType.DMA((5,)),
        ],
        compiler_params=params(4),
    )(values, anchor, owner, filtered, sensitivity)


def exact_parts(values):
    top = values.astype(BF16)
    rest = values - top.astype(F32)
    middle = rest.astype(BF16)
    last = (rest - middle.astype(F32)).astype(BF16)
    return jnp.concatenate([top, middle, last], axis=1)


def source_kernel(
    recv_ref, filtered_ref, sensitivity_ref, above_ref, below_ref, lagrange_ref, inside_ref,
    s_ref, low_ref, high_ref, volume_ref, own, beside,
):
    width_x, width_y, width_z = filtered_ref.shape
    chunks = width_z // LANES
    owners = recv_ref.shape[0]
    group = min(LANES // CAP, owners)
    peer = iota((owners, LANES), 0)
    lane = iota((owners, LANES), 1)

    def places(line):
        kept = jnp.where(lane // CAP == peer % group, recv_ref[:, line, :], 0.0)
        sums = [jnp.sum(kept[g : g + group], axis=0, keepdims=True) for g in range(0, owners, group)]
        return [t[:, : group * CAP] for t in sums]

    def slots(start):
        return recv_ref[:, start : start + CAP, :].reshape(owners * CAP, LANES)

    block_rows = width_x * width_y * chunks
    step = min(block_rows, 256)
    for ref, lines, starts in ((own, (24,), (0,)), (beside, (25, 26), (8, 16))):
        anchors = jnp.concatenate([p for line in lines for p in places(line)], axis=1)
        parts = jnp.concatenate([exact_parts(slots(start)) for start in starts], axis=0)
        for start in range(0, block_rows, step):
            row = (iota((step, anchors.shape[1]), 0) + (start + 1)).astype(F32)
            hot = jnp.where(row == anchors, 1.0, 0.0).astype(BF16)
            added = jnp.dot(hot, parts, preferred_element_type=F32)
            ref[start : start + step, :] = (
                added[:, 0:LANES] + added[:, LANES : 2 * LANES] + added[:, 2 * LANES : 3 * LANES]
            )
    base = lagrange_ref[0] + 0.25 * lagrange_ref[1]
    edge = jnp.tanh(jnp.full((8, LANES), 4.0, F32))
    inverse = 1.0 / (edge + edge)
    eight = 8.0 * inverse
    half = iota((width_y, LANES), 0) < 4
    rim = jnp.where(half, inside_ref[3], inside_ref[2]) * eight

    def pair(i, total):
        for c in range(chunks):
            at = pl.ds(c * LANES, LANES)
            sides = [(above_ref[f, i, :, at], below_ref[f, i, :, at]) for f in range(2)]
            for odd in range(2):
                x = 2 * i + odd
                line = pl.ds(pl.multiple_of((x * chunks + c) * 8, 8), 8)
                part = jnp.tanh(8.0 * (filtered_ref[x, :, at] - 0.5))
                total = total + (edge + part) * inverse
                slope = (1.0 - part * part) * eight
                source = slope * ((sensitivity_ref[x, :, at] + own[line, :]) + base)
                density, sense = [
                    pltpu.roll(jnp.where(half, high, low), 4, 0) if odd else jnp.where(half, low, high)
                    for low, high in sides
                ]
                part = jnp.tanh(8.0 * (density - 0.5))
                slope_out = (1.0 - part * part) * rim
                source_out = slope_out * ((sense + beside[line, :]) + base)
                row = pl.multiple_of((x * chunks + c) * TALL, TALL)
                for f, (inner, outer) in enumerate(((source, source_out), (slope, slope_out))):
                    s_ref[f, pl.ds(row, 8), :] = pltpu.roll(jnp.where(half, inner, outer), 4, 0)
                    s_ref[f, pl.ds(row + 8, 8), :] = pltpu.roll(jnp.where(half, outer, inner), 4, 0)
        return total

    volume_ref[...] = lax.fori_loop(0, width_x // 2, pair, jnp.zeros((8, LANES), F32))
    for f in range(2):
        for c in range(chunks):
            to = f * FACE
            for d, count in zip(range(HALO, 0, -1), FACE_ROWS):
                skip = (TALL - count) // 2
                for ref, x in ((low_ref, d - 1), (high_ref, width_x - d)):
                    row = (x * chunks + c) * TALL + skip
                    ref[c, to : to + count, :] = s_ref[f, row : row + count, :]
                to += count


def make_source(recv, filtered, sensitivity, above, below, lagrange, inside):
    width_x, width_y, width_z = filtered.shape
    chunks = width_z // LANES
    face = jax.ShapeDtypeStruct((chunks, 2 * FACE, LANES), F32)
    scratch = pltpu.VMEM((width_x * width_y * chunks, LANES), F32)
    return pl.pallas_call(
        source_kernel,
        out_shape=(
            jax.ShapeDtypeStruct((2, width_x * chunks * TALL, LANES), F32),
            face,
            face,
            jax.ShapeDtypeStruct((8, LANES), F32),
        ),
        in_specs=[VMEM] * 5 + [SMEM] * 2,
        out_specs=(VMEM,) * 4,
        scratch_shapes=[scratch] * 2,
        compiler_params=params(8),
    )(recv, filtered, sensitivity, above, below, lagrange, inside)


def smooth_kernel(
    s_ref, left_ref, right_ref, volume_ref, inside_ref, design_hbm, first_hbm, second_hbm,
    raw_ref, sums_ref, design_ref, first_ref, second_ref, source, one, two, sems,
):
    copies = start_all(((design_hbm, design_ref), (first_hbm, first_ref), (second_hbm, second_ref)), sems)
    width_x, width_y, width_z = raw_ref.shape[1:]
    chunks = width_z // LANES
    layer = chunks * TALL
    inside_left = inside_ref[0]
    inside_right = inside_ref[1]
    row = iota((width_y, LANES), 0)
    lane = iota((width_y, LANES), 1)
    half = row < 4
    rims = (jnp.where(half, inside_ref[2], 1.0), jnp.where(half, 1.0, inside_ref[3]))

    start = GUARD + HALO * layer
    for f in range(2):
        source[f, start : start + width_x * layer, :] = s_ref[f]
        for c in range(chunks):
            to = f * FACE
            for d, count in zip(range(HALO, 0, -1), FACE_ROWS):
                skip = (TALL - count) // 2
                for ref, x, keep in (
                    (left_ref, HALO - d, inside_left),
                    (right_ref, HALO + width_x - 1 + d, inside_right),
                ):
                    at = GUARD + x * layer + c * TALL + skip
                    source[f, at : at + count, :] = ref[c, to : to + count, :] * keep
                to += count

    def step(ref, f, base, weight):
        own = [ref[f, pl.ds(base + c * TALL, 8), :] for c in range(chunks)]
        up = [pltpu.roll(t, LANES - 1, 1) for t in own]
        down = [pltpu.roll(t, 1, 1) for t in own]
        zero = jnp.zeros((8, LANES), F32)
        results = []
        for c in range(chunks):
            at = base + c * TALL
            total = jnp.where(lane == LANES - 1, up[c + 1] if c + 1 < chunks else zero, up[c])
            total = total + jnp.where(lane == 0, down[c - 1] if c else zero, down[c])
            total = total + (ref[f, pl.ds(at - 1, 8), :] + ref[f, pl.ds(at + 1, 8), :])
            total = total + (ref[f, pl.ds(at - layer, 8), :] + ref[f, pl.ds(at + layer, 8), :])
            results.append(total + weight * source[f, pl.ds(at, 8), :])
        return results

    refs = (source, one, two, one)
    for k in range(1, SWEEPS):
        weight = (25.0 / 4.0) ** k / 25.0
        reach = SWEEPS - k
        old, new = refs[k - 1], refs[k]

        def body(x, carry, old=old, new=new, weight=weight):
            keep = jnp.where(x < HALO, inside_left, jnp.where(x >= HALO + width_x, inside_right, 1.0))
            for tile in range(2):
                mask = rims[tile] * keep
                base = pl.multiple_of(GUARD + x * layer + tile * 8, 8)
                for f in range(2):
                    for c, value in enumerate(step(old, f, base, weight)):
                        new[f, pl.ds(base + c * TALL, 8), :] = value * mask
            return carry

        lax.fori_loop(HALO - reach, HALO + width_x + reach, body, 0)

    weight = (25.0 / 4.0) ** SWEEPS / 25.0
    scale = (4.0 / 25.0) ** SWEEPS

    def finish(x, sums):
        base = GUARD + (x + HALO) * layer + HALO
        a, b = [step(refs[SWEEPS - 1], f, base, weight) for f in range(2)]
        aa, ab, bb = sums
        for c in range(chunks):
            at = pl.ds(c * LANES, LANES)
            u, v = a[c] * scale, b[c] * scale
            raw_ref[0, x, :, at] = u
            raw_ref[1, x, :, at] = v
            aa, ab, bb = aa + u * u, ab + u * v, bb + v * v
        return aa, ab, bb

    zeros = jnp.zeros((8, LANES), F32)
    aa, ab, bb = lax.fori_loop(0, width_x, finish, (zeros, zeros, zeros))
    rows = [jnp.sum(t, axis=0, keepdims=True) for t in (volume_ref[...], aa, ab, bb)]
    tile = jnp.where(
        row == 0, rows[0], jnp.where(row == 1, rows[1], jnp.where(row == 2, rows[2], jnp.where(row == 3, rows[3], 0.0)))
    )
    for i in range(sums_ref.shape[0]):
        sums_ref[i] = tile
    for copy in copies:
        copy.wait()


def smooth(s, left, right, volume, inside, design, first_moment, second_moment, copies):
    width_x, width_y, width_z = design.shape
    block = jax.ShapeDtypeStruct(design.shape, F32)
    extended = pltpu.VMEM((2, (width_x + 2 * HALO) * (width_z // LANES) * TALL + 2 * GUARD, LANES), F32)
    return pl.pallas_call(
        smooth_kernel,
        out_shape=(
            jax.ShapeDtypeStruct((2,) + design.shape, F32),
            jax.ShapeDtypeStruct((copies, 8, LANES), F32),
            block,
            block,
            block,
        ),
        in_specs=[VMEM] * 4 + [SMEM] + [HBM] * 3,
        out_specs=(VMEM,) * 5,
        scratch_shapes=[extended] * 3 + [pltpu.SemaphoreType.DMA((3,))],
        compiler_params=params(14),
    )(s, left, right, volume, inside, design, first_moment, second_moment)


def adam_kernel(
    cells, sums_ref, lagrange_ref, raw_ref, design_ref, first_ref, second_ref,
    d_hbm, m_hbm, v_hbm, g_hbm, d_ref, m_ref, v_ref, g_ref, sems,
):
    width_x = design_ref.shape[0]
    sums = jnp.sum(sums_ref[...], axis=0)
    volume = jnp.sum(sums[0:1], axis=1, keepdims=True)
    shift = lagrange_ref[1] * (volume / cells / 0.4 - 1.25)
    total = jnp.sum(sums[1:2] + 2.0 * shift * sums[2:3] + shift * shift * sums[3:4], axis=1, keepdims=True)
    inverse = 1.0 / jnp.sqrt(jnp.maximum(total, 0.0) / cells + 1e-06)
    blocks = 4
    size = width_x // blocks
    copies = []
    for block in range(blocks):
        part = pl.ds(block * size, size)

        def body(i, carry, block=block):
            x = block * size + i
            gradient = (raw_ref[0, x] + shift * raw_ref[1, x]) * inverse
            new_first = 0.9 * first_ref[x] + 0.1 * gradient
            new_second = 0.999 * second_ref[x] + 0.001 * gradient * gradient
            first_hat = new_first * (0.05 / (1.0 - 0.9**ADAM_STEP))
            second_hat = new_second * (1.0 / (1.0 - 0.999**ADAM_STEP))
            d_ref[x] = jnp.clip(design_ref[x] - first_hat / (jnp.sqrt(second_hat) + 1e-08), 0.0, 1.0)
            m_ref[x] = new_first
            v_ref[x] = new_second
            g_ref[x] = gradient
            return carry

        lax.fori_loop(0, size, body, 0)
        for i, (ref, hbm) in enumerate(((d_ref, d_hbm), (m_ref, m_hbm), (v_ref, v_hbm), (g_ref, g_hbm))):
            copy = pltpu.make_async_copy(ref.at[part], hbm.at[part], sems.at[block, i])
            copy.start()
            copies.append(copy)
    for copy in copies:
        copy.wait()


def adam(cells, sums, lagrange, raw, design, first_moment, second_moment):
    return pl.pallas_call(
        functools.partial(adam_kernel, cells),
        out_shape=(jax.ShapeDtypeStruct(design.shape, F32),) * 4,
        in_specs=[VMEM, SMEM] + [VMEM] * 4,
        out_specs=(HBM,) * 4,
        scratch_shapes=[pltpu.VMEM(design.shape, F32)] * 4 + [pltpu.SemaphoreType.DMA((4, 4))],
        compiler_params=params(6),
    )(sums, lagrange, raw, design, first_moment, second_moment)


def shift(cells, axis, by):
    count = lax.axis_size(axis)
    return lax.ppermute(cells, axis, [(i, (i + by) % count) for i in range(count)])


def per_device(
    design,
    filtered,
    sensitivity,
    first_moment,
    second_moment,
    lagrange,
    trace_values,
    trace_anchor,
    trace_owner,
):
    width_x, width_y, depth = design.shape
    count_x, count_y = lax.axis_size("gx"), lax.axis_size("gy")
    cells = float(width_x * width_y * depth * count_x * count_y)
    index_x, index_y = lax.axis_index("gx"), lax.axis_index("gy")
    inside = jnp.stack([index_x > 0, index_x < count_x - 1, index_y > 0, index_y < count_y - 1]).astype(F32)

    rows = trace_values.shape[1]
    sent, low, high, filtered, sensitivity = make_send(
        trace_values[0], trace_anchor, trace_owner.reshape(1, rows), filtered, sensitivity, count_y
    )
    below, above = shift(high, "gy", 1), shift(low, "gy", -1)
    received = lax.all_to_all(sent, "gy", 0, 0, tiled=True)
    s, low, high, volume = make_source(received, filtered, sensitivity, above, below, lagrange, inside)
    left, right = shift(high, "gx", 1), shift(low, "gx", -1)
    raw, sums, design, first_moment, second_moment = smooth(
        s, left, right, volume, inside, design, first_moment, second_moment, count_x
    )
    sums = jnp.sum(lax.all_to_all(sums, "gx", 0, 0, tiled=True), axis=0)
    sums = lax.all_to_all(jnp.broadcast_to(sums[None], (count_y,) + sums.shape), "gy", 0, 0, tiled=True)
    return adam(cells, sums, lagrange, raw, design, first_moment, second_moment)


def solution(mesh):
    block = P("gx", "gy", None)
    return jax.shard_map(
        per_device,
        mesh=mesh,
        in_specs=(block, block, block, block, block, P(), block, P("gx", "gy"), block),
        out_specs=(block, block, block, block),
        check_vma=False,
    )
```

time: 388 us -> 87.1 us (0.22)
  blocking collectives: 275 us -> 25.7 us
  starting transfers between devices: 50.3 us -> 18.5 us
  other arithmetic: 19 us -> 0.09 us
  Pallas kernels: 0 us -> 17.8 us
  between operations: 17.7 us -> 0.74 us
    psum x2 -> x0, blocking collectives: 156 us -> none  [the longest x1 81.3 us: per_device(): volume = lax.psum(local_volume, ('gx', 'gy'))]
    unnamed x1 -> x0, blocking collectives: 120 us -> none
    ppermute x16 -> x4, starting transfers between devices: 50.2 us -> 9.06 us  [shift(): lax.ppermute(cells, axis, [(i, (i + by) % count) for i in range(count)])]
    all_to_all x0 -> x2, blocking collectives: none -> 25.7 us  [the longest x1 14 us: per_device(): lax.all_to_all(jnp.broadcast_to(sums[None], (count_y,) + sums.shape), 'gy...]
    pallas_call x0 -> x4, Pallas kernels: none -> 17.8 us  [the longest x1 11.1 us: smooth(): pl.pallas_call(smooth_kernel, out_shape=(jax.ShapeDtypeStruct((2,) + desi...]
    scatter-add x1 -> x0, other arithmetic: 13 us -> none  [deliver(): return zeros_rows.at[every_anchor[0]].add(every_values[0] * owned[:, None])]
    ppermute x16 -> x4, waiting for transfers between devices: 19.8 us -> 8.31 us  [shift(): lax.ppermute(cells, axis, [(i, (i + by) % count) for i in range(count)])]
    all_to_all x0 -> x1, waiting for transfers between devices: none -> 11.5 us  [per_device(): received = lax.all_to_all(sent, 'gy', 0, 0, tiled=True)]
  transfers between devices with their start and end apart: 17 -> 5, of which waited for: 10 -> 2; matrix products, arithmetic and copies ran while one was open for 1% -> 0% of each run, Pallas kernels for 0% -> 0%
where the time goes in v2:
time: 87.1 us; the launch traced here: 86.7 us
  blocking collectives  25.7 us (30%)
  waiting for transfers between devices  19.8 us (23%)
  starting transfers between devices  18.5 us (21%)
  Pallas kernels  17.8 us (20%)
  local copies, waits for them, and re-layouts  4.18 us (5%)
    all_to_all x1, blocking collectives, per_device(): lax.all_to_all(jnp.broadcast_to(sums[None], (count_y,) + sums.shape), 'gy...  14 us
    all_to_all x1, blocking collectives, per_device(): sums = jnp.sum(lax.all_to_all(sums, 'gx', 0, 0, tiled=True), axis=0)  11.6 us
    all_to_all x1, waiting for transfers between devices, per_device(): received = lax.all_to_all(sent, 'gy', 0, 0, tiled=True)  11.5 us
    pallas_call x1, Pallas kernels, smooth(): pl.pallas_call(smooth_kernel, out_shape=(jax.ShapeDtypeStruct((2,) + desi...  11.1 us
    all_to_all x1, starting transfers between devices, per_device(): received = lax.all_to_all(sent, 'gy', 0, 0, tiled=True)  9.4 us
    ppermute x4, starting transfers between devices, shift(): lax.ppermute(cells, axis, [(i, (i + by) % count) for i in range(count)])  9.06 us
    ppermute x4, waiting for transfers between devices, shift(): lax.ppermute(cells, axis, [(i, (i + by) % count) for i in range(count)])  8.31 us
    unnamed x18, local copies, waits for them, and re-layouts  4.17 us
  transfers between devices with their start and end apart: 5, of which 2 were waited for; matrix products, arithmetic and copies ran while one was open for 0% of the time, Pallas kernels for 0%

profile of v2, /device:TPU:1, one launch (start us, length us, event | category | flops | bytes accessed | tf_op | source)
XLA Modules:
  0.0 86.7 jit_solution(9229104330905676668)
XLA Ops:
  0.6 0.0 copy-start.6
  0.6 0.0 copy-start
  0.7 1.0 %copy-done = f32[16,8,1024]{2,1,0:T(8,128)S(1)} copy-done((f32[16,8,1024]{2,1,0:T(8,128)S(1)}, f32[16,8,1024]{2,1,0:T(8,128)}, u32[]{:S(2)}) %copy-start) | copy-done | bytes 524312
  1.7 0.0 copy-start.1
  1.7 1.0 %copy-done.1 = f32[16,8,1024]{2,1,0:T(8,128)S(1)} copy-done((f32[16,8,1024]{2,1,0:T(8,128)S(1)}, f32[16,8,1024]{2,1,0:T(8,128)}, u32[]{:S(2)}) %copy-start.1) | copy-done | bytes 524312
  2.7 0.0 copy-start.5
  2.7 0.8 copy-done.5
  3.5 0.0 copy-start.7
  3.5 0.7 copy-done.7
  4.1 0.0 copy-start.8
  4.2 0.7 copy-done.8
  4.8 2.1 %shard_map.120 = (f32[32,32,128]{2,1,0:T(8,128)}, f32[2,8,8,1024]{3,2,1,0:T(8,128)}, f32[2,8,8,1024]{3,2,1,0:T(8,128)}, f32[16,8,1024]{2,1,0:T(8,128)S(1)}, f32[16,8,1024]{2,1,0:T(8,128)S(1)}) custom-call(f32[64,128]{1,0:T(8,128)S(1)} %bitcast.6, s32[1,64]{1,0:T(1,128)S(1)} %copy-done.7, s32[1,64]{1,0:T(1,128)S(1)} %bitcast.7, f32[16,8,1024]{2,1,0:T(8,128)S(1)} %copy-done, ...), custom_call_target="tpu_custom_call" | custom-call | tf_op jit(solution)/shard_map/pallas_call | solution.py:113
  6.9 0.0 copy-start.2
  7.0 3.3 %collective-permute-start = (f32[2,8,8,1024]{3,2,1,0:T(8,128)}, f32[2,8,8,1024]{3,2,1,0:T(8,128)S(1)}, u32[]{:S(2)}, u32[]{:S(2)}) collective-permute-start(f32[2,8,8,1024]{3,2,1,0:T(8,128)} %get-tuple-element.21), channel_id=1, source_target_pairs={{0,31},{1,0},{2,1},{3,2},{4,3},{5,4},{6,5},{7,6},{8,7},{9,8},{10,9... | collective-permute-start | bytes 1572872 | tf_op jit(solution)/shard_map/ppermute | solution.py:391
  10.3 0.0 collective-permute-start.1
  10.3 9.4 %all-to-all-start = ((f32[32,32,128]{2,1,0:T(8,128)}), f32[32,32,128]{2,1,0:T(8,128)S(1)}, u32[]{:S(2)}, u32[]{:S(2)}) async-start(f32[32,32,128]{2,1,0:T(8,128)} %get-tuple-element.18), calls=%async_computation | async-start | bytes 1048576 | tf_op jit(solution)/shard_map/all_to_all | solution.py:416
  19.7 0.1 add_convert_fusion.inside_ref
  19.8 11.5 %all-to-all-done.recv_ref = f32[32,32,128]{2,1,0:T(8,128)S(1)} async-done(((f32[32,32,128]{2,1,0:T(8,128)}), f32[32,32,128]{2,1,0:T(8,128)S(1)}, u32[]{:S(2)}, u32[]{:S(2)}) %all-to-all-start) | async-done | bytes 524320 | tf_op jit(solution)/shard_map/all_to_all | solution.py:416
  31.2 0.0 copy-start.3
  31.2 0.0 copy-start.4
  31.2 0.0 collective-permute-done.above_ref
  31.2 0.0 collective-permute-done.1.below_ref
  31.3 0.0 copy-done.6
  31.3 2.3 %shard_map.121 = (f32[2,2048,128]{2,1,0:T(8,128)S(1)}, f32[8,88,128]{2,1,0:T(8,128)S(1)}, f32[8,88,128]{2,1,0:T(8,128)S(1)}, f32[8,128]{1,0:T(8,128)S(1)}) custom-call(f32[32,32,128]{2,1,0:T(8,128)S(1)} %all-to-all-done.recv_ref, f32[16,8,1024]{2,1,0:T(8,128)S(1)} %get-tuple-element.19.filtered_ref, f32[16,8,1024]{2,1,0:T(8,128)S(1)} %get-tuple-element.20.sensitivity_ref, ...), custom_call_target="tpu_custom_call" | custom-call | tf_op jit(solution)/shard_map/pallas_call | solution.py:215
  33.5 1.7 %collective-permute-start.2 = (f32[8,88,128]{2,1,0:T(8,128)S(1)}, f32[8,88,128]{2,1,0:T(8,128)S(1)}, u32[]{:S(2)}, u32[]{:S(2)}) collective-permute-start(f32[8,88,128]{2,1,0:T(8,128)S(1)} %get-tuple-element.24), channel_id=1, source_target_pairs={{0,32},{32,64},{64,96},{96,128},{128,160},{160,192},{192,224},{224... | collective-permute-start | bytes 1081352 | tf_op jit(solution)/shard_map/ppermute | solution.py:391
  35.2 4.0 %collective-permute-start.3 = (f32[8,88,128]{2,1,0:T(8,128)S(1)}, f32[8,88,128]{2,1,0:T(8,128)S(1)}, u32[]{:S(2)}, u32[]{:S(2)}) collective-permute-start(f32[8,88,128]{2,1,0:T(8,128)S(1)} %get-tuple-element.25), channel_id=1, source_target_pairs={{0,224},{32,0},{64,32},{96,64},{128,96},{160,128},{192,160},{224,1... | collective-permute-start | bytes 1081352 | tf_op jit(solution)/shard_map/ppermute | solution.py:391
  39.3 8.3 %collective-permute-done.2.left_ref = f32[8,88,128]{2,1,0:T(8,128)S(1)} collective-permute-done((f32[8,88,128]{2,1,0:T(8,128)S(1)}, f32[8,88,128]{2,1,0:T(8,128)S(1)}, u32[]{:S(2)}, u32[]{:S(2)}) %collective-permute-start.2) | collective-permute-done | bytes 360480 | tf_op jit(solution)/shard_map/ppermute | solution.py:391
  47.6 0.0 collective-permute-done.3.right_ref
  47.6 0.0 copy-done.2
  47.6 0.0 copy-done.3
  47.6 0.0 copy-done.4
  47.6 11.1 %shard_map.122 = (f32[2,16,8,1024]{3,2,1,0:T(8,128)S(1)}, f32[8,8,128]{2,1,0:T(8,128)S(1)}, f32[16,8,1024]{2,1,0:T(8,128)S(1)}, f32[16,8,1024]{2,1,0:T(8,128)S(1)}, f32[16,8,1024]{2,1,0:T(8,128)S(1)}) custom-call(f32[2,2048,128]{2,1,0:T(8,128)S(1)} %get-tuple-element.23.s_ref, f32[8,88,128]{2,1,0:T(8,128)S(1)} %collective-permute-done.2.left_ref, ...), custom_call_target="tpu_custom_call" | custom-call | tf_op jit(solution)/shard_map/pallas_call | solution.py:324
  58.7 11.6 %all_to_all.15 = f32[8,8,128]{2,1,0:T(8,128)S(1)} all-to-all(f32[8,8,128]{2,1,0:T(8,128)S(1)} %get-tuple-element.27), channel_id=1, replica_groups=mesh['gx'=8,'gy'=32] {'gx'}, dimensions={0} | all-to-all | bytes 65536 | tf_op jit(solution)/shard_map/all_to_all | solution.py:422
  70.4 14.0 %all_to_all.16.sums_ref = f32[32,8,128]{2,1,0:T(8,128)S(1)} all-to-all(f32[32,8,128]{2,1,0:T(8,128)S(1)} %broadcast_in_dim.2), channel_id=1, replica_groups=mesh['gx'=8,'gy'=32] {'gy'}, dimensions={0} | all-to-all | bytes 262144 | tf_op jit(solution)/shard_map/all_to_all | solution.py:423
  84.4 2.3 %shard_map.123 = (f32[16,8,1024]{2,1,0:T(8,128)}, f32[16,8,1024]{2,1,0:T(8,128)}, f32[16,8,1024]{2,1,0:T(8,128)}, f32[16,8,1024]{2,1,0:T(8,128)}) custom-call(f32[32,8,128]{2,1,0:T(8,128)S(1)} %all_to_all.16.sums_ref, f32[2]{0:T(128)S(1)} %copy-done.6, f32[2,16,8,1024]{3,2,1,0:T(8,128)S(1)} %get-tuple-element.28.raw_ref, ...), custom_call_target="tpu_custom_call" | custom-call | tf_op jit(solution)/shard_map/pallas_call | solution.py:379
  (2 shorter events, 0.0 us)
Async XLA Ops:
  0.6 30.6 %copy-start.6 = (f32[2]{0:T(128)S(1)}, f32[2]{0:T(128)}, u32[]{:S(2)}) copy-start(f32[2]{0:T(128)} %lagrange_ref.3) | copy-start | bytes 28
  0.6 1.0 %copy-start = (f32[16,8,1024]{2,1,0:T(8,128)S(1)}, f32[16,8,1024]{2,1,0:T(8,128)}, u32[]{:S(2)}) copy-start(f32[16,8,1024]{2,1,0:T(8,128)} %filtered_hbm.1) | copy-start | bytes 1572868
  1.7 1.0 %copy-start.1 = (f32[16,8,1024]{2,1,0:T(8,128)S(1)}, f32[16,8,1024]{2,1,0:T(8,128)}, u32[]{:S(2)}) copy-start(f32[16,8,1024]{2,1,0:T(8,128)} %sensitivity_hbm.1) | copy-start | bytes 1572868
  2.7 0.8 copy-start.5
  3.5 0.7 copy-start.7
  4.1 0.7 copy-start.8
  6.9 40.7 %copy-start.2 = (f32[16,8,1024]{2,1,0:T(8,128)S(1)}, f32[16,8,1024]{2,1,0:T(8,128)}, u32[]{:S(2)}) copy-start(f32[16,8,1024]{2,1,0:T(8,128)} %design_hbm.1) | copy-start | bytes 1572868
  7.0 24.3 %collective-permute-start = (f32[2,8,8,1024]{3,2,1,0:T(8,128)}, f32[2,8,8,1024]{3,2,1,0:T(8,128)S(1)}, u32[]{:S(2)}, u32[]{:S(2)}) collective-permute-start(f32[2,8,8,1024]{3,2,1,0:T(8,128)} %get-tuple-element.21), channel_id=1, source_target_pairs={{0,31},{1,0},{2,1},{3,2},{4,3},{5,4},{6,5},{7,6},{8,7},{9,8},{10,9... | collective-permute-start | bytes 1572872 | tf_op jit(solution)/shard_map/ppermute | solution.py:391
  10.3 21.0 %collective-permute-start.1 = (f32[2,8,8,1024]{3,2,1,0:T(8,128)}, f32[2,8,8,1024]{3,2,1,0:T(8,128)S(1)}, u32[]{:S(2)}, u32[]{:S(2)}) collective-permute-start(f32[2,8,8,1024]{3,2,1,0:T(8,128)} %get-tuple-element.22), channel_id=1, source_target_pairs={{0,1},{1,2},{2,3},{3,4},{4,5},{5,6},{6,7},{7,8},{8,9},{9,10},{10,1... | collective-permute-start | bytes 1572872 | tf_op jit(solution)/shard_map/ppermute | solution.py:391
  10.3 21.0 %all-to-all-start = ((f32[32,32,128]{2,1,0:T(8,128)}), f32[32,32,128]{2,1,0:T(8,128)S(1)}, u32[]{:S(2)}, u32[]{:S(2)}) async-start(f32[32,32,128]{2,1,0:T(8,128)} %get-tuple-element.18), calls=%async_computation | async-start | bytes 1048576 | tf_op jit(solution)/shard_map/all_to_all | solution.py:416
  31.2 16.4 %copy-start.3 = (f32[16,8,1024]{2,1,0:T(8,128)S(1)}, f32[16,8,1024]{2,1,0:T(8,128)}, u32[]{:S(2)}) copy-start(f32[16,8,1024]{2,1,0:T(8,128)} %first_hbm.1) | copy-start | bytes 1572868
  31.2 16.4 %copy-start.4 = (f32[16,8,1024]{2,1,0:T(8,128)S(1)}, f32[16,8,1024]{2,1,0:T(8,128)}, u32[]{:S(2)}) copy-start(f32[16,8,1024]{2,1,0:T(8,128)} %second_hbm.1) | copy-start | bytes 1572868
  33.5 14.0 %collective-permute-start.2 = (f32[8,88,128]{2,1,0:T(8,128)S(1)}, f32[8,88,128]{2,1,0:T(8,128)S(1)}, u32[]{:S(2)}, u32[]{:S(2)}) collective-permute-start(f32[8,88,128]{2,1,0:T(8,128)S(1)} %get-tuple-element.24), channel_id=1, source_target_pairs={{0,32},{32,64},{64,96},{96,128},{128,160},{160,192},{192,224},{224... | collective-permute-start | bytes 1081352 | tf_op jit(solution)/shard_map/ppermute | solution.py:391
  35.2 12.3 %collective-permute-start.3 = (f32[8,88,128]{2,1,0:T(8,128)S(1)}, f32[8,88,128]{2,1,0:T(8,128)S(1)}, u32[]{:S(2)}, u32[]{:S(2)}) collective-permute-start(f32[8,88,128]{2,1,0:T(8,128)S(1)} %get-tuple-element.25), channel_id=1, source_target_pairs={{0,224},{32,0},{64,32},{96,64},{128,96},{160,128},{192,160},{224,1... | collective-permute-start | bytes 1081352 | tf_op jit(solution)/shard_map/ppermute | solution.py:391

commit v3 on v2

v3 whole, which is shorter than its diff:
```python
import functools

import jax
import jax.numpy as jnp
from jax import lax
from jax.experimental import pallas as pl
from jax.experimental.pallas import tpu as pltpu
from jax.sharding import PartitionSpec as P

SWEEPS = 4
ADAM_STEP = 10
CAP = 8
LANES = 128
HALO = 4
TALL = 16
GUARD = 8
FACE_ROWS = (8, 10, 12, 14)
FACE = sum(FACE_ROWS)
F32 = jnp.float32
BF16 = jnp.bfloat16
HIGHEST = lax.Precision.HIGHEST
MIB = 1024 * 1024


def params(mib):
    return pltpu.CompilerParams(vmem_limit_bytes=mib * MIB)


VMEM = pl.BlockSpec(memory_space=pltpu.VMEM)
SMEM = pl.BlockSpec(memory_space=pltpu.SMEM)
HBM = pl.BlockSpec(memory_space=pltpu.HBM)


def iota(shape, dim):
    return lax.broadcasted_iota(jnp.int32, shape, dim)


def in_hbm(array):
    return pltpu.with_memory_space_constraint(array, pltpu.HBM)


def start_all(pairs, sems):
    copies = [pltpu.make_async_copy(src, dst, sems.at[i]) for i, (src, dst) in enumerate(pairs)]
    for copy in copies:
        copy.start()
    return copies


def bucket_kernel(chunks, values_hbm, anchor_hbm, owner_hbm, out_ref, values_ref, anchor_ref, owner_ref, sems):
    copies = start_all(((anchor_hbm, anchor_ref), (owner_hbm, owner_ref), (values_hbm, values_ref)), sems)
    rows = values_ref.shape[0]
    owners = out_ref.shape[0]
    copies[0].wait()
    copies[1].wait()
    owner = owner_ref[...]
    anchor = anchor_ref[...]
    place = (anchor // (8 * chunks)) * (8 * chunks) + (anchor % chunks) * 8 + (anchor // chunks) % 8
    down = iota((rows, rows), 0)
    across = iota((rows, rows), 1)
    owner_f = owner.astype(F32)
    owner_column = jnp.sum(
        jnp.where(down == across, jnp.broadcast_to(owner_f, (rows, rows)), 0.0), axis=1, keepdims=True
    )
    earlier = (owner_column == owner_f) & (down < across)
    rank = jnp.sum(jnp.where(earlier, 1.0, 0.0), axis=0, keepdims=True)
    slot = iota((owners * CAP, rows), 0)
    chosen = jnp.where((slot // CAP == owner) & ((slot % CAP).astype(F32) == rank), 1.0, 0.0)
    named = jnp.where(iota((owners, rows), 0) == owner, 1.0, 0.0)
    lane = iota((LANES, rows), 0)
    marked = jnp.where((lane % CAP).astype(F32) == rank, place.astype(F32) + 1.0, 0.0)
    anchors = lax.dot_general(
        named, marked, (((1,), (1,)), ((), ())), precision=HIGHEST, preferred_element_type=F32
    )
    lower = (anchors.astype(jnp.int32) - 1) % 8 < 4
    blank = jnp.zeros((1, LANES), F32)
    from_next = jnp.concatenate([jnp.where(lower, anchors, 0.0)[1:], blank], axis=0)
    from_last = jnp.concatenate([blank, jnp.where(lower, 0.0, anchors)[:-1]], axis=0)
    for i, line in enumerate((anchors, from_next, from_last)):
        out_ref[:, 3 * CAP + i, :] = line
    copies[2].wait()
    packed = jnp.dot(chosen, values_ref[...], precision=HIGHEST, preferred_element_type=F32)
    packed = packed.reshape(owners, CAP, LANES)
    nothing = jnp.zeros((1, CAP, LANES), F32)
    out_ref[:, 0:CAP, :] = packed
    out_ref[0 : owners - 1, CAP : 2 * CAP, :] = packed[1:]
    out_ref[owners - 1 :, CAP : 2 * CAP, :] = nothing
    out_ref[1:, 2 * CAP : 3 * CAP, :] = packed[:-1]
    out_ref[0:1, 2 * CAP : 3 * CAP, :] = nothing


def bucket(values, anchor, owner, owners, chunks):
    return pl.pallas_call(
        functools.partial(bucket_kernel, chunks),
        out_shape=jax.ShapeDtypeStruct((owners, 4 * CAP, LANES), F32),
        in_specs=[HBM] * 3,
        out_specs=VMEM,
        scratch_shapes=[
            pltpu.VMEM(values.shape, F32),
            pltpu.VMEM(anchor.shape, jnp.int32),
            pltpu.VMEM(owner.shape, jnp.int32),
            pltpu.SemaphoreType.DMA((3,)),
        ],
        compiler_params=params(4),
    )(in_hbm(values), in_hbm(anchor), in_hbm(owner))


def faces_kernel(filtered_hbm, sensitivity_hbm, low_ref, high_ref, filtered_ref, sensitivity_ref, sems):
    copies = start_all(((filtered_hbm, filtered_ref), (sensitivity_hbm, sensitivity_ref)), sems)
    width_x, width_y, width_z = filtered_ref.shape
    half = iota((width_y, width_z), 0) < 4
    for f, ref in enumerate((filtered_ref, sensitivity_ref)):
        copies[f].wait()
        for i in range(width_x // 2):
            even, odd = ref[2 * i], pltpu.roll(ref[2 * i + 1], 4, 0)
            low_ref[f, i] = jnp.where(half, even, odd)
            high_ref[f, i] = jnp.where(half, odd, even)


def make_faces(filtered, sensitivity):
    width_x, width_y, width_z = filtered.shape
    block = jax.ShapeDtypeStruct(filtered.shape, F32)
    face = jax.ShapeDtypeStruct((2, width_x // 2, width_y, width_z), F32)
    return pl.pallas_call(
        faces_kernel,
        out_shape=(face, face, block, block),
        in_specs=[HBM] * 2,
        out_specs=(VMEM,) * 4,
        scratch_shapes=[pltpu.SemaphoreType.DMA((2,))],
        compiler_params=params(4),
    )(in_hbm(filtered), in_hbm(sensitivity))


def exact_parts(values):
    top = values.astype(BF16)
    rest = values - top.astype(F32)
    middle = rest.astype(BF16)
    last = (rest - middle.astype(F32)).astype(BF16)
    return jnp.concatenate([top, middle, last], axis=1)


def scatter(recv_ref, own, beside, layers, layer_rows):
    owners = recv_ref.shape[0]
    group = min(LANES // CAP, owners)
    peer = iota((owners, LANES), 0)
    lane = iota((owners, LANES), 1)

    def places(line):
        kept = jnp.where(lane // CAP == peer % group, recv_ref[:, line, :], 0.0)
        sums = [jnp.sum(kept[g : g + group], axis=0, keepdims=True) for g in range(0, owners, group)]
        return [t[:, : group * CAP] for t in sums]

    def slots(start):
        return recv_ref[:, start : start + CAP, :].reshape(owners * CAP, LANES)

    for ref, lines, starts in ((own, (24,), (0,)), (beside, (25, 26), (8, 16))):
        anchors = jnp.concatenate([p for line in lines for p in places(line)], axis=1)
        parts = jnp.concatenate([exact_parts(slots(start)) for start in starts], axis=0)
        for first in layers:
            start, step = first * layer_rows, HALO * layer_rows
            row = (iota((step, anchors.shape[1]), 0) + (start + 1)).astype(F32)
            hot = jnp.where(row == anchors, 1.0, 0.0).astype(BF16)
            added = jnp.dot(hot, parts, preferred_element_type=F32)
            ref[start : start + step, :] = (
                added[:, 0:LANES] + added[:, LANES : 2 * LANES] + added[:, 2 * LANES : 3 * LANES]
            )


def source_pair(
    i, total, s_ref, filtered_ref, sensitivity_ref, above_ref, below_ref, own, beside, lagrange_ref, inside_ref
):
    width_x, width_y, width_z = filtered_ref.shape
    chunks = width_z // LANES
    base = lagrange_ref[0] + 0.25 * lagrange_ref[1]
    edge = jnp.tanh(jnp.full((8, LANES), 4.0, F32))
    inverse = 1.0 / (edge + edge)
    eight = 8.0 * inverse
    half = iota((width_y, LANES), 0) < 4
    rim = jnp.where(half, inside_ref[3], inside_ref[2]) * eight
    for c in range(chunks):
        at = pl.ds(c * LANES, LANES)
        sides = [(above_ref[f, i, :, at], below_ref[f, i, :, at]) for f in range(2)]
        for odd in range(2):
            x = 2 * i + odd
            line = pl.ds(pl.multiple_of((x * chunks + c) * 8, 8), 8)
            part = jnp.tanh(8.0 * (filtered_ref[x, :, at] - 0.5))
            total = total + (edge + part) * inverse
            slope = (1.0 - part * part) * eight
            source = slope * ((sensitivity_ref[x, :, at] + own[line, :]) + base)
            density, sense = [
                pltpu.roll(jnp.where(half, high, low), 4, 0) if odd else jnp.where(half, low, high)
                for low, high in sides
            ]
            part = jnp.tanh(8.0 * (density - 0.5))
            slope_out = (1.0 - part * part) * rim
            source_out = slope_out * ((sense + beside[line, :]) + base)
            row = pl.multiple_of(GUARD + ((x + HALO) * chunks + c) * TALL, 8)
            for f, (inner, outer) in enumerate(((source, source_out), (slope, slope_out))):
                s_ref[f, pl.ds(row, 8), :] = pltpu.roll(jnp.where(half, inner, outer), 4, 0)
                s_ref[f, pl.ds(row + 8, 8), :] = pltpu.roll(jnp.where(half, outer, inner), 4, 0)
    return total


def face_rows(chunks):
    for f in range(2):
        to = f * FACE
        for d, count in zip(range(HALO, 0, -1), FACE_ROWS):
            skip = (TALL - count) // 2
            for c in range(chunks):
                for more in sorted({0, count - 8}):
                    yield f, c, d, to + more, skip + more
            to += count


def edge_kernel(
    recv_ref, filtered_ref, sensitivity_ref, above_ref, below_ref, lagrange_ref, inside_ref,
    s_ref, low_ref, high_ref, volume_ref, own, beside,
):
    width_x, width_y, width_z = filtered_ref.shape
    chunks = width_z // LANES
    scatter(recv_ref, own, beside, (0, width_x - HALO), width_y * chunks)

    def pair(j, total):
        i = jnp.where(j < HALO // 2, j, j + (width_x - 2 * HALO) // 2)
        return source_pair(
            i, total, s_ref, filtered_ref, sensitivity_ref, above_ref, below_ref, own, beside, lagrange_ref, inside_ref
        )

    volume_ref[...] = lax.fori_loop(0, HALO, pair, jnp.zeros((8, LANES), F32))
    for f, c, d, to, skip in face_rows(chunks):
        for ref, x in ((low_ref, d - 1), (high_ref, width_x - d)):
            row = GUARD + ((x + HALO) * chunks + c) * TALL + skip
            ref[c, to : to + 8, :] = s_ref[f, row : row + 8, :]


def extended(shape):
    width_x, width_y, width_z = shape
    return jax.ShapeDtypeStruct((2, (width_x + 2 * HALO) * (width_z // LANES) * TALL + 2 * GUARD, LANES), F32)


def make_edges(recv, filtered, sensitivity, above, below, lagrange, inside):
    width_x, width_y, width_z = filtered.shape
    chunks = width_z // LANES
    face = jax.ShapeDtypeStruct((chunks, 2 * FACE, LANES), F32)
    scratch = pltpu.VMEM((width_x * width_y * chunks, LANES), F32)
    return pl.pallas_call(
        edge_kernel,
        out_shape=(extended(filtered.shape), face, face, jax.ShapeDtypeStruct((8, LANES), F32)),
        in_specs=[VMEM] * 5 + [SMEM] * 2,
        out_specs=(VMEM,) * 4,
        scratch_shapes=[scratch] * 2,
        compiler_params=params(8),
    )(recv, filtered, sensitivity, above, below, lagrange, inside)


def sweep(ref, source, f, base, weight, chunks):
    layer = chunks * TALL
    lane = iota((8, LANES), 1)
    own = [ref[f, pl.ds(base + c * TALL, 8), :] for c in range(chunks)]
    up = [pltpu.roll(t, LANES - 1, 1) for t in own]
    down = [pltpu.roll(t, 1, 1) for t in own]
    zero = jnp.zeros((8, LANES), F32)
    results = []
    for c in range(chunks):
        at = base + c * TALL
        total = jnp.where(lane == LANES - 1, up[c + 1] if c + 1 < chunks else zero, up[c])
        total = total + jnp.where(lane == 0, down[c - 1] if c else zero, down[c])
        total = total + (ref[f, pl.ds(at - 1, 8), :] + ref[f, pl.ds(at + 1, 8), :])
        total = total + (ref[f, pl.ds(at - layer, 8), :] + ref[f, pl.ds(at + layer, 8), :])
        results.append(total + weight * source[f, pl.ds(at, 8), :])
    return results


def sweep_layer(old, new, source, x, weight, rims, keep, chunks):
    layer = chunks * TALL
    for tile in range(2):
        mask = rims[tile] if keep is None else rims[tile] * keep
        base = pl.multiple_of(GUARD + x * layer + tile * 8, 8)
        for f in range(2):
            for c, value in enumerate(sweep(old, source, f, base, weight, chunks)):
                new[f, pl.ds(base + c * TALL, 8), :] = value * mask


def last_layer(old, source, raw_ref, x, sums, chunks):
    scale = (4.0 / 25.0) ** SWEEPS
    base = GUARD + (x + HALO) * chunks * TALL + HALO
    a, b = [sweep(old, source, f, base, weight_of(SWEEPS), chunks) for f in range(2)]
    aa, ab, bb = sums
    for c in range(chunks):
        at = pl.ds(c * LANES, LANES)
        u, v = a[c] * scale, b[c] * scale
        raw_ref[0, x, :, at] = u
        raw_ref[1, x, :, at] = v
        aa, ab, bb = aa + u * u, ab + u * v, bb + v * v
    return aa, ab, bb


def weight_of(k):
    return (25.0 / 4.0) ** k / 25.0


def rims_of(inside_ref):
    half = iota((8, LANES), 0) < 4
    return (jnp.where(half, inside_ref[2], 1.0), jnp.where(half, 1.0, inside_ref[3]))


def inner_kernel(
    recv_ref, filtered_ref, sensitivity_ref, above_ref, below_ref, lagrange_ref, inside_ref, volume_ref,
    design_hbm, first_hbm, second_hbm, edges_ref,
    s_ref, one, two, three, raw_ref, sums_ref, design_ref, first_ref, second_ref, own, beside, sems,
):
    del edges_ref
    copies = start_all(((design_hbm, design_ref), (first_hbm, first_ref), (second_hbm, second_ref)), sems)
    width_x, width_y, width_z = filtered_ref.shape
    chunks = width_z // LANES
    scatter(recv_ref, own, beside, range(HALO, width_x - HALO, HALO), width_y * chunks)

    def pair(i, total):
        return source_pair(
            i, total, s_ref, filtered_ref, sensitivity_ref, above_ref, below_ref, own, beside, lagrange_ref, inside_ref
        )

    sums_ref[0] = lax.fori_loop(HALO // 2, (width_x - HALO) // 2, pair, volume_ref[...])
    rims = rims_of(inside_ref)
    refs = (s_ref, one, two, three)
    for k in range(1, SWEEPS):

        def body(x, carry, k=k):
            sweep_layer(refs[k - 1], refs[k], s_ref, x + HALO, weight_of(k), rims, None, chunks)
            return carry

        lax.fori_loop(k, width_x - k, body, 0, unroll=2)
    zeros = jnp.zeros((8, LANES), F32)
    sums = lax.fori_loop(
        HALO,
        width_x - HALO,
        lambda x, sums: last_layer(three, s_ref, raw_ref, x, sums, chunks),
        (zeros, zeros, zeros),
        unroll=4,
    )
    for i in range(3):
        sums_ref[1 + i] = sums[i]
    for copy in copies:
        copy.wait()


def make_inner(
    recv, filtered, sensitivity, above, below, lagrange, inside, volume, design, first_moment, second_moment, edges
):
    width_x, width_y, width_z = filtered.shape
    block = jax.ShapeDtypeStruct(filtered.shape, F32)
    wide = extended(filtered.shape)
    scratch = pltpu.VMEM((width_x * width_y * width_z // LANES, LANES), F32)
    return pl.pallas_call(
        inner_kernel,
        out_shape=(
            wide,
            wide,
            wide,
            wide,
            jax.ShapeDtypeStruct((2,) + filtered.shape, F32),
            jax.ShapeDtypeStruct((4, 8, LANES), F32),
            block,
            block,
            block,
        ),
        in_specs=[VMEM] * 5 + [SMEM] * 2 + [VMEM] + [HBM] * 3 + [VMEM],
        out_specs=(VMEM,) * 9,
        input_output_aliases={11: 0},
        scratch_shapes=[scratch] * 2 + [pltpu.SemaphoreType.DMA((3,))],
        compiler_params=params(8),
        cost_estimate=pl.CostEstimate(flops=40_000_000, bytes_accessed=16_000_000, transcendentals=300_000),
    )(
        recv, filtered, sensitivity, above, below, lagrange, inside, volume,
        in_hbm(design), in_hbm(first_moment), in_hbm(second_moment), edges,
    )


def outer_kernel(
    left_ref, right_ref, inside_ref, sums_ref, s_in, one_in, two_in, three_in, raw_in,
    s_ref, one, two, three, raw_ref, send_ref,
):
    del s_in, one_in, two_in, three_in, raw_in
    width_x, width_y, width_z = raw_ref.shape[1:]
    chunks = width_z // LANES
    layer = chunks * TALL
    left, right = inside_ref[0], inside_ref[1]
    for f, c, d, to, skip in face_rows(chunks):
        for ref, x, keep in ((left_ref, HALO - d, left), (right_ref, HALO + width_x - 1 + d, right)):
            row = GUARD + x * layer + c * TALL + skip
            s_ref[f, row : row + 8, :] = ref[c, to : to + 8, :] * keep
    rims = rims_of(inside_ref)
    refs = (s_ref, one, two, three)
    for k in range(1, SWEEPS):

        def body(j, carry, k=k):
            x = j + k
            sweep_layer(
                refs[k - 1], refs[k], s_ref, x, weight_of(k), rims, jnp.where(x < HALO, left, 1.0), chunks
            )
            x = 2 * HALO + width_x - 1 - x
            sweep_layer(
                refs[k - 1], refs[k], s_ref, x, weight_of(k), rims, jnp.where(x >= HALO + width_x, right, 1.0), chunks
            )
            return carry

        lax.fori_loop(0, HALO, body, 0, unroll=2)

    def finish(x, sums):
        sums = last_layer(three, s_ref, raw_ref, x, sums, chunks)
        return last_layer(three, s_ref, raw_ref, width_x - 1 - x, sums, chunks)

    sums = lax.fori_loop(0, HALO, finish, tuple(sums_ref[1 + i] for i in range(3)), unroll=2)
    lane = iota((1, LANES), 1)
    line = jnp.zeros((1, LANES), F32)
    for i, tile in enumerate((sums_ref[0],) + tuple(sums)):
        total = jnp.sum(tile, axis=0, keepdims=True)
        total = total + pltpu.roll(total, LANES // 2, 1)
        total = total + pltpu.roll(total, LANES // 4, 1)
        line = jnp.where(lane // (LANES // 4) == i, total, line)
    send_ref[...] = jnp.broadcast_to(line, send_ref.shape)


def make_outer(left, right, inside, sums, wide, raw, copies):
    return pl.pallas_call(
        outer_kernel,
        out_shape=tuple(jax.ShapeDtypeStruct(w.shape, F32) for w in wide)
        + (
            jax.ShapeDtypeStruct(raw.shape, F32),
            jax.ShapeDtypeStruct((copies, LANES), F32),
        ),
        in_specs=[VMEM] * 2 + [SMEM] + [VMEM] * 6,
        out_specs=(VMEM,) * 6,
        input_output_aliases={4: 0, 5: 1, 6: 2, 7: 3, 8: 4},
        compiler_params=params(4),
    )(left, right, inside, sums, *wide, raw)[4:]


def adam_kernel(
    cells, sums_ref, lagrange_ref, raw_ref, design_ref, first_ref, second_ref,
    d_hbm, m_hbm, v_hbm, g_hbm, d_ref, m_ref, v_ref, g_ref, sems,
):
    width_x = design_ref.shape[0]
    line = jnp.sum(sums_ref[...], axis=0, keepdims=True)
    part = iota(line.shape, 1) // (LANES // 4)

    def picked(scale):
        return jnp.sum(line * scale, axis=1, keepdims=True)

    volume = picked(jnp.where(part == 0, 1.0, 0.0))
    shift = lagrange_ref[1] * (volume / cells / 0.4 - 1.25)
    total = picked(
        jnp.where(part == 1, 1.0, jnp.where(part == 2, 2.0 * shift, jnp.where(part == 3, shift * shift, 0.0)))
    )
    inverse = 1.0 / jnp.sqrt(jnp.maximum(total, 0.0) / cells + 1e-06)
    blocks = 4
    size = width_x // blocks
    copies = []
    for block in range(blocks):
        part = pl.ds(block * size, size)

        def body(i, carry, block=block):
            x = block * size + i
            gradient = (raw_ref[0, x] + shift * raw_ref[1, x]) * inverse
            new_first = 0.9 * first_ref[x] + 0.1 * gradient
            new_second = 0.999 * second_ref[x] + 0.001 * gradient * gradient
            first_hat = new_first * (0.05 / (1.0 - 0.9**ADAM_STEP))
            second_hat = new_second * (1.0 / (1.0 - 0.999**ADAM_STEP))
            d_ref[x] = jnp.clip(design_ref[x] - first_hat / (jnp.sqrt(second_hat) + 1e-08), 0.0, 1.0)
            m_ref[x] = new_first
            v_ref[x] = new_second
            g_ref[x] = gradient
            return carry

        lax.fori_loop(0, size, body, 0)
        for i, (ref, hbm) in enumerate(((d_ref, d_hbm), (m_ref, m_hbm), (v_ref, v_hbm), (g_ref, g_hbm))):
            copy = pltpu.make_async_copy(ref.at[part], hbm.at[part], sems.at[block, i])
            copy.start()
            copies.append(copy)
    for copy in copies:
        copy.wait()


def adam(cells, sums, lagrange, raw, design, first_moment, second_moment):
    return pl.pallas_call(
        functools.partial(adam_kernel, cells),
        out_shape=(jax.ShapeDtypeStruct(design.shape, F32),) * 4,
        in_specs=[VMEM, SMEM] + [VMEM] * 4,
        out_specs=(HBM,) * 4,
        scratch_shapes=[pltpu.VMEM(design.shape, F32)] * 4 + [pltpu.SemaphoreType.DMA((4, 4))],
        compiler_params=params(6),
    )(sums, lagrange, raw, design, first_moment, second_moment)


def shift(cells, axis, by):
    count = lax.axis_size(axis)
    return lax.ppermute(cells, axis, [(i, (i + by) % count) for i in range(count)])


def per_device(
    design,
    filtered,
    sensitivity,
    first_moment,
    second_moment,
    lagrange,
    trace_values,
    trace_anchor,
    trace_owner,
):
    width_x, width_y, depth = design.shape
    count_x, count_y = lax.axis_size("gx"), lax.axis_size("gy")
    cells = float(width_x * width_y * depth * count_x * count_y)
    index_x, index_y = lax.axis_index("gx"), lax.axis_index("gy")
    inside = jnp.stack([index_x > 0, index_x < count_x - 1, index_y > 0, index_y < count_y - 1]).astype(F32)

    rows = trace_values.shape[1]
    sent = bucket(trace_values[0], trace_anchor, trace_owner.reshape(1, rows), count_y, depth // LANES)
    received = lax.all_to_all(sent, "gy", 0, 0, tiled=True)
    low, high, filtered, sensitivity = make_faces(filtered, sensitivity)
    below, above = shift(high, "gy", 1), shift(low, "gy", -1)
    s, low, high, volume = make_edges(received, filtered, sensitivity, above, below, lagrange, inside)
    left, right = shift(high, "gx", 1), shift(low, "gx", -1)
    s, one, two, three, raw, sums, design, first_moment, second_moment = make_inner(
        received, filtered, sensitivity, above, below, lagrange, inside, volume,
        design, first_moment, second_moment, s,
    )
    raw, sums = make_outer(left, right, inside, sums, (s, one, two, three), raw, count_x * count_y)
    sums = lax.all_to_all(sums, ("gx", "gy"), 0, 0, tiled=True)
    return adam(cells, sums, lagrange, raw, design, first_moment, second_moment)


def solution(mesh):
    block = P("gx", "gy", None)
    return jax.shard_map(
        per_device,
        mesh=mesh,
        in_specs=(block, block, block, block, block, P(), block, P("gx", "gy"), block),
        out_specs=(block, block, block, block),
        check_vma=False,
    )
```

time: 87.1 us -> 73.3 us (0.84)
  waiting for transfers between devices: 19.8 us -> 14 us
  blocking collectives: 25.7 us -> 21.8 us
  local copies, waits for them, and re-layouts: 4.18 us -> 0.66 us
    ppermute x4, waiting for transfers between devices: 8.31 us -> 2.56 us  [shift(): lax.ppermute(cells, axis, [(i, (i + by) % count) for i in range(count)])]
    all_to_all x2 -> x1, blocking collectives: 25.7 us -> 21.8 us  [per_device(): sums = lax.all_to_all(sums, ('gx', 'gy'), 0, 0, tiled=True)]
    unnamed x18 -> x4, local copies, waits for them, and re-layouts: 4.17 us -> 0.66 us
    pallas_call x3 -> x5, Pallas kernels: 15.5 us -> 14.9 us  [the longest x1 5.74 us: make_inner(): pl.pallas_call(inner_kernel, out_shape=(wide, wide, wide, wide, jax.Shape...]
  transfers between devices with their start and end apart: 5 -> 5, of which waited for: 2 -> 2; matrix products, arithmetic and copies ran while one was open for 0% -> 0% of each run, Pallas kernels for 0% -> 11%
where the time goes in v3:
time: 73.3 us; the launch traced here: 73 us
  blocking collectives  21.8 us (30%)
  starting transfers between devices  18.5 us (25%)
  Pallas kernels  17.3 us (24%)
  waiting for transfers between devices  14 us (19%)
    all_to_all x1, blocking collectives, per_device(): sums = lax.all_to_all(sums, ('gx', 'gy'), 0, 0, tiled=True)  21.8 us
    all_to_all x1, waiting for transfers between devices, per_device(): received = lax.all_to_all(sent, 'gy', 0, 0, tiled=True)  11.5 us
    all_to_all x1, starting transfers between devices, per_device(): received = lax.all_to_all(sent, 'gy', 0, 0, tiled=True)  9.42 us
    ppermute x4, starting transfers between devices, shift(): lax.ppermute(cells, axis, [(i, (i + by) % count) for i in range(count)])  9.06 us
    pallas_call x1, Pallas kernels, make_inner(): pl.pallas_call(inner_kernel, out_shape=(wide, wide, wide, wide, jax.Shape...  5.74 us
    pallas_call x1, Pallas kernels, make_outer(): pl.pallas_call(outer_kernel, out_shape=tuple((jax.ShapeDtypeStruct(w.shap...  3.28 us
    ppermute x4, waiting for transfers between devices, shift(): lax.ppermute(cells, axis, [(i, (i + by) % count) for i in range(count)])  2.56 us
    pallas_call x1, Pallas kernels, adam(): pl.pallas_call(functools.partial(adam_kernel, cells), out_shape=(jax.Shap...  2.35 us
  transfers between devices with their start and end apart: 5, of which 2 were waited for; matrix products, arithmetic and copies ran while one was open for 0% of the time, Pallas kernels for 11%

profile of v3, /device:TPU:1, one launch (start us, length us, event | category | flops | bytes accessed | tf_op | source)
XLA Modules:
  0.0 73.0 jit_solution(10917278342409145359)
XLA Ops:
  0.6 0.0 copy-start.1
  0.6 2.0 %shard_map.121 = (f32[2,8,8,1024]{3,2,1,0:T(8,128)}, f32[2,8,8,1024]{3,2,1,0:T(8,128)S(1)}, f32[16,8,1024]{2,1,0:T(8,128)S(1)}, f32[16,8,1024]{2,1,0:T(8,128)S(1)}) custom-call(f32[16,8,1024]{2,1,0:T(8,128)} %filtered_hbm.1, f32[16,8,1024]{2,1,0:T(8,128)} %sensitivity_hbm.1), custom_call_target="tpu_custom_call" | custom-call | tf_op jit(solution)/shard_map/pallas_call | solution.py:123
  2.7 3.3 %collective-permute-start = (f32[2,8,8,1024]{3,2,1,0:T(8,128)}, f32[2,8,8,1024]{3,2,1,0:T(8,128)S(1)}, u32[]{:S(2)}, u32[]{:S(2)}) collective-permute-start(f32[2,8,8,1024]{3,2,1,0:T(8,128)} %get-tuple-element.25), channel_id=1, source_target_pairs={{0,31},{1,0},{2,1},{3,2},{4,3},{5,4},{6,5},{7,6},{8,7},{9,8},{10,9... | collective-permute-start | bytes 1572872 | tf_op jit(solution)/shard_map/ppermute | solution.py:496
  6.0 0.0 collective-permute-start.1
  6.0 2.3 %shard_map.120 = f32[32,32,128]{2,1,0:T(8,128)} custom-call(f32[64,128]{1,0:T(8,128)} %bitcast.12, s32[1,64]{1,0:T(1,128)} %anchor_hbm.1, s32[1,64]{1,0:T(1,128)} %bitcast.13), custom_call_target="tpu_custom_call" | custom-call | tf_op jit(solution)/shard_map/pallas_call | solution.py:92
  8.3 9.4 %all-to-all-start = ((f32[32,32,128]{2,1,0:T(8,128)}), f32[32,32,128]{2,1,0:T(8,128)S(1)}, u32[]{:S(2)}, u32[]{:S(2)}) async-start(f32[32,32,128]{2,1,0:T(8,128)} %shard_map.120), calls=%async_computation | async-start | bytes 1048576 | tf_op jit(solution)/shard_map/all_to_all | solution.py:518
  17.8 0.1 add_convert_fusion.inside_ref
  17.8 11.5 %all-to-all-done.recv_ref = f32[32,32,128]{2,1,0:T(8,128)S(1)} async-done(((f32[32,32,128]{2,1,0:T(8,128)}), f32[32,32,128]{2,1,0:T(8,128)S(1)}, u32[]{:S(2)}, u32[]{:S(2)}) %all-to-all-start) | async-done | bytes 524320 | tf_op jit(solution)/shard_map/all_to_all | solution.py:518
  29.3 0.0 collective-permute-done.above_ref
  29.3 0.0 collective-permute-done.1.below_ref
  29.3 0.0 copy-start
  29.3 0.7 copy-done
  30.0 1.5 %shard_map.122 = (f32[2,3088,128]{2,1,0:T(8,128)S(1)}, f32[8,88,128]{2,1,0:T(8,128)S(1)}, f32[8,88,128]{2,1,0:T(8,128)S(1)}, f32[8,128]{1,0:T(8,128)S(1)}) custom-call(f32[32,32,128]{2,1,0:T(8,128)S(1)} %all-to-all-done.recv_ref, f32[16,8,1024]{2,1,0:T(8,128)S(1)} %get-tuple-element.23.filtered_ref, f32[16,8,1024]{2,1,0:T(8,128)S(1)} %get-tuple-element.24.sensitivity_ref, ...), custom_call_target="tpu_custom_call" | custom-call | tf_op jit(solution)/shard_map/pallas_call | solution.py:245
  31.5 1.7 %collective-permute-start.2 = (f32[8,88,128]{2,1,0:T(8,128)S(1)}, f32[8,88,128]{2,1,0:T(8,128)S(1)}, u32[]{:S(2)}, u32[]{:S(2)}) collective-permute-start(f32[8,88,128]{2,1,0:T(8,128)S(1)} %get-tuple-element.27), channel_id=1, source_target_pairs={{0,32},{32,64},{64,96},{96,128},{128,160},{160,192},{192,224},{224... | collective-permute-start | bytes 1081352 | tf_op jit(solution)/shard_map/ppermute | solution.py:496
  33.2 4.0 %collective-permute-start.3 = (f32[8,88,128]{2,1,0:T(8,128)S(1)}, f32[8,88,128]{2,1,0:T(8,128)S(1)}, u32[]{:S(2)}, u32[]{:S(2)}) collective-permute-start(f32[8,88,128]{2,1,0:T(8,128)S(1)} %get-tuple-element.28), channel_id=1, source_target_pairs={{0,224},{32,0},{64,32},{96,64},{128,96},{160,128},{192,160},{224,1... | collective-permute-start | bytes 1081352 | tf_op jit(solution)/shard_map/ppermute | solution.py:496
  37.3 0.0 copy-done.1
  37.3 5.7 %shard_map.123 = (f32[2,3088,128]{2,1,0:T(8,128)S(1)}, f32[2,3088,128]{2,1,0:T(8,128)S(1)}, f32[2,3088,128]{2,1,0:T(8,128)S(1)}, f32[2,3088,128]{2,1,0:T(8,128)S...) custom-call(f32[32,32,128]{2,1,0:T(8,128)S(1)} %all-to-all-done.recv, ...), custom_call_target="tpu_custom_call", output_to_operand_aliasing={{0}: (11, {})} | custom-call | flops 40000000 | bytes 16000000 | tf_op jit(solution)/shard_map/pallas_call | solution.py:353
  43.0 2.6 %collective-permute-done.2.left_ref = f32[8,88,128]{2,1,0:T(8,128)S(1)} collective-permute-done((f32[8,88,128]{2,1,0:T(8,128)S(1)}, f32[8,88,128]{2,1,0:T(8,128)S(1)}, u32[]{:S(2)}, u32[]{:S(2)}) %collective-permute-start.2) | collective-permute-done | bytes 360480 | tf_op jit(solution)/shard_map/ppermute | solution.py:496
  45.6 0.0 collective-permute-done.3.right_ref
  45.6 3.3 %shard_map.124 = (f32[2,3088,128]{2,1,0:T(8,128)S(1)}, f32[2,3088,128]{2,1,0:T(8,128)S(1)}, f32[2,3088,128]{2,1,0:T(8,128)S(1)}, f32[2,3088,128]{2,1,0:T(8,128)S...) custom-call(f32[8,88,128]{2,1,0:T(8,128)S(1)} %collective-permute-do, ...), custom_call_target="tpu_custom_call", output_to_operand_aliasing={{0}: (4, {}), {1}: (5, {}), {2}: (6, {}), {3}: (7, {}), {4}... | custom-call | tf_op jit(solution)/shard_map/pallas_call | solution.py:424
  48.9 21.8 %all_to_all.16 = f32[256,1,128]{2,1,0:T(1,128)S(1)} all-to-all(f32[256,1,128]{2,1,0:T(1,128)S(1)} %bitcast.11), channel_id=1, replica_groups=mesh['gx'=8,'gy'=32] {'gx','gy'}, dimensions={0} | all-to-all | bytes 262144 | tf_op jit(solution)/shard_map/all_to_all | solution.py:528
  70.7 2.3 %shard_map.125 = (f32[16,8,1024]{2,1,0:T(8,128)}, f32[16,8,1024]{2,1,0:T(8,128)}, f32[16,8,1024]{2,1,0:T(8,128)}, f32[16,8,1024]{2,1,0:T(8,128)}) custom-call(f32[256,128]{1,0:T(8,128)S(1)} %bitcast.10, f32[2]{0:T(128)S(1)} %copy-done.1, f32[2,16,8,1024]{3,2,1,0:T(8,128)S(1)} %get-tuple-element.38.raw_ref, f32[16,8,1024]{2,1,0:T(8,128)S(1)} %get-tuple-element.39.design_ref, ...), custom_call_target="tpu_custom_call" | custom-call | tf_op jit(solution)/shard_map/pallas_call | solution.py:484
Async XLA Ops:
  0.6 36.6 %copy-start.1 = (f32[2]{0:T(128)S(1)}, f32[2]{0:T(128)}, u32[]{:S(2)}) copy-start(f32[2]{0:T(128)} %lagrange_ref.5) | copy-start | bytes 28
  2.7 26.6 %collective-permute-start = (f32[2,8,8,1024]{3,2,1,0:T(8,128)}, f32[2,8,8,1024]{3,2,1,0:T(8,128)S(1)}, u32[]{:S(2)}, u32[]{:S(2)}) collective-permute-start(f32[2,8,8,1024]{3,2,1,0:T(8,128)} %get-tuple-element.25), channel_id=1, source_target_pairs={{0,31},{1,0},{2,1},{3,2},{4,3},{5,4},{6,5},{7,6},{8,7},{9,8},{10,9... | collective-permute-start | bytes 1572872 | tf_op jit(solution)/shard_map/ppermute | solution.py:496
  6.0 23.3 %collective-permute-start.1 = (f32[2,8,8,1024]{3,2,1,0:T(8,128)S(1)}, f32[2,8,8,1024]{3,2,1,0:T(8,128)S(1)}, u32[]{:S(2)}, u32[]{:S(2)}) collective-permute-start(f32[2,8,8,1024]{3,2,1,0:T(8,128)S(1)} %get-tuple-element.26), channel_id=1, source_target_pairs={{0,1},{1,2},{2,3},{3,4},{4,5},{5,6},{6,7},{7,8},{8,9},{9,10},{10,1... | collective-permute-start | bytes 1572872 | tf_op jit(solution)/shard_map/ppermute | solution.py:496
  8.3 21.0 %all-to-all-start = ((f32[32,32,128]{2,1,0:T(8,128)}), f32[32,32,128]{2,1,0:T(8,128)S(1)}, u32[]{:S(2)}, u32[]{:S(2)}) async-start(f32[32,32,128]{2,1,0:T(8,128)} %shard_map.120), calls=%async_computation | async-start | bytes 1048576 | tf_op jit(solution)/shard_map/all_to_all | solution.py:518
  29.3 0.7 copy-start
  31.5 14.0 %collective-permute-start.2 = (f32[8,88,128]{2,1,0:T(8,128)S(1)}, f32[8,88,128]{2,1,0:T(8,128)S(1)}, u32[]{:S(2)}, u32[]{:S(2)}) collective-permute-start(f32[8,88,128]{2,1,0:T(8,128)S(1)} %get-tuple-element.27), channel_id=1, source_target_pairs={{0,32},{32,64},{64,96},{96,128},{128,160},{160,192},{192,224},{224... | collective-permute-start | bytes 1081352 | tf_op jit(solution)/shard_map/ppermute | solution.py:496
  33.2 12.3 %collective-permute-start.3 = (f32[8,88,128]{2,1,0:T(8,128)S(1)}, f32[8,88,128]{2,1,0:T(8,128)S(1)}, u32[]{:S(2)}, u32[]{:S(2)}) collective-permute-start(f32[8,88,128]{2,1,0:T(8,128)S(1)} %get-tuple-element.28), channel_id=1, source_target_pairs={{0,224},{32,0},{64,32},{96,64},{128,96},{160,128},{192,160},{224,1... | collective-permute-start | bytes 1081352 | tf_op jit(solution)/shard_map/ppermute | solution.py:496

commit v4 on v3

v4 whole, which is shorter than its diff:
```python
import functools
import itertools

import jax
import jax.numpy as jnp
from jax import lax
from jax.experimental import pallas as pl
from jax.experimental.pallas import tpu as pltpu
from jax.sharding import PartitionSpec as P

SWEEPS = 4
ADAM_STEP = 10
CAP = 8
LANES = 128
HALO = 4
TALL = 16
GUARD = 8
FACE_ROWS = (8, 10, 12, 14)
FACE = sum(FACE_ROWS)
LEFT, RIGHT, RIM, RIM_HALO, BASE, PENALTY = 0, 1, 2, 4, 5, 6
F32 = jnp.float32
BF16 = jnp.bfloat16
HIGHEST = lax.Precision.HIGHEST
MIB = 1024 * 1024


def params(mib):
    return pltpu.CompilerParams(vmem_limit_bytes=mib * MIB)


VMEM = pl.BlockSpec(memory_space=pltpu.VMEM)
HBM = pl.BlockSpec(memory_space=pltpu.HBM)


def iota(shape, dim):
    return lax.broadcasted_iota(jnp.int32, shape, dim)


def in_hbm(array):
    return pltpu.with_memory_space_constraint(array, pltpu.HBM)


def start_all(pairs, sems):
    copies = [pltpu.make_async_copy(src, dst, sems.at[i]) for i, (src, dst) in enumerate(pairs)]
    for copy in copies:
        copy.start()
    return copies


def first_kernel(
    values_hbm, anchor_hbm, owner_hbm, lagrange_hbm, filtered_hbm, sensitivity_hbm,
    low_ref, high_ref, masks_ref, values_ref, anchor_ref, owner_ref, lagrange_ref, filtered_ref, sensitivity_ref, sems,
):
    copies = start_all(
        (
            (filtered_hbm, filtered_ref),
            (sensitivity_hbm, sensitivity_ref),
            (lagrange_hbm, lagrange_ref),
            (anchor_hbm, anchor_ref),
            (owner_hbm, owner_ref),
            (values_hbm, values_ref),
        ),
        sems,
    )
    width_x, width_y, width_z = filtered_ref.shape
    index_x, index_y = lax.axis_index("gx"), lax.axis_index("gy")
    one, zero = jnp.ones((8, LANES), F32), jnp.zeros((8, LANES), F32)
    upper = iota((8, LANES), 0) < 4
    before, after = jnp.where(index_y > 0, one, zero), jnp.where(index_y < lax.axis_size("gy") - 1, one, zero)
    masks_ref[LEFT] = jnp.where(index_x > 0, one, zero)
    masks_ref[RIGHT] = jnp.where(index_x < lax.axis_size("gx") - 1, one, zero)
    masks_ref[RIM] = jnp.where(upper, before, one)
    masks_ref[RIM + 1] = jnp.where(upper, one, after)
    masks_ref[RIM_HALO] = jnp.where(upper, after, before)
    half = iota((width_y, width_z), 0) < 4
    for f, ref in enumerate((filtered_ref, sensitivity_ref)):
        copies[f].wait()
        for i in range(width_x // 2):
            even, odd = ref[2 * i], pltpu.roll(ref[2 * i + 1], 4, 0)
            low_ref[f, i] = jnp.where(half, even, odd)
            high_ref[f, i] = jnp.where(half, odd, even)
    copies[2].wait()
    weight, penalty = lagrange_ref[0:1, 0:1], lagrange_ref[0:1, 1:2]
    masks_ref[BASE] = one * (weight + 0.25 * penalty)
    masks_ref[PENALTY] = one * penalty
    for copy in copies[3:]:
        copy.wait()


def make_first(values, anchor, owner, lagrange, filtered, sensitivity):
    width_x, width_y, width_z = filtered.shape
    face = jax.ShapeDtypeStruct((2, width_x // 2, width_y, width_z), F32)
    return pl.pallas_call(
        first_kernel,
        out_shape=(
            face,
            face,
            jax.ShapeDtypeStruct((7, 8, LANES), F32),
            jax.ShapeDtypeStruct(values.shape, F32),
            jax.ShapeDtypeStruct(anchor.shape, jnp.int32),
            jax.ShapeDtypeStruct(owner.shape, jnp.int32),
        ),
        in_specs=[HBM] * 6,
        out_specs=(VMEM,) * 6,
        scratch_shapes=[
            pltpu.VMEM(lagrange.shape, F32),
            pltpu.VMEM(filtered.shape, F32),
            pltpu.VMEM(filtered.shape, F32),
            pltpu.SemaphoreType.DMA((6,)),
        ],
        compiler_params=params(4),
    )(*[in_hbm(t) for t in (values, anchor, owner, lagrange, filtered, sensitivity)])


def bucket_kernel(chunks, values_ref, anchor_ref, owner_ref, out_ref):
    rows = values_ref.shape[0]
    owners = out_ref.shape[0]
    owner = owner_ref[...]
    anchor = anchor_ref[...]
    place = (anchor // (8 * chunks)) * (8 * chunks) + (anchor % chunks) * 8 + (anchor // chunks) % 8
    down = iota((rows, rows), 0)
    across = iota((rows, rows), 1)
    owner_f = owner.astype(F32)
    owner_column = jnp.sum(
        jnp.where(down == across, jnp.broadcast_to(owner_f, (rows, rows)), 0.0), axis=1, keepdims=True
    )
    earlier = (owner_column == owner_f) & (down < across)
    rank = jnp.sum(jnp.where(earlier, 1.0, 0.0), axis=0, keepdims=True)
    slot = iota((owners * CAP, rows), 0)
    chosen = jnp.where((slot // CAP == owner) & ((slot % CAP).astype(F32) == rank), 1.0, 0.0)
    named = jnp.where(iota((owners, rows), 0) == owner, 1.0, 0.0)
    lane = iota((LANES, rows), 0)
    marked = jnp.where((lane % CAP).astype(F32) == rank, place.astype(F32) + 1.0, 0.0)
    anchors = lax.dot_general(
        named, marked, (((1,), (1,)), ((), ())), precision=HIGHEST, preferred_element_type=F32
    )
    lower = (anchors.astype(jnp.int32) - 1) % 8 < 4
    blank = jnp.zeros((1, LANES), F32)
    from_next = jnp.concatenate([jnp.where(lower, anchors, 0.0)[1:], blank], axis=0)
    from_last = jnp.concatenate([blank, jnp.where(lower, 0.0, anchors)[:-1]], axis=0)
    for i, line in enumerate((anchors, from_next, from_last)):
        out_ref[:, 3 * CAP + i, :] = line
    packed = jnp.dot(chosen, values_ref[...], precision=HIGHEST, preferred_element_type=F32)
    packed = packed.reshape(owners, CAP, LANES)
    nothing = jnp.zeros((1, CAP, LANES), F32)
    out_ref[:, 0:CAP, :] = packed
    out_ref[0 : owners - 1, CAP : 2 * CAP, :] = packed[1:]
    out_ref[owners - 1 :, CAP : 2 * CAP, :] = nothing
    out_ref[1:, 2 * CAP : 3 * CAP, :] = packed[:-1]
    out_ref[0:1, 2 * CAP : 3 * CAP, :] = nothing


def bucket(values, anchor, owner, owners, chunks):
    return pl.pallas_call(
        functools.partial(bucket_kernel, chunks),
        out_shape=jax.ShapeDtypeStruct((owners, 4 * CAP, LANES), F32),
        in_specs=[VMEM] * 3,
        out_specs=VMEM,
        compiler_params=params(4),
    )(values, anchor, owner)


def exact_parts(values):
    top = values.astype(BF16)
    rest = values - top.astype(F32)
    middle = rest.astype(BF16)
    last = (rest - middle.astype(F32)).astype(BF16)
    return jnp.concatenate([top, middle, last], axis=1)


def scatter(recv_ref, own, beside, layers, layer_rows):
    owners = recv_ref.shape[0]
    group = min(LANES // CAP, owners)
    peer = iota((owners, LANES), 0)
    lane = iota((owners, LANES), 1)

    def places(line):
        kept = jnp.where(lane // CAP == peer % group, recv_ref[:, line, :], 0.0)
        sums = [jnp.sum(kept[g : g + group], axis=0, keepdims=True) for g in range(0, owners, group)]
        return [t[:, : group * CAP] for t in sums]

    def slots(start):
        return recv_ref[:, start : start + CAP, :].reshape(owners * CAP, LANES)

    for ref, lines, starts in ((own, (24,), (0,)), (beside, (25, 26), (8, 16))):
        anchors = jnp.concatenate([p for line in lines for p in places(line)], axis=1)
        parts = jnp.concatenate([exact_parts(slots(start)) for start in starts], axis=0)
        for first in layers:
            start, step = first * layer_rows, HALO * layer_rows
            row = (iota((step, anchors.shape[1]), 0) + (start + 1)).astype(F32)
            hot = jnp.where(row == anchors, 1.0, 0.0).astype(BF16)
            added = jnp.dot(hot, parts, preferred_element_type=F32)
            ref[start : start + step, :] = (
                added[:, 0:LANES] + added[:, LANES : 2 * LANES] + added[:, 2 * LANES : 3 * LANES]
            )


def tall_tiles(half, inner, outer):
    return pltpu.roll(jnp.where(half, inner, outer), 4, 0), pltpu.roll(jnp.where(half, outer, inner), 4, 0)


def halo_tile(half, odd, low, high):
    return pltpu.roll(jnp.where(half, high, low), 4, 0) if odd else jnp.where(half, low, high)


def tall_row(x, c, chunks):
    return GUARD + ((x + HALO) * chunks + c) * TALL


def face_rows(chunks):
    to = 0
    for d, count in zip(range(HALO, 0, -1), FACE_ROWS):
        skip = (TALL - count) // 2
        for c in range(chunks):
            for more in sorted({0, count - 8}):
                yield c, d, c // 2, (c % 2) * FACE + to + more, skip + more
        to += count


def fill_faces(s_ref, low_ref, high_ref, width_x, chunks):
    for c, d, page, line, skip in face_rows(chunks):
        for ref, x in ((low_ref, d - 1), (high_ref, width_x - d)):
            row = tall_row(x, c, chunks) + skip
            ref[page, line : line + 8, :] = s_ref[pl.ds(row, 8), :]


def read_faces(s_ref, left_ref, right_ref, masks_ref, width_x, chunks):
    for c, d, page, line, skip in face_rows(chunks):
        for ref, x, keep in ((left_ref, -d, masks_ref[LEFT]), (right_ref, width_x - 1 + d, masks_ref[RIGHT])):
            row = tall_row(x, c, chunks) + skip
            s_ref[pl.ds(row, 8), :] = ref[page, line : line + 8, :] * keep


def extended(shape):
    width_x, width_y, width_z = shape
    return jax.ShapeDtypeStruct(((width_x + 2 * HALO) * (width_z // LANES) * TALL + 2 * GUARD, LANES), F32)


def face_shape(shape):
    return jax.ShapeDtypeStruct((shape[2] // LANES // 2, 2 * FACE, LANES), F32)


def slope_kernel(
    filtered_hbm, above_ref, below_ref, masks_ref, s_ref, low_ref, high_ref, volume_ref, filtered_ref, sems
):
    (copy,) = start_all(((filtered_hbm, filtered_ref),), sems)
    width_x, width_y, width_z = filtered_ref.shape
    chunks = width_z // LANES
    edge = jnp.tanh(jnp.full((8, LANES), 4.0, F32))
    inverse = 1.0 / (edge + edge)
    eight = 8.0 * inverse
    half = iota((width_y, LANES), 0) < 4
    rim = masks_ref[RIM_HALO] * eight

    copy.wait()
    total = jnp.zeros((8, LANES), F32)
    for i, c in itertools.product(range(width_x // 2), range(chunks)):
        at = pl.ds(c * LANES, LANES)
        low, high = above_ref[0, i, :, at], below_ref[0, i, :, at]
        for odd in range(2):
            x = 2 * i + odd
            part = jnp.tanh(8.0 * (filtered_ref[x, :, at] - 0.5))
            total = total + (edge + part) * inverse
            side = jnp.tanh(8.0 * (halo_tile(half, odd, low, high) - 0.5))
            tiles = tall_tiles(half, (1.0 - part * part) * eight, (1.0 - side * side) * rim)
            row = tall_row(x, c, chunks)
            s_ref[pl.ds(row, 8), :] = tiles[0]
            s_ref[pl.ds(row + 8, 8), :] = tiles[1]
    volume_ref[...] = total
    fill_faces(s_ref, low_ref, high_ref, width_x, chunks)


def make_slope(filtered, above, below, masks):
    face = face_shape(filtered.shape)
    return pl.pallas_call(
        slope_kernel,
        out_shape=(extended(filtered.shape), face, face, jax.ShapeDtypeStruct((8, LANES), F32)),
        in_specs=[HBM] + [VMEM] * 3,
        out_specs=(VMEM,) * 4,
        scratch_shapes=[pltpu.VMEM(filtered.shape, F32), pltpu.SemaphoreType.DMA((1,))],
        compiler_params=params(4),
        cost_estimate=pl.CostEstimate(flops=4_000_000, bytes_accessed=4_000_000, transcendentals=300_000),
    )(in_hbm(filtered), above, below, masks)


def source_pair(i, s_ref, slope_ref, sensitivity_ref, above_ref, below_ref, own, beside, masks_ref):
    width_x, width_y, width_z = sensitivity_ref.shape
    chunks = width_z // LANES
    base = masks_ref[BASE]
    half = iota((width_y, LANES), 0) < 4
    for c in range(chunks):
        at = pl.ds(c * LANES, LANES)
        low, high = above_ref[1, i, :, at], below_ref[1, i, :, at]
        for odd in range(2):
            x = 2 * i + odd
            line = pl.ds((x * chunks + c) * 8, 8)
            inner = sensitivity_ref[x, :, at] + own[line, :]
            outer = halo_tile(half, odd, low, high) + beside[line, :]
            row = tall_row(x, c, chunks)
            for t, tile in enumerate(tall_tiles(half, inner, outer)):
                rows = pl.ds(row + 8 * t, 8)
                s_ref[rows, :] = slope_ref[rows, :] * (tile + base)


def edge_kernel(
    recv_ref, sensitivity_hbm, above_ref, below_ref, slope_ref, masks_ref,
    s_ref, low_ref, high_ref, own, beside, sensitivity_ref, sems,
):
    width_x, width_y, width_z = sensitivity_ref.shape
    parts = [pl.ds(x, HALO) for x in (0, width_x - HALO)]
    copies = start_all([(sensitivity_hbm.at[part], sensitivity_ref.at[part]) for part in parts], sems)
    chunks = width_z // LANES
    scatter(recv_ref, own, beside, (0, width_x - HALO), width_y * chunks)
    for copy in copies:
        copy.wait()
    for i in (*range(HALO // 2), *range((width_x - HALO) // 2, width_x // 2)):
        source_pair(i, s_ref, slope_ref, sensitivity_ref, above_ref, below_ref, own, beside, masks_ref)
    fill_faces(s_ref, low_ref, high_ref, width_x, chunks)


def make_edges(recv, sensitivity, above, below, slope, masks):
    width_x, width_y, width_z = sensitivity.shape
    face = face_shape(sensitivity.shape)
    scratch = pltpu.VMEM((width_x * width_y * width_z // LANES, LANES), F32)
    return pl.pallas_call(
        edge_kernel,
        out_shape=(extended(sensitivity.shape), face, face),
        in_specs=[VMEM, HBM] + [VMEM] * 4,
        out_specs=(VMEM,) * 3,
        scratch_shapes=[scratch] * 2 + [pltpu.VMEM(sensitivity.shape, F32), pltpu.SemaphoreType.DMA((2,))],
        compiler_params=params(8),
    )(recv, in_hbm(sensitivity), above, below, slope, masks)


def weight_of(k):
    return (25.0 / 4.0) ** k / 25.0


def sweep(ref, source, base, k, chunks):
    layer = chunks * TALL
    lane = iota((8, LANES), 1)
    own = [ref[pl.ds(base + c * TALL, 8), :] for c in range(chunks)]
    up = [pltpu.roll(t, LANES - 1, 1) for t in own]
    down = [pltpu.roll(t, 1, 1) for t in own]
    zero = jnp.zeros((8, LANES), F32)
    results = []
    for c in range(chunks):
        at = base + c * TALL
        total = jnp.where(lane == LANES - 1, up[c + 1] if c + 1 < chunks else zero, up[c])
        total = total + jnp.where(lane == 0, down[c - 1] if c else zero, down[c])
        total = total + (ref[pl.ds(at - 1, 8), :] + ref[pl.ds(at + 1, 8), :])
        total = total + (ref[pl.ds(at - layer, 8), :] + ref[pl.ds(at + layer, 8), :])
        results.append(total + weight_of(k) * source[pl.ds(at, 8), :])
    return results


def sweep_layer(old, new, source, x, k, rims, keep, chunks):
    for tile in range(2):
        mask = rims[tile] if keep is None else rims[tile] * keep
        base = tall_row(x, 0, chunks) + 8 * tile
        for c, value in enumerate(sweep(old, source, base, k, chunks)):
            new[pl.ds(base + c * TALL, 8), :] = value * mask


def last_layer(old, source, x, chunks):
    scale = (4.0 / 25.0) ** SWEEPS
    return [scale * t for t in sweep(old, source, tall_row(x, 0, chunks) + HALO, SWEEPS, chunks)]


def store_layer(ref, x, values):
    for c, value in enumerate(values):
        ref[x, :, pl.ds(c * LANES, LANES)] = value


def load_layer(ref, x, chunks):
    return [ref[x, :, pl.ds(c * LANES, LANES)] for c in range(chunks)]


def add_products(total, left, right):
    for a, b in zip(left, right):
        total = total + a * b
    return total


def zero_tile():
    return jnp.zeros((8, LANES), F32)


def inner_sweeps(refs, masks_ref, width_x, chunks):
    rims = (masks_ref[RIM], masks_ref[RIM + 1])
    for k in range(1, SWEEPS):
        for x in range(k, width_x - k):
            sweep_layer(refs[k - 1], refs[k], refs[0], x, k, rims, None, chunks)
    return [last_layer(refs[SWEEPS - 1], refs[0], x, chunks) for x in range(HALO, width_x - HALO)]


def outer_sweeps(refs, masks_ref, width_x, chunks):
    rims = (masks_ref[RIM], masks_ref[RIM + 1])
    for k in range(1, SWEEPS):
        for x in range(k - HALO, k):
            sweep_layer(refs[k - 1], refs[k], refs[0], x, k, rims, masks_ref[LEFT] if x < 0 else None, chunks)
            x = width_x - 1 - x
            keep = masks_ref[RIGHT] if x >= width_x else None
            sweep_layer(refs[k - 1], refs[k], refs[0], x, k, rims, keep, chunks)
    layers = (*range(HALO), *range(width_x - HALO, width_x))
    return [last_layer(refs[SWEEPS - 1], refs[0], x, chunks) for x in layers]


def half_block(shape):
    return jax.ShapeDtypeStruct((shape[0] - 2 * HALO,) + shape[1:], F32), jax.ShapeDtypeStruct(
        (2 * HALO,) + shape[1:], F32
    )


TILE = jax.ShapeDtypeStruct((8, LANES), F32)


def slope_inner_kernel(width_x, s_ref, masks_ref, one, two, three, raw_ref, square_ref):
    chunks = raw_ref.shape[2] // LANES
    total = zero_tile()
    for i, values in enumerate(inner_sweeps((s_ref, one, two, three), masks_ref, width_x, chunks)):
        store_layer(raw_ref, i, values)
        total = add_products(total, values, values)
    square_ref[...] = total


def make_slope_inner(s, masks, shape):
    wide = extended(shape)
    return pl.pallas_call(
        functools.partial(slope_inner_kernel, shape[0]),
        out_shape=(wide, wide, wide, half_block(shape)[0], TILE),
        in_specs=[VMEM] * 2,
        out_specs=(VMEM,) * 5,
        compiler_params=params(2),
        cost_estimate=pl.CostEstimate(flops=15_000_000, bytes_accessed=8_000_000, transcendentals=0),
    )(s, masks)


def slope_outer_kernel(
    width_x, left_ref, right_ref, masks_ref, inner_square_ref, s_in, one_in, two_in, three_in,
    one, two, three, raw_ref, square_ref, s_ref,
):
    del one_in, two_in, three_in
    chunks = raw_ref.shape[2] // LANES
    for x in (0, width_x - HALO):
        rows = pl.ds(tall_row(x, 0, chunks), HALO * chunks * TALL)
        s_ref[rows, :] = s_in[rows, :]
    read_faces(s_ref, left_ref, right_ref, masks_ref, width_x, chunks)
    total = inner_square_ref[...]
    for i, values in enumerate(outer_sweeps((s_ref, one, two, three), masks_ref, width_x, chunks)):
        store_layer(raw_ref, i, values)
        total = add_products(total, values, values)
    square_ref[...] = total


def make_slope_outer(left, right, masks, square, s, wide, shape):
    same = jax.ShapeDtypeStruct(s.shape, F32)
    return pl.pallas_call(
        functools.partial(slope_outer_kernel, shape[0]),
        out_shape=(same, same, same, half_block(shape)[1], TILE),
        in_specs=[VMEM] * 8,
        out_specs=(VMEM,) * 5,
        input_output_aliases={5: 0, 6: 1, 7: 2},
        scratch_shapes=[pltpu.VMEM(s.shape, F32)],
        compiler_params=params(4),
        cost_estimate=pl.CostEstimate(flops=10_000_000, bytes_accessed=6_000_000, transcendentals=0),
    )(left, right, masks, square, s, *wide)[3:]


def source_inner_kernel(
    recv_ref, sensitivity_hbm, above_ref, below_ref, slope_ref, masks_ref, slope_raw_ref,
    design_hbm, first_hbm, second_hbm, edges_ref,
    s_ref, one, two, three, raw_ref, sums_ref, design_ref, first_ref, second_ref, own, beside, sensitivity_ref, sems,
):
    del edges_ref
    width_x, width_y, width_z = sensitivity_ref.shape
    chunks = width_z // LANES
    part = pl.ds(HALO, width_x - 2 * HALO)
    copies = start_all(
        (
            (sensitivity_hbm.at[part], sensitivity_ref.at[part]),
            (design_hbm, design_ref),
            (first_hbm, first_ref),
            (second_hbm, second_ref),
        ),
        sems,
    )
    scatter(recv_ref, own, beside, range(HALO, width_x - HALO, HALO), width_y * chunks)
    copies[0].wait()
    for i in range(HALO // 2, (width_x - HALO) // 2):
        source_pair(i, s_ref, slope_ref, sensitivity_ref, above_ref, below_ref, own, beside, masks_ref)
    aa, ab = zero_tile(), zero_tile()
    for i, values in enumerate(inner_sweeps((s_ref, one, two, three), masks_ref, width_x, chunks)):
        store_layer(raw_ref, i, values)
        aa = add_products(aa, values, values)
        ab = add_products(ab, values, load_layer(slope_raw_ref, i, chunks))
    sums_ref[0] = aa
    sums_ref[1] = ab
    for copy in copies[1:]:
        copy.wait()


def make_source_inner(
    recv, sensitivity, above, below, slope, masks, slope_raw, design, first_moment, second_moment, edges
):
    block = jax.ShapeDtypeStruct(design.shape, F32)
    wide = extended(design.shape)
    scratch = pltpu.VMEM((design.size // LANES, LANES), F32)
    return pl.pallas_call(
        source_inner_kernel,
        out_shape=(wide,) * 4
        + (half_block(design.shape)[0], jax.ShapeDtypeStruct((2, 8, LANES), F32))
        + (block,) * 3,
        in_specs=[VMEM, HBM] + [VMEM] * 5 + [HBM] * 3 + [VMEM],
        out_specs=(VMEM,) * 9,
        input_output_aliases={10: 0},
        scratch_shapes=[scratch] * 2 + [pltpu.VMEM(design.shape, F32), pltpu.SemaphoreType.DMA((4,))],
        compiler_params=params(8),
        cost_estimate=pl.CostEstimate(flops=40_000_000, bytes_accessed=16_000_000, transcendentals=0),
    )(
        recv, in_hbm(sensitivity), above, below, slope, masks, slope_raw,
        in_hbm(design), in_hbm(first_moment), in_hbm(second_moment), edges,
    )


def source_outer_kernel(
    width_x, left_ref, right_ref, masks_ref, slope_raw_ref, volume_ref, sums_ref, square_ref,
    s_in, one_in, two_in, three_in,
    s_ref, one, two, three, raw_ref, send_ref,
):
    del s_in, one_in, two_in, three_in
    chunks = raw_ref.shape[2] // LANES
    read_faces(s_ref, left_ref, right_ref, masks_ref, width_x, chunks)
    aa, ab = sums_ref[0], sums_ref[1]
    for i, values in enumerate(outer_sweeps((s_ref, one, two, three), masks_ref, width_x, chunks)):
        store_layer(raw_ref, i, values)
        aa = add_products(aa, values, values)
        ab = add_products(ab, values, load_layer(slope_raw_ref, i, chunks))
    lane = iota((1, LANES), 1)
    line = jnp.zeros((1, LANES), F32)
    for i, tile in enumerate((volume_ref[...], aa, ab, square_ref[...])):
        total = jnp.sum(tile, axis=0, keepdims=True)
        total = total + pltpu.roll(total, LANES // 2, 1)
        total = total + pltpu.roll(total, LANES // 4, 1)
        line = jnp.where(lane // (LANES // 4) == i, total, line)
    send_ref[...] = jnp.broadcast_to(line, send_ref.shape)


def make_source_outer(left, right, masks, slope_raw, volume, sums, square, wide, copies, shape):
    same = jax.ShapeDtypeStruct(wide[0].shape, F32)
    return pl.pallas_call(
        functools.partial(source_outer_kernel, shape[0]),
        out_shape=(same,) * 4 + (half_block(shape)[1], jax.ShapeDtypeStruct((copies, LANES), F32)),
        in_specs=[VMEM] * 11,
        out_specs=(VMEM,) * 6,
        input_output_aliases={7: 0, 8: 1, 9: 2, 10: 3},
        compiler_params=params(4),
    )(left, right, masks, slope_raw, volume, sums, square, *wide)[4:]


def adam_kernel(
    cells, sums_ref, masks_ref, inner_ref, outer_ref, slope_inner_ref, slope_outer_ref, design_ref, first_ref, second_ref,
    d_hbm, m_hbm, v_hbm, g_hbm, d_ref, m_ref, v_ref, g_ref, sems,
):
    width_x = design_ref.shape[0]
    line = jnp.sum(sums_ref[...], axis=0, keepdims=True)
    part = iota(line.shape, 1) // (LANES // 4)

    def picked(scale):
        return jnp.sum(line * scale, axis=1, keepdims=True)

    volume = picked(jnp.where(part == 0, 1.0, 0.0))
    shift = masks_ref[PENALTY, 0:1, 0:1] * (volume / cells / 0.4 - 1.25)
    total = picked(
        jnp.where(part == 1, 1.0, jnp.where(part == 2, 2.0 * shift, jnp.where(part == 3, shift * shift, 0.0)))
    )
    inverse = 1.0 / jnp.sqrt(jnp.maximum(total, 0.0) / cells + 1e-06)
    blocks = width_x // HALO
    copies = []
    for block in range(blocks):
        part = pl.ds(block * HALO, HALO)
        if block in (0, blocks - 1):
            raw, slope_raw, start = outer_ref, slope_outer_ref, 0 if block == 0 else HALO
        else:
            raw, slope_raw, start = inner_ref, slope_inner_ref, (block - 1) * HALO
        for i in range(HALO):
            x = block * HALO + i
            gradient = (raw[start + i] + shift * slope_raw[start + i]) * inverse
            new_first = 0.9 * first_ref[x] + 0.1 * gradient
            new_second = 0.999 * second_ref[x] + 0.001 * gradient * gradient
            first_hat = new_first * (0.05 / (1.0 - 0.9**ADAM_STEP))
            second_hat = new_second * (1.0 / (1.0 - 0.999**ADAM_STEP))
            d_ref[x] = jnp.clip(design_ref[x] - first_hat / (jnp.sqrt(second_hat) + 1e-08), 0.0, 1.0)
            m_ref[x] = new_first
            v_ref[x] = new_second
            g_ref[x] = gradient
        for i, (ref, hbm) in enumerate(((d_ref, d_hbm), (m_ref, m_hbm), (v_ref, v_hbm), (g_ref, g_hbm))):
            copy = pltpu.make_async_copy(ref.at[part], hbm.at[part], sems.at[block, i])
            copy.start()
            copies.append(copy)
    for copy in copies:
        copy.wait()


def adam(cells, sums, masks, parts, design, first_moment, second_moment):
    return pl.pallas_call(
        functools.partial(adam_kernel, cells),
        out_shape=(jax.ShapeDtypeStruct(design.shape, F32),) * 4,
        in_specs=[VMEM] * 9,
        out_specs=(HBM,) * 4,
        scratch_shapes=[pltpu.VMEM(design.shape, F32)] * 4 + [pltpu.SemaphoreType.DMA((4, 4))],
        compiler_params=params(6),
    )(sums, masks, *parts, design, first_moment, second_moment)


def shift(cells, axis, by):
    count = lax.axis_size(axis)
    return lax.ppermute(cells, axis, [(i, (i + by) % count) for i in range(count)])


def per_device(
    design,
    filtered,
    sensitivity,
    first_moment,
    second_moment,
    lagrange,
    trace_values,
    trace_anchor,
    trace_owner,
):
    width_x, width_y, depth = design.shape
    count_x, count_y = lax.axis_size("gx"), lax.axis_size("gy")
    cells = float(width_x * width_y * depth * count_x * count_y)
    rows = trace_values.shape[1]
    low, high, masks, *trace = make_first(
        trace_values[0], trace_anchor, trace_owner.reshape(1, rows), lagrange.reshape(1, 2), filtered, sensitivity
    )
    below, above = shift(high, "gy", 1), shift(low, "gy", -1)
    received = lax.all_to_all(bucket(*trace, count_y, depth // LANES), "gy", 0, 0, tiled=True)

    slope, low, high, volume = make_slope(filtered, above, below, masks)
    left, right = shift(high, "gx", 1), shift(low, "gx", -1)
    shape = design.shape
    *wide, slope_inner, square = make_slope_inner(slope, masks, shape)
    slope_outer, square = make_slope_outer(left, right, masks, square, slope, wide, shape)

    source, low, high = make_edges(received, sensitivity, above, below, slope, masks)
    left, right = shift(high, "gx", 1), shift(low, "gx", -1)
    *wide, inner, sums, design, first_moment, second_moment = make_source_inner(
        received, sensitivity, above, below, slope, masks, slope_inner, design, first_moment, second_moment, source
    )
    outer, sums = make_source_outer(
        left, right, masks, slope_outer, volume, sums, square, wide, count_x * count_y, shape
    )
    sums = lax.all_to_all(sums, ("gx", "gy"), 0, 0, tiled=True)
    parts = (inner, outer, slope_inner, slope_outer)
    return adam(cells, sums, masks, parts, design, first_moment, second_moment)


def solution(mesh):
    block = P("gx", "gy", None)
    return jax.shard_map(
        per_device,
        mesh=mesh,
        in_specs=(block, block, block, block, block, P(), block, P("gx", "gy"), block),
        out_specs=(block, block, block, block),
        check_vma=False,
    )
```

time: 73.3 us -> 65.1 us (0.89)
  waiting for transfers between devices: 14 us -> 3.69 us
  starting transfers between devices: 18.5 us -> 24.4 us
  Pallas kernels: 17.3 us -> 14.7 us
    all_to_all x1, waiting for transfers between devices: 11.5 us -> 3.67 us  [per_device(): lax.all_to_all(bucket(*trace, count_y, depth // LANES), 'gy', 0, 0, tiled...]
    ppermute x4 -> x6, starting transfers between devices: 9.06 us -> 15 us  [shift(): lax.ppermute(cells, axis, [(i, (i + by) % count) for i in range(count)])]
    ppermute x4 -> x6, waiting for transfers between devices: 2.56 us -> 0.02 us  [shift(): lax.ppermute(cells, axis, [(i, (i + by) % count) for i in range(count)])]
    pallas_call x4 -> x7, Pallas kernels: 12.6 us -> 11.6 us  [the longest x1 2.85 us: make_source_inner(): pl.pallas_call(source_inner_kernel, out_shape=(wide,) * 4 + (half_block(d...]
    pallas_call x1, Pallas kernels: 2.3 us -> 1.27 us  [bucket(): pl.pallas_call(functools.partial(bucket_kernel, chunks), out_shape=jax.Sh...]
  transfers between devices with their start and end apart: 5 -> 7, of which waited for: 2 -> 1; matrix products, arithmetic and copies ran while one was open for 0% -> 0% of each run, Pallas kernels for 11% -> 16%
where the time goes in v4:
time: 65.1 us; the launch traced here: 64.8 us
  starting transfers between devices  24.4 us (37%)
  blocking collectives  21.1 us (32%)
  Pallas kernels  14.7 us (23%)
  waiting for transfers between devices  3.69 us (6%)
  between operations  0.9 us (1%)
    all_to_all x1, blocking collectives, per_device(): sums = lax.all_to_all(sums, ('gx', 'gy'), 0, 0, tiled=True)  21.1 us
    ppermute x6, starting transfers between devices, shift(): lax.ppermute(cells, axis, [(i, (i + by) % count) for i in range(count)])  15 us
    all_to_all x1, starting transfers between devices, per_device(): lax.all_to_all(bucket(*trace, count_y, depth // LANES), 'gy', 0, 0, tiled...  9.41 us
    all_to_all x1, waiting for transfers between devices, per_device(): lax.all_to_all(bucket(*trace, count_y, depth // LANES), 'gy', 0, 0, tiled...  3.67 us
    pallas_call x1, Pallas kernels, make_source_inner(): pl.pallas_call(source_inner_kernel, out_shape=(wide,) * 4 + (half_block(d...  2.85 us
    pallas_call x1, Pallas kernels, make_slope(): pl.pallas_call(slope_kernel, out_shape=(extended(filtered.shape), face, f...  2.11 us
    pallas_call x1, Pallas kernels, adam(): pl.pallas_call(functools.partial(adam_kernel, cells), out_shape=(jax.Shap...  1.85 us
    pallas_call x1, Pallas kernels, make_slope_inner(): pl.pallas_call(functools.partial(slope_inner_kernel, shape[0]), out_shape...  1.45 us
  transfers between devices with their start and end apart: 7, of which 1 were waited for; matrix products, arithmetic and copies ran while one was open for 0% of the time, Pallas kernels for 16%

profile of v4, /device:TPU:1, one launch (start us, length us, event | category | flops | bytes accessed | tf_op | source)
XLA Modules:
  0.0 64.8 jit_solution(13653861523308410915)
XLA Ops:
  0.6 1.4 %shard_map.120 = (f32[2,8,8,1024]{3,2,1,0:T(8,128)S(1)}, f32[2,8,8,1024]{3,2,1,0:T(8,128)S(1)}, f32[7,8,128]{2,1,0:T(8,128)S(1)}, f32[64,128]{1,0:T(8,128)S(1)},...) custom-call(f32[64,128]{1,0:T(8,128)} %bitcast.9, s32[1,64]{1,0:T(1,128)} %anchor_hbm.1, s32[1,64]{1,0:T(1,128)} %bitcast.10, ...), custom_call_target="tpu_custom_call" | custom-call | tf_op jit(solution)/shard_map/pallas_call | solution.py:93
  2.1 3.3 %collective-permute-start = (f32[2,8,8,1024]{3,2,1,0:T(8,128)S(1)}, f32[2,8,8,1024]{3,2,1,0:T(8,128)S(1)}, u32[]{:S(2)}, u32[]{:S(2)}) collective-permute-start(f32[2,8,8,1024]{3,2,1,0:T(8,128)S(1)} %get-tuple-element.38), channel_id=1, source_target_pairs={{0,31},{1,0},{2,1},{3,2},{4,3},{5,4},{6,5},{7,6},{8,7},{9,8},{10,9... | collective-permute-start | bytes 1572872 | tf_op jit(solution)/shard_map/ppermute | solution.py:618
  5.4 0.0 collective-permute-start.1
  5.4 1.3 %shard_map.121 = f32[32,32,128]{2,1,0:T(8,128)} custom-call(f32[64,128]{1,0:T(8,128)S(1)} %get-tuple-element.35.values_ref, s32[1,64]{1,0:T(1,128)S(1)} %get-tuple-element.36.anchor_ref, s32[1,64]{1,0:T(1,128)S(1)} %get-tuple-element.37.owner_ref), custom_call_target="tpu_custom_call" | custom-call | tf_op jit(solution)/shard_map/pallas_call | solution.py:154
  6.7 9.4 %all-to-all-start = ((f32[32,32,128]{2,1,0:T(8,128)}), f32[32,32,128]{2,1,0:T(8,128)S(1)}, u32[]{:S(2)}, u32[]{:S(2)}) async-start(f32[32,32,128]{2,1,0:T(8,128)} %shard_map.121), calls=%async_computation | async-start | bytes 1048576 | tf_op jit(solution)/shard_map/all_to_all | solution.py:640
  16.1 0.0 collective-permute-done.above_ref
  16.1 0.0 collective-permute-done.1.below_ref
  16.1 2.1 %shard_map.122 = (f32[3088,128]{1,0:T(8,128)S(1)}, f32[4,88,128]{2,1,0:T(8,128)}, f32[4,88,128]{2,1,0:T(8,128)}, f32[8,128]{1,0:T(8,128)S(1)}) custom-call(f32[16,8,1024]{2,1,0:T(8,128)} %filtered_hbm.3, f32[2,8,8,1024]{3,2,1,0:T(8,128)S(1)} %collective-permute-done.above_ref, f32[2,8,8,1024]{3,2,1,0:T(8,128)S(1)} %collective-permute-done.1.below_ref, ...), custom_call_target="tpu_custom_call" | custom-call | flops 4000000 | bytes 4000000 | tf_op jit(solution)/shard_map/pallas_call | solution.py:275
  18.2 1.7 %collective-permute-start.4 = (f32[4,88,128]{2,1,0:T(8,128)}, f32[4,88,128]{2,1,0:T(8,128)S(1)}, u32[]{:S(2)}, u32[]{:S(2)}) collective-permute-start(f32[4,88,128]{2,1,0:T(8,128)} %get-tuple-element.44), channel_id=1, source_target_pairs={{0,32},{32,64},{64,96},{96,128},{128,160},{160,192},{192,224},{224... | collective-permute-start | bytes 540680 | tf_op jit(solution)/shard_map/ppermute | solution.py:618
  19.9 4.0 %collective-permute-start.5 = (f32[4,88,128]{2,1,0:T(8,128)}, f32[4,88,128]{2,1,0:T(8,128)S(1)}, u32[]{:S(2)}, u32[]{:S(2)}) collective-permute-start(f32[4,88,128]{2,1,0:T(8,128)} %get-tuple-element.45), channel_id=1, source_target_pairs={{0,224},{32,0},{64,32},{96,64},{128,96},{160,128},{192,160},{224,1... | collective-permute-start | bytes 540680 | tf_op jit(solution)/shard_map/ppermute | solution.py:618
  24.0 3.7 %all-to-all-done.recv_ref = f32[32,32,128]{2,1,0:T(8,128)S(1)} async-done(((f32[32,32,128]{2,1,0:T(8,128)}), f32[32,32,128]{2,1,0:T(8,128)S(1)}, u32[]{:S(2)}, u32[]{:S(2)}) %all-to-all-start) | async-done | bytes 524320 | tf_op jit(solution)/shard_map/all_to_all | solution.py:640
  27.6 1.4 %shard_map.123 = (f32[3088,128]{1,0:T(8,128)S(1)}, f32[4,88,128]{2,1,0:T(8,128)S(1)}, f32[4,88,128]{2,1,0:T(8,128)S(1)}) custom-call(f32[32,32,128]{2,1,0:T(8,128)S(1)} %all-to-all-done.recv_ref, f32[16,8,1024]{2,1,0:T(8,128)} %sensitivity_hbm.5, f32[2,8,8,1024]{3,2,1,0:T(8,128)S(1)} %collective-permute-done.above_ref, ...), custom_call_target="tpu_custom_call" | custom-call | tf_op jit(solution)/shard_map/pallas_call | solution.py:325
  29.0 1.7 %collective-permute-start.2 = (f32[4,88,128]{2,1,0:T(8,128)S(1)}, f32[4,88,128]{2,1,0:T(8,128)S(1)}, u32[]{:S(2)}, u32[]{:S(2)}) collective-permute-start(f32[4,88,128]{2,1,0:T(8,128)S(1)} %get-tuple-element.42), channel_id=1, source_target_pairs={{0,32},{32,64},{64,96},{96,128},{128,160},{160,192},{192,224},{224... | collective-permute-start | bytes 540680 | tf_op jit(solution)/shard_map/ppermute | solution.py:618
  30.7 4.2 %collective-permute-start.3 = (f32[4,88,128]{2,1,0:T(8,128)S(1)}, f32[4,88,128]{2,1,0:T(8,128)S(1)}, u32[]{:S(2)}, u32[]{:S(2)}) collective-permute-start(f32[4,88,128]{2,1,0:T(8,128)S(1)} %get-tuple-element.43), channel_id=1, source_target_pairs={{0,224},{32,0},{64,32},{96,64},{128,96},{160,128},{192,160},{224,1... | collective-permute-start | bytes 540680 | tf_op jit(solution)/shard_map/ppermute | solution.py:618
  34.9 1.5 %shard_map.124 = (f32[3088,128]{1,0:T(8,128)S(1)}, f32[3088,128]{1,0:T(8,128)S(1)}, f32[3088,128]{1,0:T(8,128)S(1)}, f32[8,8,1024]{2,1,0:T(8,128)S(1)}, f32[8,128]{1,0:T(8,128)S(1)}) custom-call(f32[3088,128]{1,0:T(8,128)S(1)} %get-tuple-element.41.slope_ref.s_ref.s_in, f32[7,8,128]{2,1,0:T(8,128)S(1)} %get-tuple-element.40.masks_ref), custom_call_target="tpu_custom_call" | custom-call | flops 15000000 | bytes 8000000 | tf_op jit(solution)/shard_map/pallas_call | solution.py:429
  36.4 2.8 %shard_map.126 = (f32[3088,128]{1,0:T(8,128)S(1)}, f32[3088,128]{1,0:T(8,128)S(1)}, f32[3088,128]{1,0:T(8,128)S(1)}, f32[3088,128]{1,0:T(8,128)S(1)}, f32[8,8,10...) custom-call(f32[32,32,128]{2,1,0:T(8,128)S(1)} %all-to-all-done.recv, ...), custom_call_target="tpu_custom_call", output_to_operand_aliasing={{0}: (10, {})} | custom-call | flops 40000000 | bytes 16000000 | tf_op jit(solution)/shard_map/pallas_call | solution.py:509
  39.2 0.0 collective-permute-done.4.left_ref
  39.3 0.0 collective-permute-done.5.right_ref
  39.3 1.1 %shard_map.125 = (f32[3088,128]{1,0:T(8,128)S(1)}, f32[3088,128]{1,0:T(8,128)S(1)}, f32[3088,128]{1,0:T(8,128)S(1)}, f32[8,8,1024]{2,1,0:T(8,128)S(1)}, f32[8,128]{1,0:T(8,128)S(1)}) custom-call(f32[4,88,128]{2,1,0:T(8,128)S(1)} %collective-permute-done.4.left_ref, ...), custom_call_target="tpu_custom_call", output_to_operand_aliasing={{0}: (5, {}), {1}: (6, {}), {2}: (7, {})} | custom-call | flops 10000000 | bytes 6000000 | tf_op jit(solution)/shard_map/pallas_call | solution.py:458
  40.4 0.0 collective-permute-done.2.left_ref
  40.4 0.0 collective-permute-done.3.right_ref
  40.4 1.2 %shard_map.127 = (f32[3088,128]{1,0:T(8,128)S(1)}, f32[3088,128]{1,0:T(8,128)S(1)}, f32[3088,128]{1,0:T(8,128)S(1)}, f32[3088,128]{1,0:T(8,128)S(1)}, f32[8,8,1024]{2,1,0:T(8,128)S(1)}, /*index=5*/f32[256,128]{1,0:T(8,128)S(1)}) custom-call(f32[4,88,128]{2,1,0:T(8,128)S(1)} %collective-permute-do, ...), custom_call_target="tpu_custom_call", output_to_operand_aliasing={{0}: (7, {}), {1}: (8, {}), {2}: (9, {}), {3}: (10, {})} | custom-call | tf_op jit(solution)/shard_map/pallas_call | solution.py:551
  41.6 21.1 %all_to_all.16 = f32[256,1,128]{2,1,0:T(1,128)S(1)} all-to-all(f32[256,1,128]{2,1,0:T(1,128)S(1)} %bitcast.8), channel_id=1, replica_groups=mesh['gx'=8,'gy'=32] {'gx','gy'}, dimensions={0} | all-to-all | bytes 262144 | tf_op jit(solution)/shard_map/all_to_all | solution.py:656
  62.8 1.8 %shard_map.128 = (f32[16,8,1024]{2,1,0:T(8,128)}, f32[16,8,1024]{2,1,0:T(8,128)}, f32[16,8,1024]{2,1,0:T(8,128)}, f32[16,8,1024]{2,1,0:T(8,128)}) custom-call(f32[256,128]{1,0:T(8,128)S(1)} %bitcast.7, f32[7,8,128]{2,1,0:T(8,128)S(1)} %get-tuple-element.40.masks_ref, f32[8,8,1024]{2,1,0:T(8,128)S(1)} %get-tuple-element.61.inner_ref, ...), custom_call_target="tpu_custom_call" | custom-call | tf_op jit(solution)/shard_map/pallas_call | solution.py:606
Async XLA Ops:
  2.1 14.0 %collective-permute-start = (f32[2,8,8,1024]{3,2,1,0:T(8,128)S(1)}, f32[2,8,8,1024]{3,2,1,0:T(8,128)S(1)}, u32[]{:S(2)}, u32[]{:S(2)}) collective-permute-start(f32[2,8,8,1024]{3,2,1,0:T(8,128)S(1)} %get-tuple-element.38), channel_id=1, source_target_pairs={{0,31},{1,0},{2,1},{3,2},{4,3},{5,4},{6,5},{7,6},{8,7},{9,8},{10,9... | collective-permute-start | bytes 1572872 | tf_op jit(solution)/shard_map/ppermute | solution.py:618
  5.4 10.7 %collective-permute-start.1 = (f32[2,8,8,1024]{3,2,1,0:T(8,128)S(1)}, f32[2,8,8,1024]{3,2,1,0:T(8,128)S(1)}, u32[]{:S(2)}, u32[]{:S(2)}) collective-permute-start(f32[2,8,8,1024]{3,2,1,0:T(8,128)S(1)} %get-tuple-element.39), channel_id=1, source_target_pairs={{0,1},{1,2},{2,3},{3,4},{4,5},{5,6},{6,7},{7,8},{8,9},{9,10},{10,1... | collective-permute-start | bytes 1572872 | tf_op jit(solution)/shard_map/ppermute | solution.py:618
  6.7 21.0 %all-to-all-start = ((f32[32,32,128]{2,1,0:T(8,128)}), f32[32,32,128]{2,1,0:T(8,128)S(1)}, u32[]{:S(2)}, u32[]{:S(2)}) async-start(f32[32,32,128]{2,1,0:T(8,128)} %shard_map.121), calls=%async_computation | async-start | bytes 1048576 | tf_op jit(solution)/shard_map/all_to_all | solution.py:640
  18.2 21.0 %collective-permute-start.4 = (f32[4,88,128]{2,1,0:T(8,128)}, f32[4,88,128]{2,1,0:T(8,128)S(1)}, u32[]{:S(2)}, u32[]{:S(2)}) collective-permute-start(f32[4,88,128]{2,1,0:T(8,128)} %get-tuple-element.44), channel_id=1, source_target_pairs={{0,32},{32,64},{64,96},{96,128},{128,160},{160,192},{192,224},{224... | collective-permute-start | bytes 540680 | tf_op jit(solution)/shard_map/ppermute | solution.py:618
  19.9 19.3 %collective-permute-start.5 = (f32[4,88,128]{2,1,0:T(8,128)}, f32[4,88,128]{2,1,0:T(8,128)S(1)}, u32[]{:S(2)}, u32[]{:S(2)}) collective-permute-start(f32[4,88,128]{2,1,0:T(8,128)} %get-tuple-element.45), channel_id=1, source_target_pairs={{0,224},{32,0},{64,32},{96,64},{128,96},{160,128},{192,160},{224,1... | collective-permute-start | bytes 540680 | tf_op jit(solution)/shard_map/ppermute | solution.py:618
  29.0 11.4 %collective-permute-start.2 = (f32[4,88,128]{2,1,0:T(8,128)S(1)}, f32[4,88,128]{2,1,0:T(8,128)S(1)}, u32[]{:S(2)}, u32[]{:S(2)}) collective-permute-start(f32[4,88,128]{2,1,0:T(8,128)S(1)} %get-tuple-element.42), channel_id=1, source_target_pairs={{0,32},{32,64},{64,96},{96,128},{128,160},{160,192},{192,224},{224... | collective-permute-start | bytes 540680 | tf_op jit(solution)/shard_map/ppermute | solution.py:618
  30.7 9.7 %collective-permute-start.3 = (f32[4,88,128]{2,1,0:T(8,128)S(1)}, f32[4,88,128]{2,1,0:T(8,128)S(1)}, u32[]{:S(2)}, u32[]{:S(2)}) collective-permute-start(f32[4,88,128]{2,1,0:T(8,128)S(1)} %get-tuple-element.43), channel_id=1, source_target_pairs={{0,224},{32,0},{64,32},{96,64},{128,96},{160,128},{192,160},{224,1... | collective-permute-start | bytes 540680 | tf_op jit(solution)/shard_map/ppermute | solution.py:618

commit v5 on v4

v5 whole, which is shorter than its diff:
```python
import functools
import itertools

import jax
import jax.numpy as jnp
from jax import lax
from jax.experimental import pallas as pl
from jax.experimental.pallas import tpu as pltpu
from jax.sharding import PartitionSpec as P

SWEEPS = 4
ADAM_STEP = 10
CAP = 8
LANES = 128
HALO = 4
TALL = 16
GUARD = 8
FACE_ROWS = (8, 10, 12, 14)
FACE = sum(FACE_ROWS)
SENT = 3 * CAP + 1
GROUPS = LANES // CAP
LISTS = 5
LEFT, RIGHT, RIM, RIM_HALO, BASE, PENALTY = 0, 1, 2, 4, 5, 6
F32 = jnp.float32
BF16 = jnp.bfloat16
MIB = 1024 * 1024


def params(mib):
    return pltpu.CompilerParams(vmem_limit_bytes=mib * MIB)


VMEM = pl.BlockSpec(memory_space=pltpu.VMEM)
HBM = pl.BlockSpec(memory_space=pltpu.HBM)


def iota(shape, dim):
    return lax.broadcasted_iota(jnp.int32, shape, dim)


def in_hbm(array):
    return pltpu.with_memory_space_constraint(array, pltpu.HBM)


def start_all(pairs, sems):
    copies = [pltpu.make_async_copy(src, dst, sems.at[i]) for i, (src, dst) in enumerate(pairs)]
    for copy in copies:
        copy.start()
    return copies


def exact_parts(values):
    top = values.astype(BF16)
    rest = values - top.astype(F32)
    middle = rest.astype(BF16)
    last = (rest - middle.astype(F32)).astype(BF16)
    return jnp.concatenate([top, middle, last], axis=1)


def bucket_rows(values, anchor, owner, owners, chunks):
    rows = values.shape[0]
    place = (anchor // (8 * chunks)) * (8 * chunks) + (anchor % chunks) * 8 + (anchor // chunks) % 8
    down = iota((rows, rows), 0)
    across = iota((rows, rows), 1)
    owner_f = owner.astype(F32)
    owner_column = jnp.sum(
        jnp.where(down == across, jnp.broadcast_to(owner_f, (rows, rows)), 0.0), axis=1, keepdims=True
    )
    earlier = (owner_column == owner_f) & (down < across)
    rank = jnp.sum(jnp.where(earlier, 1.0, 0.0), axis=0, keepdims=True)
    slot = iota((owners * CAP, rows), 0)
    chosen = jnp.where((slot // CAP == owner) & ((slot % CAP).astype(F32) == rank), 1.0, 0.0).astype(BF16)
    added = jnp.dot(chosen, exact_parts(values), preferred_element_type=F32)
    packed = added[:, 0:LANES] + added[:, LANES : 2 * LANES] + added[:, 2 * LANES : 3 * LANES]
    named = jnp.where(iota((owners, rows), 0) == owner, 1.0, 0.0).astype(BF16)
    number = place + 1
    ranked = (iota((LANES, rows), 0) % CAP).astype(F32) == rank
    marked = jnp.concatenate(
        [jnp.where(ranked, t.astype(F32), 0.0).astype(BF16) for t in (number // 32, number % 32)], axis=0
    )
    found = lax.dot_general(named, marked, (((1,), (1,)), ((), ())), preferred_element_type=F32)
    return packed, 32.0 * found[:, 0:LANES] + found[:, LANES : 2 * LANES]


def first_kernel(
    values_hbm, anchor_hbm, owner_hbm, lagrange_hbm, filtered_hbm, sensitivity_hbm,
    low_ref, high_ref, masks_ref, packed_ref, anchors_ref,
    values_ref, anchor_ref, owner_ref, lagrange_ref, filtered_ref, sensitivity_ref, sems,
):
    copies = start_all(
        (
            (anchor_hbm, anchor_ref),
            (owner_hbm, owner_ref),
            (values_hbm, values_ref),
            (lagrange_hbm, lagrange_ref),
            (filtered_hbm, filtered_ref),
            (sensitivity_hbm, sensitivity_ref),
        ),
        sems,
    )
    width_x, width_y, width_z = filtered_ref.shape
    index_x, index_y = lax.axis_index("gx"), lax.axis_index("gy")
    one, zero = jnp.ones((8, LANES), F32), jnp.zeros((8, LANES), F32)
    upper = iota((8, LANES), 0) < 4
    before, after = jnp.where(index_y > 0, one, zero), jnp.where(index_y < lax.axis_size("gy") - 1, one, zero)
    masks_ref[LEFT] = jnp.where(index_x > 0, one, zero)
    masks_ref[RIGHT] = jnp.where(index_x < lax.axis_size("gx") - 1, one, zero)
    masks_ref[RIM] = jnp.where(upper, before, one)
    masks_ref[RIM + 1] = jnp.where(upper, one, after)
    masks_ref[RIM_HALO] = jnp.where(upper, after, before)
    for copy in copies[:4]:
        copy.wait()
    weight, penalty = lagrange_ref[0:1, 0:1], lagrange_ref[0:1, 1:2]
    masks_ref[BASE] = one * (weight + 0.25 * penalty)
    masks_ref[PENALTY] = one * penalty
    packed_ref[...], anchors_ref[...] = bucket_rows(
        values_ref[...], anchor_ref[...], owner_ref[...], anchors_ref.shape[0], width_z // LANES
    )
    half = iota((width_y, width_z), 0) < 4
    for f, ref in enumerate((filtered_ref, sensitivity_ref)):
        copies[4 + f].wait()
        for i in range(width_x // 2):
            even, odd = ref[2 * i], pltpu.roll(ref[2 * i + 1], 4, 0)
            low_ref[f, i] = jnp.where(half, even, odd)
            high_ref[f, i] = jnp.where(half, odd, even)


def make_first(values, anchor, owner, lagrange, filtered, sensitivity, owners):
    width_x, width_y, width_z = filtered.shape
    face = jax.ShapeDtypeStruct((2, width_x // 2, width_y, width_z), F32)
    return pl.pallas_call(
        first_kernel,
        out_shape=(
            face,
            face,
            jax.ShapeDtypeStruct((7, 8, LANES), F32),
            jax.ShapeDtypeStruct((owners * CAP, LANES), F32),
            jax.ShapeDtypeStruct((owners, LANES), F32),
        ),
        in_specs=[HBM] * 6,
        out_specs=(VMEM,) * 5,
        scratch_shapes=[
            pltpu.VMEM(values.shape, F32),
            pltpu.VMEM(anchor.shape, jnp.int32),
            pltpu.VMEM(owner.shape, jnp.int32),
            pltpu.VMEM(lagrange.shape, F32),
            pltpu.VMEM(filtered.shape, F32),
            pltpu.VMEM(filtered.shape, F32),
            pltpu.SemaphoreType.DMA((6,)),
        ],
        compiler_params=params(8),
    )(*[in_hbm(t) for t in (values, anchor, owner, lagrange, filtered, sensitivity)])


def send_kernel(packed_ref, anchors_ref, out_ref):
    owners = anchors_ref.shape[0]
    anchors = anchors_ref[...]
    lower = (anchors.astype(jnp.int32) - 1) % 8 < 4
    blank = jnp.zeros((1, LANES), F32)
    from_next = jnp.concatenate([jnp.where(lower, anchors, 0.0)[1:], blank], axis=0)
    from_last = jnp.concatenate([blank, jnp.where(lower, 0.0, anchors)[:-1]], axis=0)
    group = iota((owners, LANES), 1) // CAP
    me = lax.axis_index("gy")
    line = jnp.zeros((owners, LANES), F32)
    for i, part in enumerate((anchors, from_next, from_last)):
        line = jnp.where(group == (me + i * LISTS) % GROUPS, part, line)
    nothing = jnp.zeros((CAP, LANES), F32)
    for b in range(owners):
        for i, near in enumerate((b, b + 1, b - 1)):
            rows = packed_ref[near * CAP : (near + 1) * CAP, :] if 0 <= near < owners else nothing
            out_ref[b * SENT + i * CAP : b * SENT + (i + 1) * CAP, :] = rows
        out_ref[(b + 1) * SENT - 1 : (b + 1) * SENT, :] = line[b : b + 1]


def make_send(packed, anchors):
    return pl.pallas_call(
        send_kernel,
        out_shape=jax.ShapeDtypeStruct((anchors.shape[0] * SENT, LANES), F32),
        in_specs=[VMEM] * 2,
        out_specs=VMEM,
        compiler_params=params(8),
    )(packed, anchors)


def scatter(recv_ref, own, beside, layers, layer_rows):
    owners = recv_ref.shape[0] // SENT
    lines = recv_ref[pl.ds(SENT - 1, owners, stride=SENT), :]
    peer = iota((owners, LANES), 0)
    group = iota((owners, LANES), 1) // CAP

    def places(i):
        kept = jnp.where(group == (peer + i * LISTS) % GROUPS, lines, 0.0)
        sums = [jnp.sum(kept[g : g + GROUPS], axis=0, keepdims=True) for g in range(0, owners, GROUPS)]
        return [pltpu.roll(t, LANES - i * LISTS * CAP, 1) for t in sums] if i else sums

    def slots(i):
        return jnp.concatenate(
            [recv_ref[p * SENT + i * CAP : p * SENT + (i + 1) * CAP, :] for p in range(owners)], axis=0
        )

    for ref, lists in ((own, (0,)), (beside, (1, 2))):
        anchors = jnp.concatenate([t for i in lists for t in places(i)], axis=1)
        parts = jnp.concatenate([exact_parts(slots(i)) for i in lists], axis=0)
        for first in layers:
            start, step = first * layer_rows, HALO * layer_rows
            row = (iota((step, anchors.shape[1]), 0) + (start + 1)).astype(F32)
            hot = jnp.where(row == anchors, 1.0, 0.0).astype(BF16)
            added = jnp.dot(hot, parts, preferred_element_type=F32)
            ref[start : start + step, :] = (
                added[:, 0:LANES] + added[:, LANES : 2 * LANES] + added[:, 2 * LANES : 3 * LANES]
            )


def tall_tiles(half, inner, outer):
    return pltpu.roll(jnp.where(half, inner, outer), 4, 0), pltpu.roll(jnp.where(half, outer, inner), 4, 0)


def halo_tile(half, odd, low, high):
    return pltpu.roll(jnp.where(half, high, low), 4, 0) if odd else jnp.where(half, low, high)


def tall_row(x, c, chunks):
    return GUARD + ((x + HALO) * chunks + c) * TALL


def flat_row(x, c, chunks):
    return (x * chunks + c) * TALL


def face_rows(chunks):
    to = 0
    for d, count in zip(range(HALO, 0, -1), FACE_ROWS):
        skip = (TALL - count) // 2
        for c in range(chunks):
            for more in sorted({0, count - 8}):
                yield c, d, c // 2, (c % 2) * FACE + to + more, skip + more
        to += count


def fill_faces(s_ref, low_ref, high_ref, width_x, chunks, row_of):
    for c, d, page, line, skip in face_rows(chunks):
        for ref, x in ((low_ref, d - 1), (high_ref, width_x - d)):
            row = row_of(x, c, chunks) + skip
            ref[page, line : line + 8, :] = s_ref[pl.ds(row, 8), :]


def read_faces(s_ref, left_ref, right_ref, masks_ref, width_x, chunks):
    for c, d, page, line, skip in face_rows(chunks):
        for ref, x, keep in ((left_ref, -d, masks_ref[LEFT]), (right_ref, width_x - 1 + d, masks_ref[RIGHT])):
            row = tall_row(x, c, chunks) + skip
            s_ref[pl.ds(row, 8), :] = ref[page, line : line + 8, :] * keep


def extended(shape):
    width_x, width_y, width_z = shape
    return jax.ShapeDtypeStruct(((width_x + 2 * HALO) * (width_z // LANES) * TALL + 2 * GUARD, LANES), F32)


def flat(shape):
    return jax.ShapeDtypeStruct((shape[0] * (shape[2] // LANES) * TALL, LANES), F32)


def face_shape(shape):
    return jax.ShapeDtypeStruct((shape[2] // LANES // 2, 2 * FACE, LANES), F32)


def slope_kernel(
    filtered_hbm, sensitivity_hbm, above_ref, below_ref, masks_ref,
    s_ref, base_ref, low_ref, high_ref, volume_ref, filtered_ref, sensitivity_ref, sems,
):
    copies = start_all(((filtered_hbm, filtered_ref), (sensitivity_hbm, sensitivity_ref)), sems)
    width_x, width_y, width_z = filtered_ref.shape
    chunks = width_z // LANES
    edge = jnp.tanh(jnp.full((8, LANES), 4.0, F32))
    inverse = 1.0 / (edge + edge)
    eight = 8.0 * inverse
    half = iota((width_y, LANES), 0) < 4
    rim = masks_ref[RIM_HALO] * eight
    base = masks_ref[BASE]
    for copy in copies:
        copy.wait()

    def pair(i, total):
        for c, odd in itertools.product(range(chunks), range(2)):
            at, x = pl.ds(c * LANES, LANES), 2 * i + odd
            part = jnp.tanh(8.0 * (filtered_ref[x, :, at] - 0.5))
            total = total + (edge + part) * inverse
            side, sense = [halo_tile(half, odd, above_ref[f, i, :, at], below_ref[f, i, :, at]) for f in range(2)]
            side = jnp.tanh(8.0 * (side - 0.5))
            row = pl.multiple_of(flat_row(x, c, chunks), 8)
            for t, tile in enumerate(tall_tiles(half, (1.0 - part * part) * eight, (1.0 - side * side) * rim)):
                s_ref[pl.ds(row + 8 * t, 8), :] = tile
            for t, tile in enumerate(tall_tiles(half, sensitivity_ref[x, :, at], sense)):
                base_ref[pl.ds(row + 8 * t, 8), :] = tile + base
        return total

    volume_ref[...] = lax.fori_loop(0, width_x // 2, pair, jnp.zeros((8, LANES), F32))
    fill_faces(s_ref, low_ref, high_ref, width_x, chunks, flat_row)


def make_slope(filtered, sensitivity, above, below, masks):
    face = face_shape(filtered.shape)
    rows = flat(filtered.shape)
    block = pltpu.VMEM(filtered.shape, F32)
    return pl.pallas_call(
        slope_kernel,
        out_shape=(rows, rows, face, face, jax.ShapeDtypeStruct((8, LANES), F32)),
        in_specs=[HBM] * 2 + [VMEM] * 3,
        out_specs=(VMEM,) * 5,
        scratch_shapes=[block, block, pltpu.SemaphoreType.DMA((2,))],
        compiler_params=params(8),
        cost_estimate=pl.CostEstimate(flops=4_000_000, bytes_accessed=4_000_000, transcendentals=300_000),
    )(in_hbm(filtered), in_hbm(sensitivity), above, below, masks)


def make_layers(layers, s_ref, slope_ref, base_ref, own, beside, chunks):
    half = iota((8, LANES), 0) < 4
    for x, c in itertools.product(layers, range(chunks)):
        line = pl.ds((x * chunks + c) * 8, 8)
        for t, tile in enumerate(tall_tiles(half, own[line, :], beside[line, :])):
            rows = pl.ds(flat_row(x, c, chunks) + 8 * t, 8)
            s_ref[pl.ds(tall_row(x, c, chunks) + 8 * t, 8), :] = slope_ref[rows, :] * (base_ref[rows, :] + tile)


def edge_kernel(width_x, recv_ref, base_ref, slope_ref, s_ref, low_ref, high_ref, own, beside):
    layer_rows = own.shape[0] // width_x
    chunks = layer_rows // 8
    scatter(recv_ref, own, beside, (0, width_x - HALO), layer_rows)
    layers = (*range(HALO), *range(width_x - HALO, width_x))
    make_layers(layers, s_ref, slope_ref, base_ref, own, beside, chunks)
    fill_faces(s_ref, low_ref, high_ref, width_x, chunks, tall_row)


def make_edges(recv, base, slope, shape):
    width_x, width_y, width_z = shape
    face = face_shape(shape)
    scratch = pltpu.VMEM((width_x * width_y * width_z // LANES, LANES), F32)
    return pl.pallas_call(
        functools.partial(edge_kernel, width_x),
        out_shape=(extended(shape), face, face),
        in_specs=[VMEM] * 3,
        out_specs=(VMEM,) * 3,
        scratch_shapes=[scratch] * 2,
        compiler_params=params(8),
    )(recv, base, slope)


def weight_of(k):
    return (25.0 / 4.0) ** k / 25.0


def sweep(ref, source, base, k, chunks):
    layer = chunks * TALL
    lane = iota((8, LANES), 1)
    own = [ref[pl.ds(base + c * TALL, 8), :] for c in range(chunks)]
    up = [pltpu.roll(t, LANES - 1, 1) for t in own]
    down = [pltpu.roll(t, 1, 1) for t in own]
    zero = jnp.zeros((8, LANES), F32)
    results = []
    for c in range(chunks):
        at = base + c * TALL
        total = jnp.where(lane == LANES - 1, up[c + 1] if c + 1 < chunks else zero, up[c])
        total = total + jnp.where(lane == 0, down[c - 1] if c else zero, down[c])
        total = total + (ref[pl.ds(at - 1, 8), :] + ref[pl.ds(at + 1, 8), :])
        total = total + (ref[pl.ds(at - layer, 8), :] + ref[pl.ds(at + layer, 8), :])
        results.append(total + weight_of(k) * source[pl.ds(at, 8), :])
    return results


def sweep_layer(old, new, source, x, k, rims, keep, chunks):
    for tile in range(2):
        mask = rims[tile] if keep is None else rims[tile] * keep
        base = tall_row(x, 0, chunks) + 8 * tile
        for c, value in enumerate(sweep(old, source, base, k, chunks)):
            new[pl.ds(base + c * TALL, 8), :] = value * mask


def last_layer(old, source, x, chunks):
    scale = (4.0 / 25.0) ** SWEEPS
    return [scale * t for t in sweep(old, source, tall_row(x, 0, chunks) + HALO, SWEEPS, chunks)]


def store_layer(ref, x, values):
    for c, value in enumerate(values):
        ref[x, :, pl.ds(c * LANES, LANES)] = value


def load_layer(ref, x, chunks):
    return [ref[x, :, pl.ds(c * LANES, LANES)] for c in range(chunks)]


def add_products(total, left, right):
    for a, b in zip(left, right):
        total = total + a * b
    return total


def zero_tile():
    return jnp.zeros((8, LANES), F32)


def inner_sweeps(refs, masks_ref, width_x, chunks):
    rims = (masks_ref[RIM], masks_ref[RIM + 1])
    for k in range(1, SWEEPS):
        for x in range(k, width_x - k):
            sweep_layer(refs[k - 1], refs[k], refs[0], x, k, rims, None, chunks)
    return [last_layer(refs[SWEEPS - 1], refs[0], x, chunks) for x in range(HALO, width_x - HALO)]


def outer_sweeps(refs, masks_ref, width_x, chunks):
    rims = (masks_ref[RIM], masks_ref[RIM + 1])
    for k in range(1, SWEEPS):
        for x in range(k - HALO, k):
            sweep_layer(refs[k - 1], refs[k], refs[0], x, k, rims, masks_ref[LEFT] if x < 0 else None, chunks)
            x = width_x - 1 - x
            keep = masks_ref[RIGHT] if x >= width_x else None
            sweep_layer(refs[k - 1], refs[k], refs[0], x, k, rims, keep, chunks)
    layers = (*range(HALO), *range(width_x - HALO, width_x))
    return [last_layer(refs[SWEEPS - 1], refs[0], x, chunks) for x in layers]


def half_block(shape):
    return jax.ShapeDtypeStruct((shape[0] - 2 * HALO,) + shape[1:], F32), jax.ShapeDtypeStruct(
        (2 * HALO,) + shape[1:], F32
    )


TILE = jax.ShapeDtypeStruct((8, LANES), F32)


def slope_inner_kernel(width_x, slope_ref, masks_ref, s_ref, one, two, three, raw_ref, square_ref):
    chunks = raw_ref.shape[2] // LANES
    s_ref[pl.ds(tall_row(0, 0, chunks), slope_ref.shape[0]), :] = slope_ref[...]
    total = zero_tile()
    for i, values in enumerate(inner_sweeps((s_ref, one, two, three), masks_ref, width_x, chunks)):
        store_layer(raw_ref, i, values)
        total = add_products(total, values, values)
    square_ref[...] = total


def make_slope_inner(s, masks, shape):
    wide = extended(shape)
    return pl.pallas_call(
        functools.partial(slope_inner_kernel, shape[0]),
        out_shape=(wide, wide, wide, wide, half_block(shape)[0], TILE),
        in_specs=[VMEM] * 2,
        out_specs=(VMEM,) * 6,
        compiler_params=params(8),
        cost_estimate=pl.CostEstimate(flops=15_000_000, bytes_accessed=8_000_000, transcendentals=0),
    )(s, masks)


def slope_outer_kernel(
    width_x, left_ref, right_ref, masks_ref, inner_square_ref, s_in, one_in, two_in, three_in,
    s_ref, one, two, three, raw_ref, square_ref,
):
    del s_in, one_in, two_in, three_in
    chunks = raw_ref.shape[2] // LANES
    read_faces(s_ref, left_ref, right_ref, masks_ref, width_x, chunks)
    total = inner_square_ref[...]
    for i, values in enumerate(outer_sweeps((s_ref, one, two, three), masks_ref, width_x, chunks)):
        store_layer(raw_ref, i, values)
        total = add_products(total, values, values)
    square_ref[...] = total


def make_slope_outer(left, right, masks, square, wide, shape):
    same = extended(shape)
    return pl.pallas_call(
        functools.partial(slope_outer_kernel, shape[0]),
        out_shape=(same, same, same, same, half_block(shape)[1], TILE),
        in_specs=[VMEM] * 8,
        out_specs=(VMEM,) * 6,
        input_output_aliases={4: 0, 5: 1, 6: 2, 7: 3},
        compiler_params=params(8),
        cost_estimate=pl.CostEstimate(flops=10_000_000, bytes_accessed=6_000_000, transcendentals=0),
    )(left, right, masks, square, *wide)[4:]


def source_inner_kernel(
    recv_ref, base_ref, slope_ref, masks_ref, slope_raw_ref, design_hbm, first_hbm, second_hbm, edges_ref,
    s_ref, one, two, three, raw_ref, sums_ref, design_ref, first_ref, second_ref, own, beside, sems,
):
    del edges_ref
    copies = start_all(((design_hbm, design_ref), (first_hbm, first_ref), (second_hbm, second_ref)), sems)
    width_x, width_y, width_z = design_ref.shape
    chunks = width_z // LANES
    scatter(recv_ref, own, beside, range(HALO, width_x - HALO, HALO), width_y * chunks)
    make_layers(range(HALO, width_x - HALO), s_ref, slope_ref, base_ref, own, beside, chunks)
    aa, ab = zero_tile(), zero_tile()
    for i, values in enumerate(inner_sweeps((s_ref, one, two, three), masks_ref, width_x, chunks)):
        store_layer(raw_ref, i, values)
        aa = add_products(aa, values, values)
        ab = add_products(ab, values, load_layer(slope_raw_ref, i, chunks))
    sums_ref[0] = aa
    sums_ref[1] = ab
    for copy in copies:
        copy.wait()


def make_source_inner(
    recv, base, slope, masks, slope_raw, design, first_moment, second_moment, edges
):
    block = jax.ShapeDtypeStruct(design.shape, F32)
    wide = extended(design.shape)
    scratch = pltpu.VMEM((design.size // LANES, LANES), F32)
    return pl.pallas_call(
        source_inner_kernel,
        out_shape=(wide,) * 4
        + (half_block(design.shape)[0], jax.ShapeDtypeStruct((2, 8, LANES), F32))
        + (block,) * 3,
        in_specs=[VMEM] * 5 + [HBM] * 3 + [VMEM],
        out_specs=(VMEM,) * 9,
        input_output_aliases={8: 0},
        scratch_shapes=[scratch] * 2 + [pltpu.SemaphoreType.DMA((3,))],
        compiler_params=params(8),
        cost_estimate=pl.CostEstimate(flops=40_000_000, bytes_accessed=16_000_000, transcendentals=0),
    )(
        recv, base, slope, masks, slope_raw,
        in_hbm(design), in_hbm(first_moment), in_hbm(second_moment), edges,
    )


def source_outer_kernel(
    width_x, left_ref, right_ref, masks_ref, slope_raw_ref, volume_ref, sums_ref, square_ref,
    s_in, one_in, two_in, three_in,
    s_ref, one, two, three, raw_ref, send_ref,
):
    del s_in, one_in, two_in, three_in
    chunks = raw_ref.shape[2] // LANES
    read_faces(s_ref, left_ref, right_ref, masks_ref, width_x, chunks)
    aa, ab = sums_ref[0], sums_ref[1]
    for i, values in enumerate(outer_sweeps((s_ref, one, two, three), masks_ref, width_x, chunks)):
        store_layer(raw_ref, i, values)
        aa = add_products(aa, values, values)
        ab = add_products(ab, values, load_layer(slope_raw_ref, i, chunks))
    lane = iota((1, LANES), 1)
    line = jnp.zeros((1, LANES), F32)
    for i, tile in enumerate((volume_ref[...], aa, ab, square_ref[...])):
        total = jnp.sum(tile, axis=0, keepdims=True)
        total = total + pltpu.roll(total, LANES // 2, 1)
        total = total + pltpu.roll(total, LANES // 4, 1)
        line = jnp.where(lane // (LANES // 4) == i, total, line)
    send_ref[...] = jnp.broadcast_to(line, send_ref.shape)


def make_source_outer(left, right, masks, slope_raw, volume, sums, square, wide, copies, shape):
    same = jax.ShapeDtypeStruct(wide[0].shape, F32)
    return pl.pallas_call(
        functools.partial(source_outer_kernel, shape[0]),
        out_shape=(same,) * 4 + (half_block(shape)[1], jax.ShapeDtypeStruct((copies, LANES), F32)),
        in_specs=[VMEM] * 11,
        out_specs=(VMEM,) * 6,
        input_output_aliases={7: 0, 8: 1, 9: 2, 10: 3},
        compiler_params=params(8),
    )(left, right, masks, slope_raw, volume, sums, square, *wide)[4:]


def adam_kernel(
    cells, sums_ref, masks_ref, inner_ref, outer_ref, slope_inner_ref, slope_outer_ref, design_ref, first_ref, second_ref,
    d_hbm, m_hbm, v_hbm, g_hbm, d_ref, m_ref, v_ref, g_ref, sems,
):
    width_x = design_ref.shape[0]
    line = jnp.sum(sums_ref[...], axis=0, keepdims=True)
    part = iota(line.shape, 1) // (LANES // 4)

    def picked(scale):
        return jnp.sum(line * scale, axis=1, keepdims=True)

    volume = picked(jnp.where(part == 0, 1.0, 0.0))
    shift = masks_ref[PENALTY, 0:1, 0:1] * (volume / cells / 0.4 - 1.25)
    total = picked(
        jnp.where(part == 1, 1.0, jnp.where(part == 2, 2.0 * shift, jnp.where(part == 3, shift * shift, 0.0)))
    )
    inverse = 1.0 / jnp.sqrt(jnp.maximum(total, 0.0) / cells + 1e-06)
    blocks = width_x // HALO
    copies = []
    for block in range(blocks):
        part = pl.ds(block * HALO, HALO)
        if block in (0, blocks - 1):
            raw, slope_raw, start = outer_ref, slope_outer_ref, 0 if block == 0 else HALO
        else:
            raw, slope_raw, start = inner_ref, slope_inner_ref, (block - 1) * HALO
        for i in range(HALO):
            x = block * HALO + i
            gradient = (raw[start + i] + shift * slope_raw[start + i]) * inverse
            new_first = 0.9 * first_ref[x] + 0.1 * gradient
            new_second = 0.999 * second_ref[x] + 0.001 * gradient * gradient
            first_hat = new_first * (0.05 / (1.0 - 0.9**ADAM_STEP))
            second_hat = new_second * (1.0 / (1.0 - 0.999**ADAM_STEP))
            d_ref[x] = jnp.clip(design_ref[x] - first_hat / (jnp.sqrt(second_hat) + 1e-08), 0.0, 1.0)
            m_ref[x] = new_first
            v_ref[x] = new_second
            g_ref[x] = gradient
        for i, (ref, hbm) in enumerate(((d_ref, d_hbm), (m_ref, m_hbm), (v_ref, v_hbm), (g_ref, g_hbm))):
            copy = pltpu.make_async_copy(ref.at[part], hbm.at[part], sems.at[block, i])
            copy.start()
            copies.append(copy)
    for copy in copies:
        copy.wait()


def adam(cells, sums, masks, parts, design, first_moment, second_moment):
    return pl.pallas_call(
        functools.partial(adam_kernel, cells),
        out_shape=(jax.ShapeDtypeStruct(design.shape, F32),) * 4,
        in_specs=[VMEM] * 9,
        out_specs=(HBM,) * 4,
        scratch_shapes=[pltpu.VMEM(design.shape, F32)] * 4 + [pltpu.SemaphoreType.DMA((4, 4))],
        compiler_params=params(8),
    )(sums, masks, *parts, design, first_moment, second_moment)


def shift(cells, axis, by):
    count = lax.axis_size(axis)
    return lax.ppermute(cells, axis, [(i, (i + by) % count) for i in range(count)])


def per_device(
    design,
    filtered,
    sensitivity,
    first_moment,
    second_moment,
    lagrange,
    trace_values,
    trace_anchor,
    trace_owner,
):
    width_x, width_y, depth = design.shape
    count_x, count_y = lax.axis_size("gx"), lax.axis_size("gy")
    cells = float(width_x * width_y * depth * count_x * count_y)
    rows = trace_values.shape[1]
    low, high, masks, packed, anchors = make_first(
        trace_values[0], trace_anchor, trace_owner.reshape(1, rows), lagrange.reshape(1, 2), filtered, sensitivity, count_y
    )
    below, above = shift(high, "gy", 1), shift(low, "gy", -1)
    sent = make_send(packed, anchors)
    received = lax.all_to_all(sent.reshape(count_y, SENT * LANES), "gy", 0, 0, tiled=True).reshape(sent.shape)

    slope, base, low, high, volume = make_slope(filtered, sensitivity, above, below, masks)
    left, right = shift(high, "gx", 1), shift(low, "gx", -1)
    shape = design.shape
    *wide, slope_inner, square = make_slope_inner(slope, masks, shape)
    slope_outer, square = make_slope_outer(left, right, masks, square, wide, shape)

    source, low, high = make_edges(received, base, slope, shape)
    left, right = shift(high, "gx", 1), shift(low, "gx", -1)
    *wide, inner, sums, design, first_moment, second_moment = make_source_inner(
        received, base, slope, masks, slope_inner, design, first_moment, second_moment, source
    )
    outer, sums = make_source_outer(
        left, right, masks, slope_outer, volume, sums, square, wide, count_x * count_y, shape
    )
    sums = lax.all_to_all(sums, ("gx", "gy"), 0, 0, tiled=True)
    parts = (inner, outer, slope_inner, slope_outer)
    return adam(cells, sums, masks, parts, design, first_moment, second_moment)


def solution(mesh):
    block = P("gx", "gy", None)
    return jax.shard_map(
        per_device,
        mesh=mesh,
        in_specs=(block, block, block, block, block, P(), block, P("gx", "gy"), block),
        out_specs=(block, block, block, block),
        check_vma=False,
    )
```

time: 65.1 us -> 63.1 us (0.969)
  waiting for transfers between devices: 3.69 us -> 0.93 us
  local copies, waits for them, and re-layouts: 0 us -> 1.83 us
  Pallas kernels: 14.7 us -> 13.6 us
    all_to_all x1, waiting for transfers between devices: 3.67 us -> 0.92 us  [per_device(): lax.all_to_all(sent.reshape(count_y, SENT * LANES), 'gy', 0, 0, tiled=True)]
    unnamed x0 -> x4, local copies, waits for them, and re-layouts: none -> 1.83 us
    pallas_call x3, Pallas kernels: 4.75 us -> 3.26 us  [the longest x1 1.81 us: make_slope(): pl.pallas_call(slope_kernel, out_shape=(rows, rows, face, face, jax.Shape...]
  transfers between devices with their start and end apart: 7 -> 7, of which waited for: 1 -> 1; matrix products, arithmetic and copies ran while one was open for 0% -> 0% of each run, Pallas kernels for 16% -> 14%
where the time goes in v5:
time: 63.1 us; the launch traced here: 62.8 us
  starting transfers between devices  24.2 us (38%)
  blocking collectives  21.5 us (34%)
  Pallas kernels  13.6 us (22%)
  local copies, waits for them, and re-layouts  1.83 us (3%)
  waiting for transfers between devices  0.93 us (1%)
  between operations  0.74 us (1%)
    all_to_all x1, blocking collectives, per_device(): sums = lax.all_to_all(sums, ('gx', 'gy'), 0, 0, tiled=True)  21.5 us
    ppermute x6, starting transfers between devices, shift(): lax.ppermute(cells, axis, [(i, (i + by) % count) for i in range(count)])  14.8 us
    all_to_all x1, starting transfers between devices, per_device(): lax.all_to_all(sent.reshape(count_y, SENT * LANES), 'gy', 0, 0, tiled=True)  9.41 us
    pallas_call x1, Pallas kernels, make_source_inner(): pl.pallas_call(source_inner_kernel, out_shape=(wide,) * 4 + (half_block(d...  3.14 us
    pallas_call x1, Pallas kernels, adam(): pl.pallas_call(functools.partial(adam_kernel, cells), out_shape=(jax.Shap...  1.85 us
    unnamed x4, local copies, waits for them, and re-layouts  1.83 us
    pallas_call x1, Pallas kernels, make_slope(): pl.pallas_call(slope_kernel, out_shape=(rows, rows, face, face, jax.Shape...  1.81 us
    pallas_call x1, Pallas kernels, make_slope_inner(): pl.pallas_call(functools.partial(slope_inner_kernel, shape[0]), out_shape...  1.56 us
  transfers between devices with their start and end apart: 7, of which 1 were waited for; matrix products, arithmetic and copies ran while one was open for 0% of the time, Pallas kernels for 14%

profile of v5, /device:TPU:1, one launch (start us, length us, event | category | flops | bytes accessed | tf_op | source)
XLA Modules:
  0.0 62.8 jit_solution(312677660287090903)
XLA Ops:
  0.6 1.4 %shard_map.120 = (f32[2,8,8,1024]{3,2,1,0:T(8,128)S(1)}, f32[2,8,8,1024]{3,2,1,0:T(8,128)S(1)}, f32[7,8,128]{2,1,0:T(8,128)S(1)}, f32[256,128]{1,0:T(8,128)S(1)}, f32[32,128]{1,0:T(8,128)S(1)}) custom-call(f32[64,128]{1,0:T(8,128)} %bitcast.13, s32[1,64]{1,0:T(1,128)} %anchor_hbm.1, s32[1,64]{1,0:T(1,128)} %bitcast.14, f32[1,2]{1,0:T(1,128)} %bitcast.15, ...), custom_call_target="tpu_custom_call" | custom-call | tf_op jit(solution)/shard_map/pallas_call | solution.py:131
  2.0 3.3 %collective-permute-start = (f32[2,8,8,1024]{3,2,1,0:T(8,128)S(1)}, f32[2,8,8,1024]{3,2,1,0:T(8,128)S(1)}, u32[]{:S(2)}, u32[]{:S(2)}) collective-permute-start(f32[2,8,8,1024]{3,2,1,0:T(8,128)S(1)} %get-tuple-element.38), channel_id=1, source_target_pairs={{0,31},{1,0},{2,1},{3,2},{4,3},{5,4},{6,5},{7,6},{8,7},{9,8},{10,9... | collective-permute-start | bytes 1572872 | tf_op jit(solution)/shard_map/ppermute | solution.py:616
  5.3 0.0 collective-permute-start.1
  5.4 0.8 %shard_map.121 = f32[800,128]{1,0:T(8,128)} custom-call(f32[256,128]{1,0:T(8,128)S(1)} %get-tuple-element.36.packed_ref, f32[32,128]{1,0:T(8,128)S(1)} %get-tuple-element.37.anchors_ref), custom_call_target="tpu_custom_call" | custom-call | tf_op jit(solution)/shard_map/pallas_call | solution.py:176
  6.1 9.4 %all-to-all-start = ((f32[32,1,3200]{2,1,0:T(1,128)}), f32[32,1,3200]{2,1,0:T(1,128)S(1)}, u32[]{:S(2)}, u32[]{:S(2)}) async-start(f32[32,1,3200]{2,1,0:T(1,128)} %bitcast.3), calls=%async_computation | async-start | bytes 819200 | tf_op jit(solution)/shard_map/all_to_all | solution.py:639
  15.6 0.0 collective-permute-done.above_ref
  15.6 0.0 collective-permute-done.1.below_ref
  15.6 0.0 copy-start
  15.6 0.8 %copy-done = f32[2,8,8,1024]{3,2,1,0:T(8,128)} copy-done((f32[2,8,8,1024]{3,2,1,0:T(8,128)}, f32[2,8,8,1024]{3,2,1,0:T(8,128)S(1)}, u32[]{:S(2)}) %copy-start) | copy-done | bytes 524312
  16.4 0.0 copy-start.1
  16.4 1.0 %copy-done.1 = f32[2,8,8,1024]{3,2,1,0:T(8,128)S(1)} copy-done((f32[2,8,8,1024]{3,2,1,0:T(8,128)S(1)}, f32[2,8,8,1024]{3,2,1,0:T(8,128)}, u32[]{:S(2)}) %copy-start.1) | copy-done | bytes 524312
  17.4 1.8 %shard_map.122 = (f32[2048,128]{1,0:T(8,128)S(1)}, f32[2048,128]{1,0:T(8,128)S(1)}, f32[4,88,128]{2,1,0:T(8,128)S(1)}, f32[4,88,128]{2,1,0:T(8,128)S(1)}, f32[8,128]{1,0:T(8,128)S(1)}) custom-call(f32[16,8,1024]{2,1,0:T(8,128)} %filtered_hbm.3, f32[16,8,1024]{2,1,0:T(8,128)} %sensitivity_hbm.3, f32[2,8,8,1024]{3,2,1,0:T(8,128)S(1)} %collective-permute-done.above_ref, ...), custom_call_target="tpu_custom_call" | custom-call | flops 4000000 | bytes 4000000 | tf_op jit(solution)/shard_map/pallas_call | solution.py:305
  19.2 1.7 %collective-permute-start.4 = (f32[4,88,128]{2,1,0:T(8,128)S(1)}, f32[4,88,128]{2,1,0:T(8,128)S(1)}, u32[]{:S(2)}, u32[]{:S(2)}) collective-permute-start(f32[4,88,128]{2,1,0:T(8,128)S(1)} %get-tuple-element.45), channel_id=1, source_target_pairs={{0,32},{32,64},{64,96},{96,128},{128,160},{160,192},{192,224},{224... | collective-permute-start | bytes 540680 | tf_op jit(solution)/shard_map/ppermute | solution.py:616
  20.9 4.0 %collective-permute-start.5 = (f32[4,88,128]{2,1,0:T(8,128)S(1)}, f32[4,88,128]{2,1,0:T(8,128)S(1)}, u32[]{:S(2)}, u32[]{:S(2)}) collective-permute-start(f32[4,88,128]{2,1,0:T(8,128)S(1)} %get-tuple-element.46), channel_id=1, source_target_pairs={{0,224},{32,0},{64,32},{96,64},{128,96},{160,128},{192,160},{224,1... | collective-permute-start | bytes 540680 | tf_op jit(solution)/shard_map/ppermute | solution.py:616
  25.0 0.9 %all-to-all-done = f32[32,1,3200]{2,1,0:T(1,128)S(1)} async-done(((f32[32,1,3200]{2,1,0:T(1,128)}), f32[32,1,3200]{2,1,0:T(1,128)S(1)}, u32[]{:S(2)}, u32[]{:S(2)}) %all-to-all-start) | async-done | bytes 409632 | tf_op jit(solution)/shard_map/all_to_all | solution.py:639
  25.9 0.7 %shard_map.123 = (f32[3088,128]{1,0:T(8,128)S(1)}, f32[4,88,128]{2,1,0:T(8,128)S(1)}, f32[4,88,128]{2,1,0:T(8,128)S(1)}) custom-call(f32[800,128]{1,0:T(8,128)S(1)} %bitcast.9, f32[2048,128]{1,0:T(8,128)S(1)} %get-tuple-element.41.base_ref, f32[2048,128]{1,0:T(8,128)S(1)} %get-tuple-element.42.slope_ref), custom_call_target="tpu_custom_call" | custom-call | tf_op jit(solution)/shard_map/pallas_call | solution.py:338
  26.6 1.7 %collective-permute-start.2 = (f32[4,88,128]{2,1,0:T(8,128)S(1)}, f32[4,88,128]{2,1,0:T(8,128)S(1)}, u32[]{:S(2)}, u32[]{:S(2)}) collective-permute-start(f32[4,88,128]{2,1,0:T(8,128)S(1)} %get-tuple-element.43), channel_id=1, source_target_pairs={{0,32},{32,64},{64,96},{96,128},{128,160},{160,192},{192,224},{224... | collective-permute-start | bytes 540680 | tf_op jit(solution)/shard_map/ppermute | solution.py:616
  28.3 4.0 %collective-permute-start.3 = (f32[4,88,128]{2,1,0:T(8,128)S(1)}, f32[4,88,128]{2,1,0:T(8,128)S(1)}, u32[]{:S(2)}, u32[]{:S(2)}) collective-permute-start(f32[4,88,128]{2,1,0:T(8,128)S(1)} %get-tuple-element.44), channel_id=1, source_target_pairs={{0,224},{32,0},{64,32},{96,64},{128,96},{160,128},{192,160},{224,1... | collective-permute-start | bytes 540680 | tf_op jit(solution)/shard_map/ppermute | solution.py:616
  32.3 1.6 %shard_map.124 = (f32[3088,128]{1,0:T(8,128)S(1)}, f32[3088,128]{1,0:T(8,128)S(1)}, f32[3088,128]{1,0:T(8,128)S(1)}, f32[3088,128]{1,0:T(8,128)S(1)}, f32[8,8,1024]{2,1,0:T(8,128)S(1)}, /*index=5*/f32[8,128]{1,0:T(8,128)S(1)}) custom-call(f32[2048,128]{1,0:T(8,128)S(1)} %get-tuple-element.42.slope_ref, f32[7,8,128]{2,1,0:T(8,128)S(1)} %get-tuple-element.40.masks_ref), custom_call_target="tpu_custom_call" | custom-call | flops 15000000 | bytes 8000000 | tf_op jit(solution)/shard_map/pallas_call | solution.py:443
  33.9 3.1 %shard_map.126 = (f32[3088,128]{1,0:T(8,128)S(1)}, f32[3088,128]{1,0:T(8,128)S(1)}, f32[3088,128]{1,0:T(8,128)S(1)}, f32[3088,128]{1,0:T(8,128)S(1)}, f32[8,8,10...) custom-call(f32[800,128]{1,0:T(8,128)S(1)} %bitcast.10, ...), custom_call_target="tpu_custom_call", output_to_operand_aliasing={{0}: (8, {})} | custom-call | flops 40000000 | bytes 16000000 | tf_op jit(solution)/shard_map/pallas_call | solution.py:507
  37.0 0.0 collective-permute-done.4.left_ref
  37.0 0.0 collective-permute-done.5.right_ref
  37.0 1.1 %shard_map.125 = (f32[3088,128]{1,0:T(8,128)S(1)}, f32[3088,128]{1,0:T(8,128)S(1)}, f32[3088,128]{1,0:T(8,128)S(1)}, f32[3088,128]{1,0:T(8,128)S(1)}, f32[8,8,1024]{2,1,0:T(8,128)S(1)}, /*index=5*/f32[8,128]{1,0:T(8,128)S(1)}) custom-call(f32[4,88,128]{2,1,0:T(8,128)S(1)} %collective-permute-do, ...), custom_call_target="tpu_custom_call", output_to_operand_aliasing={{0}: (4, {}), {1}: (5, {}), {2}: (6, {}), {3}: (7, {})} | custom-call | flops 10000000 | bytes 6000000 | tf_op jit(solution)/shard_map/pallas_call | solution.py:469
  38.1 0.0 collective-permute-done.2.left_ref
  38.1 0.0 collective-permute-done.3.right_ref
  38.2 1.3 %shard_map.127 = (f32[3088,128]{1,0:T(8,128)S(1)}, f32[3088,128]{1,0:T(8,128)S(1)}, f32[3088,128]{1,0:T(8,128)S(1)}, f32[3088,128]{1,0:T(8,128)S(1)}, f32[8,8,1024]{2,1,0:T(8,128)S(1)}, /*index=5*/f32[256,128]{1,0:T(8,128)S(1)}) custom-call(f32[4,88,128]{2,1,0:T(8,128)S(1)} %collective-permute-do, ...), custom_call_target="tpu_custom_call", output_to_operand_aliasing={{0}: (7, {}), {1}: (8, {}), {2}: (9, {}), {3}: (10, {})} | custom-call | tf_op jit(solution)/shard_map/pallas_call | solution.py:549
  39.5 21.5 %all_to_all.20 = f32[256,1,128]{2,1,0:T(1,128)S(1)} all-to-all(f32[256,1,128]{2,1,0:T(1,128)S(1)} %bitcast.12), channel_id=1, replica_groups=mesh['gx'=8,'gy'=32] {'gx','gy'}, dimensions={0} | all-to-all | bytes 262144 | tf_op jit(solution)/shard_map/all_to_all | solution.py:655
  60.9 1.9 %shard_map.128 = (f32[16,8,1024]{2,1,0:T(8,128)}, f32[16,8,1024]{2,1,0:T(8,128)}, f32[16,8,1024]{2,1,0:T(8,128)}, f32[16,8,1024]{2,1,0:T(8,128)}) custom-call(f32[256,128]{1,0:T(8,128)S(1)} %bitcast.11, f32[7,8,128]{2,1,0:T(8,128)S(1)} %get-tuple-element.40.masks_ref, f32[8,8,1024]{2,1,0:T(8,128)S(1)} %get-tuple-element.63.inner_ref, ...), custom_call_target="tpu_custom_call" | custom-call | tf_op jit(solution)/shard_map/pallas_call | solution.py:604
Async XLA Ops:
  2.0 13.5 %collective-permute-start = (f32[2,8,8,1024]{3,2,1,0:T(8,128)S(1)}, f32[2,8,8,1024]{3,2,1,0:T(8,128)S(1)}, u32[]{:S(2)}, u32[]{:S(2)}) collective-permute-start(f32[2,8,8,1024]{3,2,1,0:T(8,128)S(1)} %get-tuple-element.38), channel_id=1, source_target_pairs={{0,31},{1,0},{2,1},{3,2},{4,3},{5,4},{6,5},{7,6},{8,7},{9,8},{10,9... | collective-permute-start | bytes 1572872 | tf_op jit(solution)/shard_map/ppermute | solution.py:616
  5.3 10.2 %collective-permute-start.1 = (f32[2,8,8,1024]{3,2,1,0:T(8,128)S(1)}, f32[2,8,8,1024]{3,2,1,0:T(8,128)S(1)}, u32[]{:S(2)}, u32[]{:S(2)}) collective-permute-start(f32[2,8,8,1024]{3,2,1,0:T(8,128)S(1)} %get-tuple-element.39), channel_id=1, source_target_pairs={{0,1},{1,2},{2,3},{3,4},{4,5},{5,6},{6,7},{7,8},{8,9},{9,10},{10,1... | collective-permute-start | bytes 1572872 | tf_op jit(solution)/shard_map/ppermute | solution.py:616
  6.1 19.7 %all-to-all-start = ((f32[32,1,3200]{2,1,0:T(1,128)}), f32[32,1,3200]{2,1,0:T(1,128)S(1)}, u32[]{:S(2)}, u32[]{:S(2)}) async-start(f32[32,1,3200]{2,1,0:T(1,128)} %bitcast.3), calls=%async_computation | async-start | bytes 819200 | tf_op jit(solution)/shard_map/all_to_all | solution.py:639
  15.6 0.8 %copy-start = (f32[2,8,8,1024]{3,2,1,0:T(8,128)}, f32[2,8,8,1024]{3,2,1,0:T(8,128)S(1)}, u32[]{:S(2)}) copy-start(f32[2,8,8,1024]{3,2,1,0:T(8,128)S(1)} %collective-permute-done.1.below_ref) | copy-start | bytes 1572868
  16.4 1.0 %copy-start.1 = (f32[2,8,8,1024]{3,2,1,0:T(8,128)S(1)}, f32[2,8,8,1024]{3,2,1,0:T(8,128)}, u32[]{:S(2)}) copy-start(f32[2,8,8,1024]{3,2,1,0:T(8,128)} %copy-done) | copy-start | bytes 1572868
  19.2 17.8 %collective-permute-start.4 = (f32[4,88,128]{2,1,0:T(8,128)S(1)}, f32[4,88,128]{2,1,0:T(8,128)S(1)}, u32[]{:S(2)}, u32[]{:S(2)}) collective-permute-start(f32[4,88,128]{2,1,0:T(8,128)S(1)} %get-tuple-element.45), channel_id=1, source_target_pairs={{0,32},{32,64},{64,96},{96,128},{128,160},{160,192},{192,224},{224... | collective-permute-start | bytes 540680 | tf_op jit(solution)/shard_map/ppermute | solution.py:616
  20.9 16.1 %collective-permute-start.5 = (f32[4,88,128]{2,1,0:T(8,128)S(1)}, f32[4,88,128]{2,1,0:T(8,128)S(1)}, u32[]{:S(2)}, u32[]{:S(2)}) collective-permute-start(f32[4,88,128]{2,1,0:T(8,128)S(1)} %get-tuple-element.46), channel_id=1, source_target_pairs={{0,224},{32,0},{64,32},{96,64},{128,96},{160,128},{192,160},{224,1... | collective-permute-start | bytes 540680 | tf_op jit(solution)/shard_map/ppermute | solution.py:616
  26.6 11.6 %collective-permute-start.2 = (f32[4,88,128]{2,1,0:T(8,128)S(1)}, f32[4,88,128]{2,1,0:T(8,128)S(1)}, u32[]{:S(2)}, u32[]{:S(2)}) collective-permute-start(f32[4,88,128]{2,1,0:T(8,128)S(1)} %get-tuple-element.43), channel_id=1, source_target_pairs={{0,32},{32,64},{64,96},{96,128},{128,160},{160,192},{192,224},{224... | collective-permute-start | bytes 540680 | tf_op jit(solution)/shard_map/ppermute | solution.py:616
  28.3 9.9 %collective-permute-start.3 = (f32[4,88,128]{2,1,0:T(8,128)S(1)}, f32[4,88,128]{2,1,0:T(8,128)S(1)}, u32[]{:S(2)}, u32[]{:S(2)}) collective-permute-start(f32[4,88,128]{2,1,0:T(8,128)S(1)} %get-tuple-element.44), channel_id=1, source_target_pairs={{0,224},{32,0},{64,32},{96,64},{128,96},{160,128},{192,160},{224,1... | collective-permute-start | bytes 540680 | tf_op jit(solution)/shard_map/ppermute | solution.py:616

commit v6 on v5

--- a/solution.py
+++ b/solution.py
@@ -260,13 +260,17 @@
     return jax.ShapeDtypeStruct((shape[0] * (shape[2] // LANES) * TALL, LANES), F32)
 
 
+def half_rows(rows):
+    return jax.ShapeDtypeStruct((rows.shape[0] // 2, LANES), F32)
+
+
 def face_shape(shape):
     return jax.ShapeDtypeStruct((shape[2] // LANES // 2, 2 * FACE, LANES), F32)
 
 
 def slope_kernel(
     filtered_hbm, sensitivity_hbm, above_ref, below_ref, masks_ref,
-    s_ref, base_ref, low_ref, high_ref, volume_ref, filtered_ref, sensitivity_ref, sems,
+    s_ref, edge_ref, inner_hbm, low_ref, high_ref, volume_ref, filtered_ref, sensitivity_ref, base_ref, sems,
 ):
     copies = start_all(((filtered_hbm, filtered_ref), (sensitivity_hbm, sensitivity_ref)), sems)
     width_x, width_y, width_z = filtered_ref.shape
@@ -295,19 +299,26 @@
         return total
 
     volume_ref[...] = lax.fori_loop(0, width_x // 2, pair, jnp.zeros((8, LANES), F32))
+    part = HALO * chunks * TALL
+    copy = pltpu.make_async_copy(base_ref.at[pl.ds(part, 2 * part)], inner_hbm, sems.at[2])
+    copy.start()
+    edge_ref[0:part, :] = base_ref[0:part, :]
+    edge_ref[part:, :] = base_ref[3 * part :, :]
     fill_faces(s_ref, low_ref, high_ref, width_x, chunks, flat_row)
+    copy.wait()
 
 
 def make_slope(filtered, sensitivity, above, below, masks):
     face = face_shape(filtered.shape)
     rows = flat(filtered.shape)
+    part = half_rows(rows)
     block = pltpu.VMEM(filtered.shape, F32)
     return pl.pallas_call(
         slope_kernel,
-        out_shape=(rows, rows, face, face, jax.ShapeDtypeStruct((8, LANES), F32)),
+        out_shape=(rows, part, part, face, face, jax.ShapeDtypeStruct((8, LANES), F32)),
         in_specs=[HBM] * 2 + [VMEM] * 3,
-        out_specs=(VMEM,) * 5,
-        scratch_shapes=[block, block, pltpu.SemaphoreType.DMA((2,))],
+        out_specs=(VMEM, VMEM, HBM, VMEM, VMEM, VMEM),
+        scratch_shapes=[block, block, pltpu.VMEM(rows.shape, F32), pltpu.SemaphoreType.DMA((3,))],
         compiler_params=params(8),
         cost_estimate=pl.CostEstimate(flops=4_000_000, bytes_accessed=4_000_000, transcendentals=300_000),
     )(in_hbm(filtered), in_hbm(sensitivity), above, below, masks)
@@ -315,11 +326,12 @@
 
 def make_layers(layers, s_ref, slope_ref, base_ref, own, beside, chunks):
     half = iota((8, LANES), 0) < 4
-    for x, c in itertools.product(layers, range(chunks)):
+    for (i, x), c in itertools.product(enumerate(layers), range(chunks)):
         line = pl.ds((x * chunks + c) * 8, 8)
         for t, tile in enumerate(tall_tiles(half, own[line, :], beside[line, :])):
-            rows = pl.ds(flat_row(x, c, chunks) + 8 * t, 8)
-            s_ref[pl.ds(tall_row(x, c, chunks) + 8 * t, 8), :] = slope_ref[rows, :] * (base_ref[rows, :] + tile)
+            slope = slope_ref[pl.ds(flat_row(x, c, chunks) + 8 * t, 8), :]
+            base = base_ref[pl.ds(flat_row(i, c, chunks) + 8 * t, 8), :]
+            s_ref[pl.ds(tall_row(x, c, chunks) + 8 * t, 8), :] = slope * (base + tile)
 
 
 def edge_kernel(width_x, recv_ref, base_ref, slope_ref, s_ref, low_ref, high_ref, own, beside):
@@ -428,7 +440,10 @@
 TILE = jax.ShapeDtypeStruct((8, LANES), F32)
 
 
-def slope_inner_kernel(width_x, slope_ref, masks_ref, s_ref, one, two, three, raw_ref, square_ref):
+def slope_inner_kernel(
+    width_x, slope_ref, masks_ref, base_hbm, design_hbm, s_ref, one, two, three, raw_ref, square_ref, base_ref, design_ref, sems
+):
+    copies = start_all(((base_hbm, base_ref), (design_hbm, design_ref)), sems)
     chunks = raw_ref.shape[2] // LANES
     s_ref[pl.ds(tall_row(0, 0, chunks), slope_ref.shape[0]), :] = slope_ref[...]
     total = zero_tile()
@@ -436,25 +451,31 @@
         store_layer(raw_ref, i, values)
         total = add_products(total, values, values)
     square_ref[...] = total
-
-
-def make_slope_inner(s, masks, shape):
+    for copy in copies:
+        copy.wait()
+
+
+def make_slope_inner(s, masks, base, design):
+    shape = design.shape
     wide = extended(shape)
     return pl.pallas_call(
         functools.partial(slope_inner_kernel, shape[0]),
-        out_shape=(wide, wide, wide, wide, half_block(shape)[0], TILE),
-        in_specs=[VMEM] * 2,
-        out_specs=(VMEM,) * 6,
+        out_shape=(wide, wide, wide, wide, half_block(shape)[0], TILE)
+        + (jax.ShapeDtypeStruct(base.shape, F32), jax.ShapeDtypeStruct(shape, F32)),
+        in_specs=[VMEM] * 2 + [HBM] * 2,
+        out_specs=(VMEM,) * 8,
+        scratch_shapes=[pltpu.SemaphoreType.DMA((2,))],
         compiler_params=params(8),
         cost_estimate=pl.CostEstimate(flops=15_000_000, bytes_accessed=8_000_000, transcendentals=0),
-    )(s, masks)
+    )(s, masks, in_hbm(base), in_hbm(design))
 
 
 def slope_outer_kernel(
-    width_x, left_ref, right_ref, masks_ref, inner_square_ref, s_in, one_in, two_in, three_in,
-    s_ref, one, two, three, raw_ref, square_ref,
+    width_x, left_ref, right_ref, masks_ref, inner_square_ref, s_in, one_in, two_in, three_in, second_hbm,
+    s_ref, one, two, three, raw_ref, square_ref, second_ref, sems,
 ):
     del s_in, one_in, two_in, three_in
+    (copy,) = start_all(((second_hbm, second_ref),), sems)
     chunks = raw_ref.shape[2] // LANES
     read_faces(s_ref, left_ref, right_ref, masks_ref, width_x, chunks)
     total = inner_square_ref[...]
@@ -462,28 +483,31 @@
         store_layer(raw_ref, i, values)
         total = add_products(total, values, values)
     square_ref[...] = total
-
-
-def make_slope_outer(left, right, masks, square, wide, shape):
+    copy.wait()
+
+
+def make_slope_outer(left, right, masks, square, wide, second_moment):
+    shape = second_moment.shape
     same = extended(shape)
     return pl.pallas_call(
         functools.partial(slope_outer_kernel, shape[0]),
-        out_shape=(same, same, same, same, half_block(shape)[1], TILE),
-        in_specs=[VMEM] * 8,
-        out_specs=(VMEM,) * 6,
+        out_shape=(same, same, same, same, half_block(shape)[1], TILE, jax.ShapeDtypeStruct(shape, F32)),
+        in_specs=[VMEM] * 8 + [HBM],
+        out_specs=(VMEM,) * 7,
+        scratch_shapes=[pltpu.SemaphoreType.DMA((1,))],
         input_output_aliases={4: 0, 5: 1, 6: 2, 7: 3},
         compiler_params=params(8),
         cost_estimate=pl.CostEstimate(flops=10_000_000, bytes_accessed=6_000_000, transcendentals=0),
-    )(left, right, masks, square, *wide)[4:]
+    )(left, right, masks, square, *wide, in_hbm(second_moment))[4:]
 
 
 def source_inner_kernel(
-    recv_ref, base_ref, slope_ref, masks_ref, slope_raw_ref, design_hbm, first_hbm, second_hbm, edges_ref,
-    s_ref, one, two, three, raw_ref, sums_ref, design_ref, first_ref, second_ref, own, beside, sems,
+    recv_ref, base_ref, slope_ref, masks_ref, slope_raw_ref, first_hbm, edges_ref,
+    s_ref, one, two, three, raw_ref, sums_ref, first_ref, own, beside, sems,
 ):
     del edges_ref
-    copies = start_all(((design_hbm, design_ref), (first_hbm, first_ref), (second_hbm, second_ref)), sems)
-    width_x, width_y, width_z = design_ref.shape
+    (copy,) = start_all(((first_hbm, first_ref),), sems)
+    width_x, width_y, width_z = first_ref.shape
     chunks = width_z // LANES
     scatter(recv_ref, own, beside, range(HALO, width_x - HALO, HALO), width_y * chunks)
     make_layers(range(HALO, width_x - HALO), s_ref, slope_ref, base_ref, own, beside, chunks)
@@ -494,31 +518,24 @@
         ab = add_products(ab, values, load_layer(slope_raw_ref, i, chunks))
     sums_ref[0] = aa
     sums_ref[1] = ab
-    for copy in copies:
-        copy.wait()
-
-
-def make_source_inner(
-    recv, base, slope, masks, slope_raw, design, first_moment, second_moment, edges
-):
-    block = jax.ShapeDtypeStruct(design.shape, F32)
-    wide = extended(design.shape)
-    scratch = pltpu.VMEM((design.size // LANES, LANES), F32)
+    copy.wait()
+
+
+def make_source_inner(recv, base, slope, masks, slope_raw, first_moment, edges):
+    shape = first_moment.shape
+    wide = extended(shape)
+    scratch = pltpu.VMEM((first_moment.size // LANES, LANES), F32)
     return pl.pallas_call(
         source_inner_kernel,
         out_shape=(wide,) * 4
-        + (half_block(design.shape)[0], jax.ShapeDtypeStruct((2, 8, LANES), F32))
-        + (block,) * 3,
-        in_specs=[VMEM] * 5 + [HBM] * 3 + [VMEM],
-        out_specs=(VMEM,) * 9,
-        input_output_aliases={8: 0},
-        scratch_shapes=[scratch] * 2 + [pltpu.SemaphoreType.DMA((3,))],
+        + (half_block(shape)[0], jax.ShapeDtypeStruct((2, 8, LANES), F32), jax.ShapeDtypeStruct(shape, F32)),
+        in_specs=[VMEM] * 5 + [HBM] + [VMEM],
+        out_specs=(VMEM,) * 7,
+        input_output_aliases={6: 0},
+        scratch_shapes=[scratch] * 2 + [pltpu.SemaphoreType.DMA((1,))],
         compiler_params=params(8),
         cost_estimate=pl.CostEstimate(flops=40_000_000, bytes_accessed=16_000_000, transcendentals=0),
-    )(
-        recv, base, slope, masks, slope_raw,
-        in_hbm(design), in_hbm(first_moment), in_hbm(second_moment), edges,
-    )
+    )(recv, base, slope, masks, slope_raw, in_hbm(first_moment), edges)
 
 
 def source_outer_kernel(
@@ -638,16 +655,16 @@
     sent = make_send(packed, anchors)
     received = lax.all_to_all(sent.reshape(count_y, SENT * LANES), "gy", 0, 0, tiled=True).reshape(sent.shape)
 
-    slope, base, low, high, volume = make_slope(filtered, sensitivity, above, below, masks)
+    slope, base_edges, base, low, high, volume = make_slope(filtered, sensitivity, above, below, masks)
     left, right = shift(high, "gx", 1), shift(low, "gx", -1)
     shape = design.shape
-    *wide, slope_inner, square = make_slope_inner(slope, masks, shape)
-    slope_outer, square = make_slope_outer(left, right, masks, square, wide, shape)
-
-    source, low, high = make_edges(received, base, slope, shape)
+    *wide, slope_inner, square, base, design = make_slope_inner(slope, masks, base, design)
+    slope_outer, square, second_moment = make_slope_outer(left, right, masks, square, wide, second_moment)
+
+    source, low, high = make_edges(received, base_edges, slope, shape)
     left, right = shift(high, "gx", 1), shift(low, "gx", -1)
-    *wide, inner, sums, design, first_moment, second_moment = make_source_inner(
-        received, base, slope, masks, slope_inner, design, first_moment, second_moment, source
+    *wide, inner, sums, first_moment = make_source_inner(
+        received, base, slope, masks, slope_inner, first_moment, source
     )
     outer, sums = make_source_outer(
         left, right, masks, slope_outer, volume, sums, square, wide, count_x * count_y, shape

time: 63.1 us -> 62.5 us (level)
  waiting for transfers between devices: 0.93 us -> 2.05 us
  local copies, waits for them, and re-layouts: 1.83 us -> 0.79 us
    pallas_call x2, Pallas kernels: 4.95 us -> 3.71 us  [the longest x1 1.89 us: make_slope(): pl.pallas_call(slope_kernel, out_shape=(rows, part, part, face, face, jax...]
    all_to_all x1, waiting for transfers between devices: 0.92 us -> 2.04 us  [per_device(): lax.all_to_all(sent.reshape(count_y, SENT * LANES), 'gy', 0, 0, tiled=True)]
    unnamed x4 -> x2, local copies, waits for them, and re-layouts: 1.83 us -> 0.79 us
    pallas_call x1, Pallas kernels: 1.1 us -> 2.06 us  [make_slope_outer(): pl.pallas_call(functools.partial(slope_outer_kernel, shape[0]), out_shape...]
where the time goes in v6:
time: 62.5 us; the launch traced here: 62.2 us
  starting transfers between devices  24 us (38%)
  blocking collectives  21.3 us (34%)
  Pallas kernels  13.3 us (21%)
  waiting for transfers between devices  2.05 us (3%)
  local copies, waits for them, and re-layouts  0.79 us (1%)
  between operations  0.75 us (1%)
    all_to_all x1, blocking collectives, per_device(): sums = lax.all_to_all(sums, ('gx', 'gy'), 0, 0, tiled=True)  21.3 us
    ppermute x6, starting transfers between devices, shift(): lax.ppermute(cells, axis, [(i, (i + by) % count) for i in range(count)])  14.6 us
    all_to_all x1, starting transfers between devices, per_device(): lax.all_to_all(sent.reshape(count_y, SENT * LANES), 'gy', 0, 0, tiled=True)  9.41 us
    pallas_call x1, Pallas kernels, make_slope_outer(): pl.pallas_call(functools.partial(slope_outer_kernel, shape[0]), out_shape...  2.06 us
    all_to_all x1, waiting for transfers between devices, per_device(): lax.all_to_all(sent.reshape(count_y, SENT * LANES), 'gy', 0, 0, tiled=True)  2.04 us
    pallas_call x1, Pallas kernels, make_slope(): pl.pallas_call(slope_kernel, out_shape=(rows, part, part, face, face, jax...  1.89 us
    pallas_call x1, Pallas kernels, adam(): pl.pallas_call(functools.partial(adam_kernel, cells), out_shape=(jax.Shap...  1.85 us
    pallas_call x1, Pallas kernels, make_source_inner(): pl.pallas_call(source_inner_kernel, out_shape=(wide,) * 4 + (half_block(s...  1.82 us
  transfers between devices with their start and end apart: 7, of which 1 were waited for; matrix products, arithmetic and copies ran while one was open for 0% of the time, Pallas kernels for 14%

profile of v6, /device:TPU:1, one launch (start us, length us, event | category | flops | bytes accessed | tf_op | source)
XLA Modules:
  0.0 62.2 jit_solution(15572719685638380262)
XLA Ops:
  0.6 1.4 %shard_map.120 = (f32[2,8,8,1024]{3,2,1,0:T(8,128)S(1)}, f32[2,8,8,1024]{3,2,1,0:T(8,128)S(1)}, f32[7,8,128]{2,1,0:T(8,128)S(1)}, f32[256,128]{1,0:T(8,128)S(1)}, f32[32,128]{1,0:T(8,128)S(1)}) custom-call(f32[64,128]{1,0:T(8,128)} %bitcast.13, s32[1,64]{1,0:T(1,128)} %anchor_hbm.1, s32[1,64]{1,0:T(1,128)} %bitcast.14, f32[1,2]{1,0:T(1,128)} %bitcast.15, ...), custom_call_target="tpu_custom_call" | custom-call | tf_op jit(solution)/shard_map/pallas_call | solution.py:131
  2.0 3.3 %collective-permute-start = (f32[2,8,8,1024]{3,2,1,0:T(8,128)S(1)}, f32[2,8,8,1024]{3,2,1,0:T(8,128)S(1)}, u32[]{:S(2)}, u32[]{:S(2)}) collective-permute-start(f32[2,8,8,1024]{3,2,1,0:T(8,128)S(1)} %get-tuple-element.40), channel_id=1, source_target_pairs={{0,31},{1,0},{2,1},{3,2},{4,3},{5,4},{6,5},{7,6},{8,7},{9,8},{10,9... | collective-permute-start | bytes 1572872 | tf_op jit(solution)/shard_map/ppermute | solution.py:633
  5.3 0.0 collective-permute-start.1
  5.4 0.8 %shard_map.121 = f32[800,128]{1,0:T(8,128)} custom-call(f32[256,128]{1,0:T(8,128)S(1)} %get-tuple-element.38.packed_ref, f32[32,128]{1,0:T(8,128)S(1)} %get-tuple-element.39.anchors_ref), custom_call_target="tpu_custom_call" | custom-call | tf_op jit(solution)/shard_map/pallas_call | solution.py:176
  6.1 9.4 %all-to-all-start = ((f32[32,1,3200]{2,1,0:T(1,128)}), f32[32,1,3200]{2,1,0:T(1,128)S(1)}, u32[]{:S(2)}, u32[]{:S(2)}) async-start(f32[32,1,3200]{2,1,0:T(1,128)} %bitcast.3), calls=%async_computation | async-start | bytes 819200 | tf_op jit(solution)/shard_map/all_to_all | solution.py:656
  15.6 0.0 collective-permute-done.above_ref
  15.6 0.0 collective-permute-done.1.below_ref
  15.6 1.9 %shard_map.122 = (f32[2048,128]{1,0:T(8,128)S(1)}, f32[1024,128]{1,0:T(8,128)S(1)}, f32[1024,128]{1,0:T(8,128)S(1)}, f32[4,88,128]{2,1,0:T(8,128)S(1)}, f32[4,88,128]{2,1,0:T(8,128)S(1)}, /*index=5*/f32[8,128]{1,0:T(8,128)S(1)}) custom-call(f32[16,8,1024]{2,1,0:T(8,128)} %filtered_hbm.3, f32[16,8,1024]{2,1,0:T(8,128)} %sensitivity_hbm.3, ...), custom_call_target="tpu_custom_call" | custom-call | flops 4000000 | bytes 4000000 | tf_op jit(solution)/shard_map/pallas_call | solution.py:316
  17.5 0.0 copy-start
  17.5 0.8 %copy-done = f32[1024,128]{1,0:T(8,128)} copy-done((f32[1024,128]{1,0:T(8,128)}, f32[1024,128]{1,0:T(8,128)S(1)}, u32[]{:S(2)}) %copy-start) | copy-done | bytes 524312
  18.3 1.6 %collective-permute-start.4 = (f32[4,88,128]{2,1,0:T(8,128)S(1)}, f32[4,88,128]{2,1,0:T(8,128)S(1)}, u32[]{:S(2)}, u32[]{:S(2)}) collective-permute-start(f32[4,88,128]{2,1,0:T(8,128)S(1)} %get-tuple-element.47), channel_id=1, source_target_pairs={{0,32},{32,64},{64,96},{96,128},{128,160},{160,192},{192,224},{224... | collective-permute-start | bytes 540680 | tf_op jit(solution)/shard_map/ppermute | solution.py:633
  19.9 3.9 %collective-permute-start.5 = (f32[4,88,128]{2,1,0:T(8,128)S(1)}, f32[4,88,128]{2,1,0:T(8,128)S(1)}, u32[]{:S(2)}, u32[]{:S(2)}) collective-permute-start(f32[4,88,128]{2,1,0:T(8,128)S(1)} %get-tuple-element.48), channel_id=1, source_target_pairs={{0,224},{32,0},{64,32},{96,64},{128,96},{160,128},{192,160},{224,1... | collective-permute-start | bytes 540680 | tf_op jit(solution)/shard_map/ppermute | solution.py:633
  23.9 2.0 %all-to-all-done = f32[32,1,3200]{2,1,0:T(1,128)S(1)} async-done(((f32[32,1,3200]{2,1,0:T(1,128)}), f32[32,1,3200]{2,1,0:T(1,128)S(1)}, u32[]{:S(2)}, u32[]{:S(2)}) %all-to-all-start) | async-done | bytes 409632 | tf_op jit(solution)/shard_map/all_to_all | solution.py:656
  25.9 0.7 %shard_map.123 = (f32[3088,128]{1,0:T(8,128)S(1)}, f32[4,88,128]{2,1,0:T(8,128)S(1)}, f32[4,88,128]{2,1,0:T(8,128)S(1)}) custom-call(f32[800,128]{1,0:T(8,128)S(1)} %bitcast.9, f32[1024,128]{1,0:T(8,128)S(1)} %get-tuple-element.43.base_ref, f32[2048,128]{1,0:T(8,128)S(1)} %get-tuple-element.44.slope_ref), custom_call_target="tpu_custom_call" | custom-call | tf_op jit(solution)/shard_map/pallas_call | solution.py:350
  26.6 1.7 %collective-permute-start.2 = (f32[4,88,128]{2,1,0:T(8,128)S(1)}, f32[4,88,128]{2,1,0:T(8,128)S(1)}, u32[]{:S(2)}, u32[]{:S(2)}) collective-permute-start(f32[4,88,128]{2,1,0:T(8,128)S(1)} %get-tuple-element.45), channel_id=1, source_target_pairs={{0,32},{32,64},{64,96},{96,128},{128,160},{160,192},{192,224},{224... | collective-permute-start | bytes 540680 | tf_op jit(solution)/shard_map/ppermute | solution.py:633
  28.3 4.0 %collective-permute-start.3 = (f32[4,88,128]{2,1,0:T(8,128)S(1)}, f32[4,88,128]{2,1,0:T(8,128)S(1)}, u32[]{:S(2)}, u32[]{:S(2)}) collective-permute-start(f32[4,88,128]{2,1,0:T(8,128)S(1)} %get-tuple-element.46), channel_id=1, source_target_pairs={{0,224},{32,0},{64,32},{96,64},{128,96},{160,128},{192,160},{224,1... | collective-permute-start | bytes 540680 | tf_op jit(solution)/shard_map/ppermute | solution.py:633
  32.3 1.6 %shard_map.124 = (f32[3088,128]{1,0:T(8,128)S(1)}, f32[3088,128]{1,0:T(8,128)S(1)}, f32[3088,128]{1,0:T(8,128)S(1)}, f32[3088,128]{1,0:T(8,128)S(1)}, f32[8,8,10...) custom-call(f32[2048,128]{1,0:T(8,128)S(1)} %get-tuple-element.44.slope_ref, ...), custom_call_target="tpu_custom_call" | custom-call | flops 15000000 | bytes 8000000 | tf_op jit(solution)/shard_map/pallas_call | solution.py:461
  33.9 1.8 %shard_map.126 = (f32[3088,128]{1,0:T(8,128)S(1)}, f32[3088,128]{1,0:T(8,128)S(1)}, f32[3088,128]{1,0:T(8,128)S(1)}, f32[3088,128]{1,0:T(8,128)S(1)}, f32[8,8,10...) custom-call(f32[800,128]{1,0:T(8,128)S(1)} %bitcast.10, ...), custom_call_target="tpu_custom_call", output_to_operand_aliasing={{0}: (6, {})} | custom-call | flops 40000000 | bytes 16000000 | tf_op jit(solution)/shard_map/pallas_call | solution.py:528
  35.7 0.0 collective-permute-done.4.left_ref
  35.7 0.0 collective-permute-done.5.right_ref
  35.7 2.1 %shard_map.125 = (f32[3088,128]{1,0:T(8,128)S(1)}, f32[3088,128]{1,0:T(8,128)S(1)}, f32[3088,128]{1,0:T(8,128)S(1)}, f32[3088,128]{1,0:T(8,128)S(1)}, f32[8,8,10...) custom-call(f32[4,88,128]{2,1,0:T(8,128)S(1)} %collective-permute-do, ...), custom_call_target="tpu_custom_call", output_to_operand_aliasing={{0}: (4, {}), {1}: (5, {}), {2}: (6, {}), {3}: (7, {})} | custom-call | flops 10000000 | bytes 6000000 | tf_op jit(solution)/shard_map/pallas_call | solution.py:492
  37.8 0.0 collective-permute-done.2.left_ref
  37.8 0.0 collective-permute-done.3.right_ref
  37.8 1.3 %shard_map.127 = (f32[3088,128]{1,0:T(8,128)S(1)}, f32[3088,128]{1,0:T(8,128)S(1)}, f32[3088,128]{1,0:T(8,128)S(1)}, f32[3088,128]{1,0:T(8,128)S(1)}, f32[8,8,1024]{2,1,0:T(8,128)S(1)}, /*index=5*/f32[256,128]{1,0:T(8,128)S(1)}) custom-call(f32[4,88,128]{2,1,0:T(8,128)S(1)} %collective-permute-do, ...), custom_call_target="tpu_custom_call", output_to_operand_aliasing={{0}: (7, {}), {1}: (8, {}), {2}: (9, {}), {3}: (10, {})} | custom-call | tf_op jit(solution)/shard_map/pallas_call | solution.py:566
  39.1 21.3 %all_to_all.20 = f32[256,1,128]{2,1,0:T(1,128)S(1)} all-to-all(f32[256,1,128]{2,1,0:T(1,128)S(1)} %bitcast.12), channel_id=1, replica_groups=mesh['gx'=8,'gy'=32] {'gx','gy'}, dimensions={0} | all-to-all | bytes 262144 | tf_op jit(solution)/shard_map/all_to_all | solution.py:672
  60.3 1.9 %shard_map.128 = (f32[16,8,1024]{2,1,0:T(8,128)}, f32[16,8,1024]{2,1,0:T(8,128)}, f32[16,8,1024]{2,1,0:T(8,128)}, f32[16,8,1024]{2,1,0:T(8,128)}) custom-call(f32[256,128]{1,0:T(8,128)S(1)} %bitcast.11, f32[7,8,128]{2,1,0:T(8,128)S(1)} %get-tuple-element.42.masks_ref, f32[8,8,1024]{2,1,0:T(8,128)S(1)} %get-tuple-element.67.inner_ref, ...), custom_call_target="tpu_custom_call" | custom-call | tf_op jit(solution)/shard_map/pallas_call | solution.py:621
Async XLA Ops:
  2.0 13.5 %collective-permute-start = (f32[2,8,8,1024]{3,2,1,0:T(8,128)S(1)}, f32[2,8,8,1024]{3,2,1,0:T(8,128)S(1)}, u32[]{:S(2)}, u32[]{:S(2)}) collective-permute-start(f32[2,8,8,1024]{3,2,1,0:T(8,128)S(1)} %get-tuple-element.40), channel_id=1, source_target_pairs={{0,31},{1,0},{2,1},{3,2},{4,3},{5,4},{6,5},{7,6},{8,7},{9,8},{10,9... | collective-permute-start | bytes 1572872 | tf_op jit(solution)/shard_map/ppermute | solution.py:633
  5.3 10.2 %collective-permute-start.1 = (f32[2,8,8,1024]{3,2,1,0:T(8,128)S(1)}, f32[2,8,8,1024]{3,2,1,0:T(8,128)S(1)}, u32[]{:S(2)}, u32[]{:S(2)}) collective-permute-start(f32[2,8,8,1024]{3,2,1,0:T(8,128)S(1)} %get-tuple-element.41), channel_id=1, source_target_pairs={{0,1},{1,2},{2,3},{3,4},{4,5},{5,6},{6,7},{7,8},{8,9},{9,10},{10,1... | collective-permute-start | bytes 1572872 | tf_op jit(solution)/shard_map/ppermute | solution.py:633
  6.1 19.7 %all-to-all-start = ((f32[32,1,3200]{2,1,0:T(1,128)}), f32[32,1,3200]{2,1,0:T(1,128)S(1)}, u32[]{:S(2)}, u32[]{:S(2)}) async-start(f32[32,1,3200]{2,1,0:T(1,128)} %bitcast.3), calls=%async_computation | async-start | bytes 819200 | tf_op jit(solution)/shard_map/all_to_all | solution.py:656
  17.5 0.8 %copy-start = (f32[1024,128]{1,0:T(8,128)}, f32[1024,128]{1,0:T(8,128)S(1)}, u32[]{:S(2)}) copy-start(f32[1024,128]{1,0:T(8,128)S(1)} %get-tuple-element.49.base_hbm) | copy-start | bytes 1572868
  18.3 17.4 %collective-permute-start.4 = (f32[4,88,128]{2,1,0:T(8,128)S(1)}, f32[4,88,128]{2,1,0:T(8,128)S(1)}, u32[]{:S(2)}, u32[]{:S(2)}) collective-permute-start(f32[4,88,128]{2,1,0:T(8,128)S(1)} %get-tuple-element.47), channel_id=1, source_target_pairs={{0,32},{32,64},{64,96},{96,128},{128,160},{160,192},{192,224},{224... | collective-permute-start | bytes 540680 | tf_op jit(solution)/shard_map/ppermute | solution.py:633
  19.9 15.8 %collective-permute-start.5 = (f32[4,88,128]{2,1,0:T(8,128)S(1)}, f32[4,88,128]{2,1,0:T(8,128)S(1)}, u32[]{:S(2)}, u32[]{:S(2)}) collective-permute-start(f32[4,88,128]{2,1,0:T(8,128)S(1)} %get-tuple-element.48), channel_id=1, source_target_pairs={{0,224},{32,0},{64,32},{96,64},{128,96},{160,128},{192,160},{224,1... | collective-permute-start | bytes 540680 | tf_op jit(solution)/shard_map/ppermute | solution.py:633
  26.6 11.2 %collective-permute-start.2 = (f32[4,88,128]{2,1,0:T(8,128)S(1)}, f32[4,88,128]{2,1,0:T(8,128)S(1)}, u32[]{:S(2)}, u32[]{:S(2)}) collective-permute-start(f32[4,88,128]{2,1,0:T(8,128)S(1)} %get-tuple-element.45), channel_id=1, source_target_pairs={{0,32},{32,64},{64,96},{96,128},{128,160},{160,192},{192,224},{224... | collective-permute-start | bytes 540680 | tf_op jit(solution)/shard_map/ppermute | solution.py:633
  28.3 9.5 %collective-permute-start.3 = (f32[4,88,128]{2,1,0:T(8,128)S(1)}, f32[4,88,128]{2,1,0:T(8,128)S(1)}, u32[]{:S(2)}, u32[]{:S(2)}) collective-permute-start(f32[4,88,128]{2,1,0:T(8,128)S(1)} %get-tuple-element.46), channel_id=1, source_target_pairs={{0,224},{32,0},{64,32},{96,64},{128,96},{160,128},{192,160},{224,1... | collective-permute-start | bytes 540680 | tf_op jit(solution)/shard_map/ppermute | solution.py:633

commit v7 on v6

--- a/solution.py
+++ b/solution.py
@@ -441,9 +441,9 @@
 
 
 def slope_inner_kernel(
-    width_x, slope_ref, masks_ref, base_hbm, design_hbm, s_ref, one, two, three, raw_ref, square_ref, base_ref, design_ref, sems
-):
-    copies = start_all(((base_hbm, base_ref), (design_hbm, design_ref)), sems)
+    width_x, slope_ref, masks_ref, base_hbm, s_ref, one, two, three, raw_ref, square_ref, base_ref, sems
+):
+    copies = start_all(((base_hbm, base_ref),), sems)
     chunks = raw_ref.shape[2] // LANES
     s_ref[pl.ds(tall_row(0, 0, chunks), slope_ref.shape[0]), :] = slope_ref[...]
     total = zero_tile()
@@ -455,27 +455,25 @@
         copy.wait()
 
 
-def make_slope_inner(s, masks, base, design):
-    shape = design.shape
+def make_slope_inner(s, masks, base, shape):
     wide = extended(shape)
     return pl.pallas_call(
         functools.partial(slope_inner_kernel, shape[0]),
         out_shape=(wide, wide, wide, wide, half_block(shape)[0], TILE)
-        + (jax.ShapeDtypeStruct(base.shape, F32), jax.ShapeDtypeStruct(shape, F32)),
-        in_specs=[VMEM] * 2 + [HBM] * 2,
-        out_specs=(VMEM,) * 8,
-        scratch_shapes=[pltpu.SemaphoreType.DMA((2,))],
+        + (jax.ShapeDtypeStruct(base.shape, F32),),
+        in_specs=[VMEM] * 2 + [HBM],
+        out_specs=(VMEM,) * 7,
+        scratch_shapes=[pltpu.SemaphoreType.DMA((1,))],
         compiler_params=params(8),
         cost_estimate=pl.CostEstimate(flops=15_000_000, bytes_accessed=8_000_000, transcendentals=0),
-    )(s, masks, in_hbm(base), in_hbm(design))
+    )(s, masks, in_hbm(base))
 
 
 def slope_outer_kernel(
-    width_x, left_ref, right_ref, masks_ref, inner_square_ref, s_in, one_in, two_in, three_in, second_hbm,
-    s_ref, one, two, three, raw_ref, square_ref, second_ref, sems,
+    width_x, left_ref, right_ref, masks_ref, inner_square_ref, s_in, one_in, two_in, three_in,
+    s_ref, one, two, three, raw_ref, square_ref,
 ):
     del s_in, one_in, two_in, three_in
-    (copy,) = start_all(((second_hbm, second_ref),), sems)
     chunks = raw_ref.shape[2] // LANES
     read_faces(s_ref, left_ref, right_ref, masks_ref, width_x, chunks)
     total = inner_square_ref[...]
@@ -483,31 +481,26 @@
         store_layer(raw_ref, i, values)
         total = add_products(total, values, values)
     square_ref[...] = total
-    copy.wait()
-
-
-def make_slope_outer(left, right, masks, square, wide, second_moment):
-    shape = second_moment.shape
+
+
+def make_slope_outer(left, right, masks, square, wide, shape):
     same = extended(shape)
     return pl.pallas_call(
         functools.partial(slope_outer_kernel, shape[0]),
-        out_shape=(same, same, same, same, half_block(shape)[1], TILE, jax.ShapeDtypeStruct(shape, F32)),
-        in_specs=[VMEM] * 8 + [HBM],
-        out_specs=(VMEM,) * 7,
-        scratch_shapes=[pltpu.SemaphoreType.DMA((1,))],
+        out_shape=(same, same, same, same, half_block(shape)[1], TILE),
+        in_specs=[VMEM] * 8,
+        out_specs=(VMEM,) * 6,
         input_output_aliases={4: 0, 5: 1, 6: 2, 7: 3},
         compiler_params=params(8),
         cost_estimate=pl.CostEstimate(flops=10_000_000, bytes_accessed=6_000_000, transcendentals=0),
-    )(left, right, masks, square, *wide, in_hbm(second_moment))[4:]
+    )(left, right, masks, square, *wide)[4:]
 
 
 def source_inner_kernel(
-    recv_ref, base_ref, slope_ref, masks_ref, slope_raw_ref, first_hbm, edges_ref,
-    s_ref, one, two, three, raw_ref, sums_ref, first_ref, own, beside, sems,
+    shape, recv_ref, base_ref, slope_ref, masks_ref, slope_raw_ref, edges_ref, s_ref, one, two, three, raw_ref, sums_ref, own, beside,
 ):
     del edges_ref
-    (copy,) = start_all(((first_hbm, first_ref),), sems)
-    width_x, width_y, width_z = first_ref.shape
+    width_x, width_y, width_z = shape
     chunks = width_z // LANES
     scatter(recv_ref, own, beside, range(HALO, width_x - HALO, HALO), width_y * chunks)
     make_layers(range(HALO, width_x - HALO), s_ref, slope_ref, base_ref, own, beside, chunks)
@@ -518,24 +511,21 @@
         ab = add_products(ab, values, load_layer(slope_raw_ref, i, chunks))
     sums_ref[0] = aa
     sums_ref[1] = ab
-    copy.wait()
-
-
-def make_source_inner(recv, base, slope, masks, slope_raw, first_moment, edges):
-    shape = first_moment.shape
+
+
+def make_source_inner(recv, base, slope, masks, slope_raw, edges, shape):
     wide = extended(shape)
-    scratch = pltpu.VMEM((first_moment.size // LANES, LANES), F32)
-    return pl.pallas_call(
-        source_inner_kernel,
-        out_shape=(wide,) * 4
-        + (half_block(shape)[0], jax.ShapeDtypeStruct((2, 8, LANES), F32), jax.ShapeDtypeStruct(shape, F32)),
-        in_specs=[VMEM] * 5 + [HBM] + [VMEM],
-        out_specs=(VMEM,) * 7,
-        input_output_aliases={6: 0},
-        scratch_shapes=[scratch] * 2 + [pltpu.SemaphoreType.DMA((1,))],
+    scratch = pltpu.VMEM((shape[0] * shape[1] * shape[2] // LANES, LANES), F32)
+    return pl.pallas_call(
+        functools.partial(source_inner_kernel, shape),
+        out_shape=(wide,) * 4 + (half_block(shape)[0], jax.ShapeDtypeStruct((2, 8, LANES), F32)),
+        in_specs=[VMEM] * 6,
+        out_specs=(VMEM,) * 6,
+        input_output_aliases={5: 0},
+        scratch_shapes=[scratch] * 2,
         compiler_params=params(8),
         cost_estimate=pl.CostEstimate(flops=40_000_000, bytes_accessed=16_000_000, transcendentals=0),
-    )(recv, base, slope, masks, slope_raw, in_hbm(first_moment), edges)
+    )(recv, base, slope, masks, slope_raw, edges)
 
 
 def source_outer_kernel(
@@ -658,14 +648,12 @@
     slope, base_edges, base, low, high, volume = make_slope(filtered, sensitivity, above, below, masks)
     left, right = shift(high, "gx", 1), shift(low, "gx", -1)
     shape = design.shape
-    *wide, slope_inner, square, base, design = make_slope_inner(slope, masks, base, design)
-    slope_outer, square, second_moment = make_slope_outer(left, right, masks, square, wide, second_moment)
+    *wide, slope_inner, square, base = make_slope_inner(slope, masks, base, shape)
+    slope_outer, square = make_slope_outer(left, right, masks, square, wide, shape)
 
     source, low, high = make_edges(received, base_edges, slope, shape)
     left, right = shift(high, "gx", 1), shift(low, "gx", -1)
-    *wide, inner, sums, first_moment = make_source_inner(
-        received, base, slope, masks, slope_inner, first_moment, source
-    )
+    *wide, inner, sums = make_source_inner(received, base, slope, masks, slope_inner, source, shape)
     outer, sums = make_source_outer(
         left, right, masks, slope_outer, volume, sums, square, wide, count_x * count_y, shape
     )

time: 62.5 us -> 62 us (level)
  Pallas kernels: 13.3 us -> 12.4 us
    pallas_call x1, Pallas kernels: 2.06 us -> 1.1 us  [make_slope_outer(): pl.pallas_call(functools.partial(slope_outer_kernel, shape[0]), out_shape...]
  transfers between devices with their start and end apart: 7 -> 7, of which waited for: 1 -> 1; matrix products, arithmetic and copies ran while one was open for 0% -> 0% of each run, Pallas kernels for 14% -> 13%
where the time goes in v7:
time: 62 us; the launch traced here: 61.7 us
  starting transfers between devices  24 us (39%)
  blocking collectives  21.6 us (35%)
  Pallas kernels  12.4 us (20%)
  waiting for transfers between devices  2.05 us (3%)
  local copies, waits for them, and re-layouts  0.81 us (1%)
  between operations  0.77 us (1%)
    all_to_all x1, blocking collectives, per_device(): sums = lax.all_to_all(sums, ('gx', 'gy'), 0, 0, tiled=True)  21.6 us
    ppermute x6, starting transfers between devices, shift(): lax.ppermute(cells, axis, [(i, (i + by) % count) for i in range(count)])  14.6 us
    all_to_all x1, starting transfers between devices, per_device(): lax.all_to_all(sent.reshape(count_y, SENT * LANES), 'gy', 0, 0, tiled=True)  9.41 us
    all_to_all x1, waiting for transfers between devices, per_device(): lax.all_to_all(sent.reshape(count_y, SENT * LANES), 'gy', 0, 0, tiled=True)  2.04 us
    pallas_call x1, Pallas kernels, make_slope(): pl.pallas_call(slope_kernel, out_shape=(rows, part, part, face, face, jax...  1.89 us
    pallas_call x1, Pallas kernels, adam(): pl.pallas_call(functools.partial(adam_kernel, cells), out_shape=(jax.Shap...  1.85 us
    pallas_call x1, Pallas kernels, make_source_inner(): pl.pallas_call(functools.partial(source_inner_kernel, shape), out_shape=(...  1.84 us
    pallas_call x1, Pallas kernels, make_slope_inner(): pl.pallas_call(functools.partial(slope_inner_kernel, shape[0]), out_shape...  1.58 us
  transfers between devices with their start and end apart: 7, of which 1 were waited for; matrix products, arithmetic and copies ran while one was open for 0% of the time, Pallas kernels for 13%

profile of v7, /device:TPU:1, one launch (start us, length us, event | category | flops | bytes accessed | tf_op | source)
XLA Modules:
  0.0 61.7 jit_solution(12962648490274877140)
XLA Ops:
  0.6 1.4 %shard_map.120 = (f32[2,8,8,1024]{3,2,1,0:T(8,128)S(1)}, f32[2,8,8,1024]{3,2,1,0:T(8,128)S(1)}, f32[7,8,128]{2,1,0:T(8,128)S(1)}, f32[256,128]{1,0:T(8,128)S(1)}, f32[32,128]{1,0:T(8,128)S(1)}) custom-call(f32[64,128]{1,0:T(8,128)} %bitcast.13, s32[1,64]{1,0:T(1,128)} %anchor_hbm.1, s32[1,64]{1,0:T(1,128)} %bitcast.14, f32[1,2]{1,0:T(1,128)} %bitcast.15, ...), custom_call_target="tpu_custom_call" | custom-call | tf_op jit(solution)/shard_map/pallas_call | solution.py:131
  2.0 3.3 %collective-permute-start = (f32[2,8,8,1024]{3,2,1,0:T(8,128)S(1)}, f32[2,8,8,1024]{3,2,1,0:T(8,128)S(1)}, u32[]{:S(2)}, u32[]{:S(2)}) collective-permute-start(f32[2,8,8,1024]{3,2,1,0:T(8,128)S(1)} %get-tuple-element.37), channel_id=1, source_target_pairs={{0,31},{1,0},{2,1},{3,2},{4,3},{5,4},{6,5},{7,6},{8,7},{9,8},{10,9... | collective-permute-start | bytes 1572872 | tf_op jit(solution)/shard_map/ppermute | solution.py:623
  5.3 0.0 collective-permute-start.1
  5.4 0.8 %shard_map.121 = f32[800,128]{1,0:T(8,128)} custom-call(f32[256,128]{1,0:T(8,128)S(1)} %get-tuple-element.35.packed_ref, f32[32,128]{1,0:T(8,128)S(1)} %get-tuple-element.36.anchors_ref), custom_call_target="tpu_custom_call" | custom-call | tf_op jit(solution)/shard_map/pallas_call | solution.py:176
  6.1 9.4 %all-to-all-start = ((f32[32,1,3200]{2,1,0:T(1,128)}), f32[32,1,3200]{2,1,0:T(1,128)S(1)}, u32[]{:S(2)}, u32[]{:S(2)}) async-start(f32[32,1,3200]{2,1,0:T(1,128)} %bitcast.3), calls=%async_computation | async-start | bytes 819200 | tf_op jit(solution)/shard_map/all_to_all | solution.py:646
  15.6 0.0 collective-permute-done.above_ref
  15.6 0.0 collective-permute-done.1.below_ref
  15.6 1.9 %shard_map.122 = (f32[2048,128]{1,0:T(8,128)S(1)}, f32[1024,128]{1,0:T(8,128)S(1)}, f32[1024,128]{1,0:T(8,128)S(1)}, f32[4,88,128]{2,1,0:T(8,128)S(1)}, f32[4,88,128]{2,1,0:T(8,128)S(1)}, /*index=5*/f32[8,128]{1,0:T(8,128)S(1)}) custom-call(f32[16,8,1024]{2,1,0:T(8,128)} %filtered_hbm.3, f32[16,8,1024]{2,1,0:T(8,128)} %sensitivity_hbm.3, ...), custom_call_target="tpu_custom_call" | custom-call | flops 4000000 | bytes 4000000 | tf_op jit(solution)/shard_map/pallas_call | solution.py:316
  17.5 0.0 copy-start
  17.5 0.8 %copy-done = f32[1024,128]{1,0:T(8,128)} copy-done((f32[1024,128]{1,0:T(8,128)}, f32[1024,128]{1,0:T(8,128)S(1)}, u32[]{:S(2)}) %copy-start) | copy-done | bytes 524312
  18.3 1.6 %collective-permute-start.4 = (f32[4,88,128]{2,1,0:T(8,128)S(1)}, f32[4,88,128]{2,1,0:T(8,128)S(1)}, u32[]{:S(2)}, u32[]{:S(2)}) collective-permute-start(f32[4,88,128]{2,1,0:T(8,128)S(1)} %get-tuple-element.44), channel_id=1, source_target_pairs={{0,32},{32,64},{64,96},{96,128},{128,160},{160,192},{192,224},{224... | collective-permute-start | bytes 540680 | tf_op jit(solution)/shard_map/ppermute | solution.py:623
  19.9 3.9 %collective-permute-start.5 = (f32[4,88,128]{2,1,0:T(8,128)S(1)}, f32[4,88,128]{2,1,0:T(8,128)S(1)}, u32[]{:S(2)}, u32[]{:S(2)}) collective-permute-start(f32[4,88,128]{2,1,0:T(8,128)S(1)} %get-tuple-element.45), channel_id=1, source_target_pairs={{0,224},{32,0},{64,32},{96,64},{128,96},{160,128},{192,160},{224,1... | collective-permute-start | bytes 540680 | tf_op jit(solution)/shard_map/ppermute | solution.py:623
  23.9 2.0 %all-to-all-done = f32[32,1,3200]{2,1,0:T(1,128)S(1)} async-done(((f32[32,1,3200]{2,1,0:T(1,128)}), f32[32,1,3200]{2,1,0:T(1,128)S(1)}, u32[]{:S(2)}, u32[]{:S(2)}) %all-to-all-start) | async-done | bytes 409632 | tf_op jit(solution)/shard_map/all_to_all | solution.py:646
  25.9 0.7 %shard_map.123 = (f32[3088,128]{1,0:T(8,128)S(1)}, f32[4,88,128]{2,1,0:T(8,128)S(1)}, f32[4,88,128]{2,1,0:T(8,128)S(1)}) custom-call(f32[800,128]{1,0:T(8,128)S(1)} %bitcast.9, f32[1024,128]{1,0:T(8,128)S(1)} %get-tuple-element.40.base_ref, f32[2048,128]{1,0:T(8,128)S(1)} %get-tuple-element.41.slope_ref), custom_call_target="tpu_custom_call" | custom-call | tf_op jit(solution)/shard_map/pallas_call | solution.py:350
  26.6 1.7 %collective-permute-start.2 = (f32[4,88,128]{2,1,0:T(8,128)S(1)}, f32[4,88,128]{2,1,0:T(8,128)S(1)}, u32[]{:S(2)}, u32[]{:S(2)}) collective-permute-start(f32[4,88,128]{2,1,0:T(8,128)S(1)} %get-tuple-element.42), channel_id=1, source_target_pairs={{0,32},{32,64},{64,96},{96,128},{128,160},{160,192},{192,224},{224... | collective-permute-start | bytes 540680 | tf_op jit(solution)/shard_map/ppermute | solution.py:623
  28.3 4.0 %collective-permute-start.3 = (f32[4,88,128]{2,1,0:T(8,128)S(1)}, f32[4,88,128]{2,1,0:T(8,128)S(1)}, u32[]{:S(2)}, u32[]{:S(2)}) collective-permute-start(f32[4,88,128]{2,1,0:T(8,128)S(1)} %get-tuple-element.43), channel_id=1, source_target_pairs={{0,224},{32,0},{64,32},{96,64},{128,96},{160,128},{192,160},{224,1... | collective-permute-start | bytes 540680 | tf_op jit(solution)/shard_map/ppermute | solution.py:623
  32.3 1.6 %shard_map.124 = (f32[3088,128]{1,0:T(8,128)S(1)}, f32[3088,128]{1,0:T(8,128)S(1)}, f32[3088,128]{1,0:T(8,128)S(1)}, f32[3088,128]{1,0:T(8,128)S(1)}, f32[8,8,10...) custom-call(f32[2048,128]{1,0:T(8,128)S(1)} %get-tuple-element.41.slope_ref, ...), custom_call_target="tpu_custom_call" | custom-call | flops 15000000 | bytes 8000000 | tf_op jit(solution)/shard_map/pallas_call | solution.py:460
  33.9 1.8 %shard_map.126 = (f32[3088,128]{1,0:T(8,128)S(1)}, f32[3088,128]{1,0:T(8,128)S(1)}, f32[3088,128]{1,0:T(8,128)S(1)}, f32[3088,128]{1,0:T(8,128)S(1)}, f32[8,8,10...) custom-call(f32[800,128]{1,0:T(8,128)S(1)} %bitcast.10, ...), custom_call_target="tpu_custom_call", output_to_operand_aliasing={{0}: (5, {})} | custom-call | flops 40000000 | bytes 16000000 | tf_op jit(solution)/shard_map/pallas_call | solution.py:519
  35.7 0.0 collective-permute-done.4.left_ref
  35.7 0.0 collective-permute-done.5.right_ref
  35.8 1.1 %shard_map.125 = (f32[3088,128]{1,0:T(8,128)S(1)}, f32[3088,128]{1,0:T(8,128)S(1)}, f32[3088,128]{1,0:T(8,128)S(1)}, f32[3088,128]{1,0:T(8,128)S(1)}, f32[8,8,1024]{2,1,0:T(8,128)S(1)}, /*index=5*/f32[8,128]{1,0:T(8,128)S(1)}) custom-call(f32[4,88,128]{2,1,0:T(8,128)S(1)} %collective-permute-do, ...), custom_call_target="tpu_custom_call", output_to_operand_aliasing={{0}: (4, {}), {1}: (5, {}), {2}: (6, {}), {3}: (7, {})} | custom-call | flops 10000000 | bytes 6000000 | tf_op jit(solution)/shard_map/pallas_call | solution.py:488
  36.9 0.0 collective-permute-done.2.left_ref
  36.9 0.0 collective-permute-done.3.right_ref
  36.9 0.0 copy-start.1
  36.9 0.0 copy-start.2
  36.9 0.0 copy-start.3
  36.9 1.3 %shard_map.127 = (f32[3088,128]{1,0:T(8,128)S(1)}, f32[3088,128]{1,0:T(8,128)S(1)}, f32[3088,128]{1,0:T(8,128)S(1)}, f32[3088,128]{1,0:T(8,128)S(1)}, f32[8,8,1024]{2,1,0:T(8,128)S(1)}, /*index=5*/f32[256,128]{1,0:T(8,128)S(1)}) custom-call(f32[4,88,128]{2,1,0:T(8,128)S(1)} %collective-permute-do, ...), custom_call_target="tpu_custom_call", output_to_operand_aliasing={{0}: (7, {}), {1}: (8, {}), {2}: (9, {}), {3}: (10, {})} | custom-call | tf_op jit(solution)/shard_map/pallas_call | solution.py:556
  38.2 21.6 %all_to_all.20 = f32[256,1,128]{2,1,0:T(1,128)S(1)} all-to-all(f32[256,1,128]{2,1,0:T(1,128)S(1)} %bitcast.12), channel_id=1, replica_groups=mesh['gx'=8,'gy'=32] {'gx','gy'}, dimensions={0} | all-to-all | bytes 262144 | tf_op jit(solution)/shard_map/all_to_all | solution.py:660
  59.9 0.0 copy-done.1
  59.9 0.0 copy-done.2
  59.9 0.0 copy-done.3
  59.9 1.9 %shard_map.128 = (f32[16,8,1024]{2,1,0:T(8,128)}, f32[16,8,1024]{2,1,0:T(8,128)}, f32[16,8,1024]{2,1,0:T(8,128)}, f32[16,8,1024]{2,1,0:T(8,128)}) custom-call(f32[256,128]{1,0:T(8,128)S(1)} %bitcast.11, f32[7,8,128]{2,1,0:T(8,128)S(1)} %get-tuple-element.39.masks_ref, f32[8,8,1024]{2,1,0:T(8,128)S(1)} %get-tuple-element.64.inner_ref, ...), custom_call_target="tpu_custom_call" | custom-call | tf_op jit(solution)/shard_map/pallas_call | solution.py:611
Async XLA Ops:
  2.0 13.5 %collective-permute-start = (f32[2,8,8,1024]{3,2,1,0:T(8,128)S(1)}, f32[2,8,8,1024]{3,2,1,0:T(8,128)S(1)}, u32[]{:S(2)}, u32[]{:S(2)}) collective-permute-start(f32[2,8,8,1024]{3,2,1,0:T(8,128)S(1)} %get-tuple-element.37), channel_id=1, source_target_pairs={{0,31},{1,0},{2,1},{3,2},{4,3},{5,4},{6,5},{7,6},{8,7},{9,8},{10,9... | collective-permute-start | bytes 1572872 | tf_op jit(solution)/shard_map/ppermute | solution.py:623
  5.3 10.2 %collective-permute-start.1 = (f32[2,8,8,1024]{3,2,1,0:T(8,128)S(1)}, f32[2,8,8,1024]{3,2,1,0:T(8,128)S(1)}, u32[]{:S(2)}, u32[]{:S(2)}) collective-permute-start(f32[2,8,8,1024]{3,2,1,0:T(8,128)S(1)} %get-tuple-element.38), channel_id=1, source_target_pairs={{0,1},{1,2},{2,3},{3,4},{4,5},{5,6},{6,7},{7,8},{8,9},{9,10},{10,1... | collective-permute-start | bytes 1572872 | tf_op jit(solution)/shard_map/ppermute | solution.py:623
  6.1 19.7 %all-to-all-start = ((f32[32,1,3200]{2,1,0:T(1,128)}), f32[32,1,3200]{2,1,0:T(1,128)S(1)}, u32[]{:S(2)}, u32[]{:S(2)}) async-start(f32[32,1,3200]{2,1,0:T(1,128)} %bitcast.3), calls=%async_computation | async-start | bytes 819200 | tf_op jit(solution)/shard_map/all_to_all | solution.py:646
  17.5 0.8 %copy-start = (f32[1024,128]{1,0:T(8,128)}, f32[1024,128]{1,0:T(8,128)S(1)}, u32[]{:S(2)}) copy-start(f32[1024,128]{1,0:T(8,128)S(1)} %get-tuple-element.46.base_hbm) | copy-start | bytes 1572868
  18.3 17.5 %collective-permute-start.4 = (f32[4,88,128]{2,1,0:T(8,128)S(1)}, f32[4,88,128]{2,1,0:T(8,128)S(1)}, u32[]{:S(2)}, u32[]{:S(2)}) collective-permute-start(f32[4,88,128]{2,1,0:T(8,128)S(1)} %get-tuple-element.44), channel_id=1, source_target_pairs={{0,32},{32,64},{64,96},{96,128},{128,160},{160,192},{192,224},{224... | collective-permute-start | bytes 540680 | tf_op jit(solution)/shard_map/ppermute | solution.py:623
  19.9 15.8 %collective-permute-start.5 = (f32[4,88,128]{2,1,0:T(8,128)S(1)}, f32[4,88,128]{2,1,0:T(8,128)S(1)}, u32[]{:S(2)}, u32[]{:S(2)}) collective-permute-start(f32[4,88,128]{2,1,0:T(8,128)S(1)} %get-tuple-element.45), channel_id=1, source_target_pairs={{0,224},{32,0},{64,32},{96,64},{128,96},{160,128},{192,160},{224,1... | collective-permute-start | bytes 540680 | tf_op jit(solution)/shard_map/ppermute | solution.py:623
  26.6 10.3 %collective-permute-start.2 = (f32[4,88,128]{2,1,0:T(8,128)S(1)}, f32[4,88,128]{2,1,0:T(8,128)S(1)}, u32[]{:S(2)}, u32[]{:S(2)}) collective-permute-start(f32[4,88,128]{2,1,0:T(8,128)S(1)} %get-tuple-element.42), channel_id=1, source_target_pairs={{0,32},{32,64},{64,96},{96,128},{128,160},{160,192},{192,224},{224... | collective-permute-start | bytes 540680 | tf_op jit(solution)/shard_map/ppermute | solution.py:623
  28.3 8.6 %collective-permute-start.3 = (f32[4,88,128]{2,1,0:T(8,128)S(1)}, f32[4,88,128]{2,1,0:T(8,128)S(1)}, u32[]{:S(2)}, u32[]{:S(2)}) collective-permute-start(f32[4,88,128]{2,1,0:T(8,128)S(1)} %get-tuple-element.43), channel_id=1, source_target_pairs={{0,224},{32,0},{64,32},{96,64},{128,96},{160,128},{192,160},{224,1... | collective-permute-start | bytes 540680 | tf_op jit(solution)/shard_map/ppermute | solution.py:623
  36.9 23.0 %copy-start.1 = (f32[16,8,1024]{2,1,0:T(8,128)S(1)}, f32[16,8,1024]{2,1,0:T(8,128)}, u32[]{:S(2)}) copy-start(f32[16,8,1024]{2,1,0:T(8,128)} %design_ref.1) | copy-start | bytes 1572868
  36.9 23.0 %copy-start.2 = (f32[16,8,1024]{2,1,0:T(8,128)S(1)}, f32[16,8,1024]{2,1,0:T(8,128)}, u32[]{:S(2)}) copy-start(f32[16,8,1024]{2,1,0:T(8,128)} %first_ref.1) | copy-start | bytes 1572868
  36.9 23.0 %copy-start.3 = (f32[16,8,1024]{2,1,0:T(8,128)S(1)}, f32[16,8,1024]{2,1,0:T(8,128)}, u32[]{:S(2)}) copy-start(f32[16,8,1024]{2,1,0:T(8,128)} %second_ref.1) | copy-start | bytes 1572868
